TPU v7x, 32 devices: a whole 2x2x4 slice. The times are simulated.
32 devices in a mesh: row: 8 (over z, x), ch: 4 (over y, core).
Axes of the slice: x: 2, y: 2, z: 4, core: 2. Of those that a mesh axis runs over, the one named last changes fastest.
Arguments:
- feats: bfloat16 [2048, 9216], P('ch', 'row'), may hold values from -6 to 6
- lowlevel: bfloat16 [256, 147456], P('ch', 'row'), may hold values from -6 to 6
- heights: int32 [6], replicated, may hold values from 1 to 64, 288 in all
- widths: int32 [6], replicated, may hold values from 8 to 32, as said below
- w_one: bfloat16 [256, 2048], P('ch'), may hold values from -0.125 to 0.125
- w_atrous: bfloat16 [3, 256, 9, 2048], P(None, 'ch'), may hold values from -0.046875 to 0.046875
- w_pool: bfloat16 [256, 2048], P('ch'), may hold values from -0.125 to 0.125
- w_proj: bfloat16 [256, 1280], P('ch'), may hold values from -0.15625 to 0.15625
- w_low: bfloat16 [48, 256], P(None, 'ch'), may hold values from -0.375 to 0.375
- w_dec1: bfloat16 [256, 9, 304], P('ch'), may hold values from -0.109375 to 0.109375
- w_dec2: bfloat16 [256, 9, 256], P('ch'), may hold values from -0.125 to 0.125
- w_cls: bfloat16 [21, 256], replicated, may hold values from -0.375 to 0.375
- b_cls: bfloat16 [21], replicated, may hold values from -3 to 3
- mid_gain: bfloat16 [6, 256], P(None, 'ch'), may hold values from 0.099609375 to 1.8984375
- mid_shift: bfloat16 [6, 256], P(None, 'ch'), may hold values from -3 to 3
- low_gain: bfloat16 [48], P('ch'), may hold values from 0.099609375 to 1.8984375
- low_shift: bfloat16 [48], P('ch'), may hold values from -3 to 3
- dec_gain: bfloat16 [2, 256], P(None, 'ch'), may hold values from 0.099609375 to 1.8984375
- dec_shift: bfloat16 [2, 256], P(None, 'ch'), may hold values from -3 to 3
- cotangent: bfloat16 [21, 147456], P(None, ('row', 'ch')), may hold values from -6 to 6
Outputs:
- logits: float32 [21, 147456], P(None, ('row', 'ch'))
- g_feats: float32 [2048, 9216], P('ch', 'row')
- g_lowlevel: float32 [256, 147456], P('ch', 'row')
- g_w_one: float32 [256, 2048], P('ch')
- g_w_atrous: float32 [3, 256, 9, 2048], P(None, 'ch')
- g_w_pool: float32 [256, 2048], P('ch')
- g_w_proj: float32 [256, 1280], P('ch')
- g_w_low: float32 [48, 256], P(None, 'ch')
- g_w_dec1: float32 [256, 9, 304], P('ch')
- g_w_dec2: float32 [256, 9, 256], P('ch')
- g_w_cls: float32 [21, 256], replicated
- g_b_cls: float32 [21], replicated
- g_mid_gain: float32 [6, 256], P(None, 'ch')
- g_mid_shift: float32 [6, 256], P(None, 'ch')
- g_low_gain: float32 [48], P('ch')
- g_low_shift: float32 [48], P('ch')
- g_dec_gain: float32 [2, 256], P(None, 'ch')
- g_dec_shift: float32 [2, 256], P(None, 'ch')
Inputs may be any that keep to these rules, and one draw needn't show every extreme that they name: The heights sum to 288. `widths`: one image is 32 columns wide and one 32 // 4.
All inputs are finite; a program needn't handle non-finite values.
Results may differ from a plain program's by a relative error of at most 0.03.
Values may be sent and summed in bfloat16 or wider, within the bound.
No kernel may reach another device: no remote copies, remote signals or barrier semaphores. Data moves between devices by JAX's collectives and lax.ppermute only.
A program may use at most 512 MiB of HBM per device.

v0:
```python
import jax
import jax.numpy as jnp
from jax import lax
from jax.sharding import PartitionSpec as P

LOWC = 48
WS = 32


EPSILON = 1e-05
DILATIONS = (6, 12, 18)
HIGHEST = lax.Precision.HIGHEST


def with_halo(x, sides, width):
    for axis, dim in sides:
        count, length = (lax.axis_size(axis), x.shape[dim])
        up = [(i, (i + 1) % count) for i in range(count - 1)]
        down = [(j, i) for i, j in up]
        last = lax.slice_in_dim(x, length - width, length, axis=dim)
        initial = lax.slice_in_dim(x, 0, width, axis=dim)
        before = lax.ppermute(last, axis, up)
        after = lax.ppermute(initial, axis, down)
        x = jnp.concatenate([before, x, after], axis=dim)
    return x


def segment_of(indices, image_ends):
    return jnp.sum((indices[:, None] >= image_ends[None, :]).astype(jnp.int32), axis=1)


def same_rows(first_row, row_count, offset, image_ends, total_rows):
    indices = first_row + jnp.arange(row_count, dtype=jnp.int32)
    others = indices + offset
    inside = (others >= 0) & (others < total_rows)
    return (inside & (segment_of(indices, image_ends) == segment_of(others, image_ends))).astype(
        jnp.float32
    )


def geometry(heights, widths, factor, first_row, row_count, col_count):
    image_ends = jnp.cumsum(heights) * factor
    starts = image_ends - heights * factor
    indices = first_row + jnp.arange(row_count, dtype=jnp.int32)
    inside = (indices[:, None] >= starts[None, :]) & (indices[:, None] < image_ends[None, :])
    limit = jnp.sum(jnp.where(inside, widths[None, :] * factor, 0), axis=1)
    valid_mask = (jnp.arange(col_count, dtype=jnp.int32)[None, :] < limit[:, None]).astype(
        jnp.float32
    )
    return (inside.astype(jnp.float32), valid_mask, image_ends)


def upsample(earlier, middle, later):
    stacked = jnp.stack(
        [
            0.375 * earlier + 0.625 * middle,
            0.125 * earlier + 0.875 * middle,
            0.875 * middle + 0.125 * later,
            0.625 * middle + 0.375 * later,
        ],
        axis=2,
    )
    channels, height, _, width = stacked.shape
    tall = stacked.reshape(channels, 4 * height, width)
    leftward = jnp.pad(tall, ((0, 0), (0, 0), (1, 0)))[:, :, :-1]
    rightward = jnp.pad(tall, ((0, 0), (0, 0), (0, 1)))[:, :, 1:]
    spread = jnp.stack(
        [
            0.375 * leftward + 0.625 * tall,
            0.125 * leftward + 0.875 * tall,
            0.875 * tall + 0.125 * rightward,
            0.625 * tall + 0.375 * rightward,
        ],
        axis=3,
    )
    return spread.reshape(channels, 4 * height, 4 * width)


def channel_gather(values):
    return lax.all_gather(values, "ch", axis=0, tiled=True)


def channel_sum(values):
    return lax.psum_scatter(
        values.astype(jnp.bfloat16), "ch", scatter_dimension=0, tiled=True
    ).astype(jnp.float32)


def pixel_sums(values):
    return lax.psum(values, "row")


def rows_halo(values, margin):
    return with_halo(values, (("row", 1),), margin)


def rim_sums(padded, margin):
    both_rims = jnp.concatenate([padded[:, :margin], padded[:, -margin:]], axis=1)
    arrived = with_halo(both_rims.astype(jnp.bfloat16), (("row", 1),), margin).astype(
        both_rims.dtype
    )
    interior = padded[:, margin:-margin]
    interior = interior.at[:, :margin].add(arrived[:, :margin])
    return interior.at[:, -margin:].add(arrived[:, -margin:])


def norm_forward(pre_act, gain, shift, valid_mask, pixel_count):
    centre = pixel_sums(jnp.sum(pre_act * valid_mask, axis=(1, 2))) / pixel_count
    centered = pre_act - centre[:, None, None]
    spread = pixel_sums(jnp.sum(centered * centered * valid_mask, axis=(1, 2))) / pixel_count
    scale = lax.rsqrt(spread + EPSILON)
    normed = centered * scale[:, None, None]
    shifted = gain[:, None, None] * normed + shift[:, None, None]
    return (jax.nn.silu(shifted) * valid_mask, (normed, shifted, scale))


def norm_backward(grad_act, kept, gain, valid_mask, pixel_count):
    normed, shifted, scale = kept
    gate_value = jax.nn.sigmoid(shifted)
    grad_pre = grad_act * valid_mask * (gate_value * (1.0 + shifted * (1.0 - gate_value)))
    totals = pixel_sums(
        jnp.stack([jnp.sum(grad_pre, axis=(1, 2)), jnp.sum(grad_pre * normed, axis=(1, 2))])
    )
    grad_normed = gain[:, None, None] * grad_pre
    offsets = valid_mask * (
        (gain * totals[0] / pixel_count)[:, None, None]
        + normed * (gain * totals[1] / pixel_count)[:, None, None]
    )
    return (scale[:, None, None] * (grad_normed - offsets), totals[1], totals[0])


def dilated_forward(padded, weight, dilation, row_masks):
    strip_rows = padded.shape[1] - 2 * dilation
    strip_cols = padded.shape[2]
    widened = jnp.pad(padded, ((0, 0), (0, 0), (dilation, dilation)))
    result = jnp.zeros((weight.shape[0], strip_rows, strip_cols), jnp.float32)
    for row_tap in range(3):
        partial_sum = jnp.zeros_like(result)
        for col_tap in range(3):
            window_in = widened[
                :,
                row_tap * dilation : row_tap * dilation + strip_rows,
                col_tap * dilation : col_tap * dilation + strip_cols,
            ]
            partial_sum = partial_sum + jnp.einsum(
                "oc,crw->orw",
                weight[:, row_tap * 3 + col_tap],
                window_in,
                preferred_element_type=jnp.float32,
            )
        result = result + partial_sum * row_masks[row_tap][None, :, None]
    return result


def dilated_backward(padded, weight, dilation, row_masks, grad_out):
    strip_rows = padded.shape[1] - 2 * dilation
    strip_cols = padded.shape[2]
    widened = jnp.pad(padded, ((0, 0), (0, 0), (dilation, dilation)))
    weight_grads = []
    placed = []
    for row_tap in range(3):
        masked = grad_out * row_masks[row_tap][None, :, None].astype(jnp.bfloat16)
        for col_tap in range(3):
            window_in = widened[
                :,
                row_tap * dilation : row_tap * dilation + strip_rows,
                col_tap * dilation : col_tap * dilation + strip_cols,
            ]
            weight_grads.append(
                jnp.einsum("orw,crw->oc", masked, window_in, preferred_element_type=jnp.float32)
            )
            placed.append(
                jnp.pad(
                    masked,
                    (
                        (0, 0),
                        (row_tap * dilation, (2 - row_tap) * dilation),
                        (col_tap * dilation, (2 - col_tap) * dilation),
                    ),
                )
            )
    grad_wide = jnp.einsum(
        "otc,torw->crw", weight, jnp.stack(placed), preferred_element_type=jnp.float32
    )
    return (grad_wide[:, :, dilation : dilation + strip_cols], jnp.stack(weight_grads, axis=1))


def local(
    feats,
    lowlevel,
    heights,
    widths,
    w_one,
    w_atrous,
    w_pool,
    w_proj,
    w_low,
    w_dec1,
    w_dec2,
    w_cls,
    b_cls,
    mid_gain,
    mid_shift,
    low_gain,
    low_shift,
    dec_gain,
    dec_shift,
    cotangent,
):
    channel_devices = lax.axis_size("ch")
    strip_rows = feats.shape[1] // WS
    total_rows = strip_rows * lax.axis_size("row")
    first_row = lax.axis_index("row") * strip_rows
    member, valid_mask, image_ends = geometry(heights, widths, 1, first_row, strip_rows, WS)
    member_fine, valid_fine, ends_fine = geometry(
        heights, widths, 4, 4 * first_row, 4 * strip_rows, 4 * WS
    )
    image_area = (heights * widths).astype(jnp.float32)
    pixel_count = jnp.sum(image_area)
    fine_count = 16.0 * pixel_count
    coarse_masks = {
        dilation: [
            same_rows(first_row, strip_rows, (row_tap - 1) * dilation, image_ends, total_rows)
            for row_tap in range(3)
        ]
        for dilation in DILATIONS
    }
    fine_masks = [
        same_rows(4 * first_row, 4 * strip_rows, row_tap - 1, ends_fine, 4 * total_rows)
        for row_tap in range(3)
    ]
    branch_width = w_one.shape[0]
    low_share = LOWC // channel_devices
    reach = DILATIONS[-1]
    image_total = heights.shape[0]
    shard = feats.reshape(-1, strip_rows, WS) * valid_mask.astype(jnp.bfloat16)
    padded = rows_halo(channel_gather(shard), reach)
    inner = padded[:, reach : reach + strip_rows]
    plain = jnp.einsum("oc,crw->orw", w_one, inner, preferred_element_type=jnp.float32)
    atrous = [
        dilated_forward(
            padded[:, reach - dilation : reach + strip_rows + dilation],
            w_atrous[branch_index],
            dilation,
            coarse_masks[dilation],
        )
        for branch_index, dilation in enumerate(DILATIONS)
    ]
    column_sums = jnp.sum(inner, axis=2, dtype=jnp.float32)
    pooled = (
        pixel_sums(jnp.dot(column_sums, member, precision=HIGHEST)) / image_area[None, :]
    ).astype(jnp.bfloat16)
    pool_pre = jnp.dot(w_pool, pooled, preferred_element_type=jnp.float32)
    pool_mean = jnp.mean(pool_pre, axis=1)
    pool_scale = lax.rsqrt(jnp.mean(pool_pre * pool_pre, axis=1) - pool_mean * pool_mean + EPSILON)
    pool_normed = (pool_pre - pool_mean[:, None]) * pool_scale[:, None]
    pool_shifted = mid_gain[4][:, None] * pool_normed + mid_shift[4][:, None]
    pool_act = jax.nn.silu(pool_shifted).astype(jnp.bfloat16)
    spread_rows = jnp.dot(
        pool_act, member.T.astype(jnp.bfloat16), preferred_element_type=jnp.float32
    ).astype(jnp.bfloat16)
    broad = spread_rows[:, :, None] * valid_mask.astype(jnp.bfloat16)[None]
    stacked = jnp.concatenate([plain] + atrous, axis=0)
    branch_gain = mid_gain[:4].reshape(-1)
    branch_shift = mid_shift[:4].reshape(-1)
    branch_act, branch_kept = norm_forward(
        stacked, branch_gain, branch_shift, valid_mask, pixel_count
    )
    branch_out = jnp.concatenate([branch_act.astype(jnp.bfloat16), broad], axis=0)
    gathered = channel_gather(branch_out)
    ordered = (
        w_proj.reshape(branch_width, 5, channel_devices, branch_width)
        .transpose(0, 2, 1, 3)
        .reshape(branch_width, -1)
    )
    proj_pre = jnp.einsum("oc,crw->orw", ordered, gathered, preferred_element_type=jnp.float32)
    proj_act, proj_kept = norm_forward(proj_pre, mid_gain[5], mid_shift[5], valid_mask, pixel_count)
    coarse_pad = rows_halo(proj_act.astype(jnp.bfloat16), 1).astype(jnp.float32)
    above = same_rows(first_row, strip_rows, -1, image_ends, total_rows)
    below = same_rows(first_row, strip_rows, 1, image_ends, total_rows)

    def expand(source):
        return (
            upsample(
                source[:, :-2] * above[None, :, None],
                source[:, 1:-1],
                source[:, 2:] * below[None, :, None],
            )
            * valid_fine[None]
        )

    upsampled, expand_back = jax.vjp(expand, coarse_pad)
    upsampled = upsampled.astype(jnp.bfloat16)
    fine_shard = lowlevel.reshape(-1, 4 * strip_rows, 4 * WS) * valid_fine.astype(jnp.bfloat16)
    low_pre = channel_sum(
        jnp.einsum("oc,crw->orw", w_low, fine_shard, preferred_element_type=jnp.float32)
    )
    low_act, low_kept = norm_forward(low_pre, low_gain, low_shift, valid_fine, fine_count)
    decoder_in = rows_halo(
        channel_gather(jnp.concatenate([low_act.astype(jnp.bfloat16), upsampled], axis=0)), 1
    )
    dec_out = w_dec1.shape[0]
    first_weight = jnp.concatenate(
        [
            w_dec1[:, :, :LOWC].reshape(dec_out, 9, channel_devices, low_share),
            w_dec1[:, :, LOWC:].reshape(dec_out, 9, channel_devices, branch_width),
        ],
        axis=3,
    ).reshape(dec_out, 9, -1)
    first_pre = dilated_forward(decoder_in, first_weight, 1, fine_masks)
    first_act, first_kept = norm_forward(
        first_pre, dec_gain[0], dec_shift[0], valid_fine, fine_count
    )
    second_in = rows_halo(channel_gather(first_act.astype(jnp.bfloat16)), 1)
    second_pre = dilated_forward(second_in, w_dec2, 1, fine_masks)
    second_act, second_kept = norm_forward(
        second_pre, dec_gain[1], dec_shift[1], valid_fine, fine_count
    )
    features = lax.all_to_all(
        second_act.astype(jnp.bfloat16).reshape(branch_width, -1),
        "ch",
        split_axis=1,
        concat_axis=0,
        tiled=True,
    )
    logits = jnp.dot(w_cls, features, preferred_element_type=jnp.float32) + b_cls[:, None].astype(
        jnp.float32
    )
    class_grads = lax.psum(
        (
            jnp.einsum("kp,cp->kc", cotangent, features, preferred_element_type=jnp.float32),
            jnp.sum(cotangent, axis=1, dtype=jnp.float32),
        ),
        ("row", "ch"),
    )
    grad_features = jnp.einsum(
        "kc,kp->cp", w_cls, cotangent, preferred_element_type=jnp.float32
    ).astype(jnp.bfloat16)
    grad_second = lax.all_to_all(
        grad_features, "ch", split_axis=0, concat_axis=1, tiled=True
    ).reshape(branch_width, 4 * strip_rows, 4 * WS)
    second_grad_pre, g_second_gain, g_second_shift = norm_backward(
        grad_second.astype(jnp.float32), second_kept, dec_gain[1], valid_fine, fine_count
    )
    grad_second_in, g_second_weight = dilated_backward(
        second_in, w_dec2, 1, fine_masks, second_grad_pre.astype(jnp.bfloat16)
    )
    grad_first = channel_sum(rim_sums(grad_second_in, 1))
    first_grad_pre, g_first_gain, g_first_shift = norm_backward(
        grad_first, first_kept, dec_gain[0], valid_fine, fine_count
    )
    grad_decoder_in, g_first_weight = dilated_backward(
        decoder_in, first_weight, 1, fine_masks, first_grad_pre.astype(jnp.bfloat16)
    )
    grad_joined = channel_sum(rim_sums(grad_decoder_in, 1))
    low_grad_pre, g_low_gain, g_low_shift = norm_backward(
        grad_joined[:low_share], low_kept, low_gain, valid_fine, fine_count
    )
    low_grad_all = channel_gather(low_grad_pre.astype(jnp.bfloat16))
    g_low_weight = jnp.einsum(
        "orw,crw->oc", low_grad_all, fine_shard, preferred_element_type=jnp.float32
    )
    g_lowlevel = (
        jnp.einsum("oc,orw->crw", w_low, low_grad_all, preferred_element_type=jnp.float32)
        * valid_fine[None]
    ).reshape(lowlevel.shape)
    (grad_coarse_pad,) = expand_back(grad_joined[low_share:])
    grad_coarse = rim_sums(grad_coarse_pad, 1)
    proj_grad_pre, g_proj_gain, g_proj_shift = norm_backward(
        grad_coarse, proj_kept, mid_gain[5], valid_mask, pixel_count
    )
    proj_grad_low = proj_grad_pre.astype(jnp.bfloat16)
    grad_branches = channel_sum(
        jnp.einsum("oc,orw->crw", ordered, proj_grad_low, preferred_element_type=jnp.float32)
    )
    proj_term = (
        jnp.einsum("orw,crw->oc", proj_grad_low, gathered, preferred_element_type=jnp.float32)
        .reshape(branch_width, channel_devices, 5, branch_width)
        .transpose(0, 2, 1, 3)
        .reshape(branch_width, -1)
    )
    grad_broad = grad_branches[4 * branch_width :]
    grad_pool_act = pixel_sums(
        jnp.dot(jnp.sum(grad_broad * valid_mask[None], axis=2), member, precision=HIGHEST)
    )
    gate_value = jax.nn.sigmoid(pool_shifted)
    grad_pool_shifted = grad_pool_act * gate_value * (1.0 + pool_shifted * (1.0 - gate_value))
    g_pool_gain = jnp.sum(grad_pool_shifted * pool_normed, axis=1)
    g_pool_shift = jnp.sum(grad_pool_shifted, axis=1)
    grad_pool_normed = mid_gain[4][:, None] * grad_pool_shifted
    grad_pool_pre = pool_scale[:, None] * (
        grad_pool_normed
        - (mid_gain[4] * g_pool_shift / image_total)[:, None]
        - pool_normed * (mid_gain[4] * g_pool_gain / image_total)[:, None]
    )
    pool_grad_low = grad_pool_pre.astype(jnp.bfloat16)
    g_w_pool = jnp.dot(pool_grad_low, pooled.T, preferred_element_type=jnp.float32)
    grad_pooled = (
        jnp.dot(w_pool.T, pool_grad_low, preferred_element_type=jnp.float32) / image_area[None, :]
    )
    spread_grad = jnp.dot(grad_pooled, member.T, precision=HIGHEST)
    branch_grad_pre, g_branch_gain, g_branch_shift = norm_backward(
        grad_branches[: 4 * branch_width], branch_kept, branch_gain, valid_mask, pixel_count
    )
    branch_grad_low = branch_grad_pre.astype(jnp.bfloat16)
    plain_grad = branch_grad_low[:branch_width]
    g_plain_weight = jnp.einsum(
        "orw,crw->oc", plain_grad, inner, preferred_element_type=jnp.float32
    )
    grad_padded = jnp.zeros(padded.shape, jnp.float32)
    grad_padded = grad_padded.at[:, reach : reach + strip_rows].add(
        jnp.einsum("oc,orw->crw", w_one, plain_grad, preferred_element_type=jnp.float32)
        + spread_grad[:, :, None]
    )
    atrous_grads = []
    for branch_index, dilation in enumerate(DILATIONS):
        lower_row = reach - dilation
        grad_piece, weight_piece = dilated_backward(
            padded[:, lower_row : reach + strip_rows + dilation],
            w_atrous[branch_index],
            dilation,
            coarse_masks[dilation],
            branch_grad_low[(branch_index + 1) * branch_width : (branch_index + 2) * branch_width],
        )
        grad_padded = grad_padded.at[:, lower_row : reach + strip_rows + dilation].add(grad_piece)
        atrous_grads.append(weight_piece)
    grad_shard = channel_sum(rim_sums(grad_padded, reach))
    g_feats = (grad_shard * valid_mask[None]).reshape(feats.shape)
    summed = (
        lax.psum(g_plain_weight.astype(jnp.bfloat16), "row").astype(jnp.float32),
        lax.psum(jnp.stack(atrous_grads).astype(jnp.bfloat16), "row").astype(jnp.float32),
        lax.psum(proj_term.astype(jnp.bfloat16), "row").astype(jnp.float32),
        lax.psum(g_low_weight.astype(jnp.bfloat16), "row").astype(jnp.float32),
        lax.psum(g_first_weight.astype(jnp.bfloat16), "row").astype(jnp.float32),
        lax.psum(g_second_weight.astype(jnp.bfloat16), "row").astype(jnp.float32),
    )
    first_summed = summed[4].reshape(dec_out, 9, channel_devices, low_share + branch_width)
    g_w_dec1 = jnp.concatenate(
        [
            first_summed[:, :, :, :low_share].reshape(dec_out, 9, LOWC),
            first_summed[:, :, :, low_share:].reshape(dec_out, 9, -1),
        ],
        axis=2,
    )
    g_w_proj = summed[2]
    g_mid_gain = jnp.concatenate(
        [g_branch_gain.reshape(4, branch_width), g_pool_gain[None], g_proj_gain[None]], axis=0
    )
    g_mid_shift = jnp.concatenate(
        [g_branch_shift.reshape(4, branch_width), g_pool_shift[None], g_proj_shift[None]], axis=0
    )
    g_dec_gain = jnp.stack([g_first_gain, g_second_gain])
    g_dec_shift = jnp.stack([g_first_shift, g_second_shift])
    return (
        logits,
        g_feats,
        g_lowlevel,
        summed[0],
        summed[1],
        g_w_pool,
        g_w_proj,
        summed[3],
        g_w_dec1,
        summed[5],
        class_grads[0],
        class_grads[1],
        g_mid_gain,
        g_mid_shift,
        g_low_gain,
        g_low_shift,
        g_dec_gain,
        g_dec_shift,
    )


def solution(mesh):
    placed = (
        P("ch", "row"),
        P("ch", "row"),
        P(),
        P(),
        P("ch", None),
        P(None, "ch", None, None),
        P("ch", None),
        P("ch", None),
        P(None, "ch"),
        P("ch", None, None),
        P("ch", None, None),
        P(),
        P(),
        P(None, "ch"),
        P(None, "ch"),
        P("ch"),
        P("ch"),
        P(None, "ch"),
        P(None, "ch"),
        P(None, ("row", "ch")),
    )
    return jax.shard_map(
        local,
        mesh=mesh,
        in_specs=placed,
        out_specs=(
            P(None, ("row", "ch")),
            P("ch", "row"),
            P("ch", "row"),
            P("ch", None),
            P(None, "ch", None, None),
            P("ch", None),
            P("ch", None),
            P(None, "ch"),
            P("ch", None, None),
            P("ch", None, None),
            P(),
            P(),
            P(None, "ch"),
            P(None, "ch"),
            P("ch"),
            P("ch"),
            P(None, "ch"),
            P(None, "ch"),
        ),
        check_vma=False,
    )
```

profile of v0, /device:TPU:0, one launch (start us, length us, event | category | flops | bytes accessed | tf_op | source)
XLA Modules:
  0.0 2343.8 jit_solution(1446719707495281754)
XLA Ops:
  28.6 26.0 %all-gather.6.cloned.1.call-done = bf16[2048,36,32]{0,2,1:T(8,128)(2,1)} async-done(((bf16[512,36,32]{0,2,1:T(8,128)(2,1)}), bf16[2048,36,32]{0,2,1:T(8,128)(2,1)}) %all-gather.6.cloned.1.call-update) | async-done | bytes 4718608 | tf_op jit(solution)/shard_map/all_gather | solution.py:80
  84.9 80.1 %collective-permute-done = bf16[2048,18,32]{0,2,1:T(8,128)(2,1)} collective-permute-done((bf16[2048,18,32]{0,2,1:T(8,128)(2,1)}, bf16[2048,18,32]{0,2,1:T(8,128)(2,1)}, u32[]{:S(2)}, u32[]{:S(2)}) %collective-permute-start) | collective-permute-done | bytes 2359328 | tf_op jit(solution)/shard_map/ppermute | solution.py:22
  259.1 20.2 psum.177
  282.1 34.9 %all-reduce.62 = (f32[2048,6]{0,1:T(8,128)}, f32[256]{0:T(256)}) all-reduce(f32[2048,6]{0,1:T(8,128)} %fusion.659, f32[256]{0:T(256)} %multiply_reduce_fusion.6), channel_id=1, replica_groups=mesh['row'=8,'ch'=4] {'row'}, use_global_device_ids=true, to_apply=%region_21.22 | all-reduce | flops 12544 | bytes 100352 | tf_op jit(solution)/shard_map/psum | solution.py:90
  334.7 63.5 %all-gather.8.cloned.1.call-done = bf16[1280,36,32]{1,2,0:T(8,128)(2,1)} async-done(((bf16[320,36,32]{1,2,0:T(8,128)(2,1)}), bf16[1280,36,32]{1,2,0:T(8,128)(2,1)}) %all-gather.8.cloned.1.call-update) | async-done | bytes 2949136 | tf_op jit(solution)/shard_map/all_gather | solution.py:80
  416.0 21.4 all-reduce.61
  505.0 65.8 %all-gather.10.cloned.1.call-done = bf16[304,144,128]{2,1,0:T(8,128)(2,1)} async-done(((bf16[76,144,128]{2,1,0:T(8,128)(2,1)}), bf16[304,144,128]{2,1,0:T(8,128)(2,1)}) %all-gather.10.cloned.1.call-update) | async-done | bytes 11206672 | tf_op jit(solution)/shard_map/all_gather | solution.py:80
  598.6 20.4 fusion.6
  685.7 21.5 multiply_reduce_fusion.4
  707.2 22.6 psum.182
  762.7 53.7 %all-to-all-done.1 = bf16[4,64,4608]{2,1,0:T(8,128)(2,1)} async-done(((bf16[4,64,4608]{2,1,0:T(8,128)(2,1)}), bf16[4,64,4608]{2,1,0:T(8,128)(2,1)}, u32[]{:S(2)}, u32[]{:S(2)}) %all-to-all-start.1) | async-done | bytes 2359328 | tf_op jit(solution)/shard_map/all_to_all | solution.py:339
  907.9 20.6 multiply_reduce_fusion.1
  928.5 19.8 psum.184
  976.6 19.1 psum.186
  1042.1 35.6 %fusion.696 = (bf16[256,146,130]{2,0,1:T(8,128)(2,1)}, f32[256,146,130]{2,0,1:T(8,128)}) fusion(bf16[9,64,146,130]{3,1,2,0:T(8,128)(2,1)} %bitcast_dynamic-update-slice_fusion.9, bf16[64,9,256]{2,0,1:T(8,128)(2,1)S(1)} %copy-done.71), kind=kOutput, calls=%fused_computation.913 | convolution fusion | flops 5602288640 | bytes 51313152 | tf_op jit(solution)/shard_map/otc,torw->crw/dot_general | solution.py:182
  1102.5 75.5 %reduce-scatter.10.cloned.1.call-done = bf16[64,144,128]{2,0,1:T(8,128)(2,1)} async-done(((bf16[256,144,128]{2,0,1:T(8,128)(2,1)}), bf16[64,144,128]{2,0,1:T(8,128)(2,1)}) %reduce-scatter.10.cloned.1.call-update) | async-done | bytes 2359312 | tf_op jit(solution)/shard_map/reduce_scatter | solution.py:84
  1184.5 21.4 psum.187
  1251.6 75.6 %copy.420 = bf16[9,64,146,130]{2,1,0,3:T(8,128)(2,1)} copy(bf16[9,64,146,130]{3,1,2,0:T(8,128)(2,1)} %bitcast_dynamic-update-slice_fusion) | data formatting | bytes 43729920 | tf_op jit(solution)/shard_map/stack | solution.py:183
  1327.2 29.4 %convolution_bitcast_fusion.3 = f32[304,146,130]{0,1,2:T(8,128)} fusion(bf16[64,9,304,1]{2,0,1,3:T(8,128)(2,1)S(1)} %reshape.1131, bf16[9,64,146,130]{2,1,0,3:T(8,128)(2,1)} %copy.420), kind=kOutput, calls=%fused_computation.34 | convolution fusion | flops 6646947840 | bytes 45294848 | tf_op jit(solution)/shard_map/otc,torw->crw/dot_general | solution.py:182
  1356.6 54.2 %copy.421 = f32[304,146,130]{2,1,0:T(8,128)} copy(f32[304,146,130]{0,1,2:T(8,128)} %convolution_bitcast_fusion.3) | data formatting | bytes 46159360 | tf_op jit(solution)/shard_map/otc,torw->crw/dot_general | solution.py:182
  1410.7 24.6 %convert.224 = bf16[304,146,130]{2,1,0:T(8,128)(2,1)} convert(f32[304,146,130]{2,1,0:T(8,128)} %copy.421) | non-fusion elementwise | flops 5769920 | bytes 34619520 | tf_op jit(solution)/shard_map/convert.119
  1440.3 22.9 slice.1120
  1627.2 22.4 psum.188
  1873.2 20.4 convolution_bitcast_fusion.1
  1893.6 26.1 %convolution_bitcast_fusion = f32[2048,72,68]{0,2,1:T(8,128)} fusion(bf16[9,64,72,68]{1,3,2,0:T(8,128)(2,1)} %bitcast_dynamic-update-slice_fusion.18, bf16[3,64,9,2048]{3,1,2,0:T(8,128)(2,1)} %param.51), kind=kOutput, calls=%fused_computation.29 | convolution fusion | flops 11551113216 | bytes 54411264 | tf_op jit(solution)/shard_map/otc,torw->crw/dot_general | solution.py:182
  1956.0 19.8 fusion.12
  1975.8 22.7 fusion.670
  2008.9 101.0 %collective-permute-done.14 = bf16[2048,18,32]{0,2,1:T(8,128)(2,1)S(1)} collective-permute-done((bf16[2048,18,32]{0,2,1:T(8,128)(2,1)S(1)}, bf16[2048,18,32]{0,2,1:T(8,128)(2,1)S(1)}, u32[]{:S(2)}, u32[]{:S(2)}) %collective-permute-start.14) | collective-permute-done | bytes 2359328 | tf_op jit(solution)/shard_map/ppermute | solution.py:22
  2139.7 28.4 %all-to-all-done = bf16[64,4,4608]{2,0,1:T(8,128)(2,1)} async-done(((bf16[64,4,4608]{2,0,1:T(8,128)(2,1)}), bf16[64,4,4608]{2,0,1:T(8,128)(2,1)}, u32[]{:S(2)}, u32[]{:S(2)}) %all-to-all-start) | async-done | bytes 2359328 | tf_op jit(solution)/shard_map/all_to_all | solution.py:319
  2170.5 42.4 %all-reduce.58 = (f32[21,256]{1,0:T(8,128)}, f32[21]{0:T(128)}) all-reduce(f32[21,256]{1,0:T(8,128)S(1)} %convolution_bitcast_fusion.19, f32[21]{0:T(128)S(1)} %convert_reduce_fusion.1), channel_id=1, replica_groups=mesh['row'=8,'ch'=4] {'row','ch'}, use_global_device_ids=true, to_apply=%region_70.71 | all-reduce | flops 5397 | bytes 43176 | tf_op jit(solution)/shard_map/psum | solution.py:329
  2221.8 39.3 %psum.195 = bf16[48,64]{1,0:T(8,128)(2,1)S(1)} all-reduce(bf16[48,64]{1,0:T(8,128)(2,1)S(1)} %fusion.525), channel_id=1, replica_groups=mesh['row'=8,'ch'=4] {'row'}, use_global_device_ids=true, to_apply=%region_67.68 | all-reduce | flops 3072 | bytes 12288 | tf_op jit(solution)/shard_map/psum | solution.py:433
  2305.8 24.9 %reduce-scatter.14.cloned.1.call-done = bf16[512,36,32]{0,2,1:T(8,128)(2,1)} async-done(((bf16[2048,36,32]{0,2,1:T(8,128)(2,1)}), bf16[512,36,32]{0,2,1:T(8,128)(2,1)}) %reduce-scatter.14.cloned.1.call-update) | async-done | bytes 1179664 | tf_op jit(solution)/shard_map/reduce_scatter | solution.py:84
  (936 shorter events, 1149.2 us)
Async XLA Ops:
  7.2 47.4 %all-gather.6.cloned.1.call-start = ((), (), s32[]{:S(2)}) async-start(), calls=%async_computation.8 | async-start | bytes 5898240 | tf_op jit(solution)/shard_map/all_gather | solution.py:80
  14.3 318.9 %reduce-scatter.8.cloned.1.call-start = ((), (), s32[]{:S(2)}) async-start(), calls=%async_computation.7 | async-start | bytes 2211840 | tf_op jit(solution)/shard_map/reduce_scatter | solution.py:84
  20.8 377.3 %all-gather.8.cloned.1.call-start = ((), (), s32[]{:S(2)}) async-start(), calls=%async_computation.9 | async-start | bytes 13107200 | tf_op jit(solution)/shard_map/all_gather | solution.py:80
  59.9 105.1 %collective-permute-start = (bf16[2048,18,32]{0,2,1:T(8,128)(2,1)}, bf16[2048,18,32]{0,2,1:T(8,128)(2,1)}, u32[]{:S(2)}, u32[]{:S(2)}) collective-permute-start(bf16[2048,18,32]{0,2,1:T(8,128)(2,1)} %get-tuple-element.385), channel_id=1, source_target_pairs={{0,4},{4,8},{8,12},{12,16},{16,20},{20,24},{24,28},{1,5},{5,9},{9,... | collective-permute-start | bytes 7077896 | tf_op jit(solution)/shard_map/ppermute | solution.py:22
  67.9 108.7 %collective-permute-start.1 = (bf16[2048,18,32]{0,2,1:T(8,128)(2,1)}, bf16[2048,18,32]{0,2,1:T(8,128)(2,1)}, u32[]{:S(2)}, u32[]{:S(2)}) collective-permute-start(bf16[2048,18,32]{0,2,1:T(8,128)(2,1)} %get-tuple-element.384), channel_id=1, source_target_pairs={{4,0},{8,4},{12,8},{16,12},{20,16},{24,20},{28,24},{5,1},{9,5},{13... | collective-permute-start | bytes 7077896 | tf_op jit(solution)/shard_map/ppermute | solution.py:23
  330.0 240.8 %all-gather.10.cloned.1.call-start = ((), (), s32[]{:S(2)}) async-start(), calls=%async_computation.10 | async-start | bytes 14008320 | tf_op jit(solution)/shard_map/all_gather | solution.py:80
  330.5 131.5 %copy-start.140 = (f32[12]{0:T(128)}, f32[12]{0:T(128)S(1)}, u32[]{:S(2)}) copy-start(f32[12]{0:T(128)S(1)} %convert_element_type.727) | copy-start | bytes 148
  456.7 6.6 collective-permute-start.2
  460.7 5.5 collective-permute-start.3
  499.7 343.5 %all-gather.12.cloned.1.call-start = ((), (), s32[]{:S(2)}) async-start(), calls=%async_computation.11 | async-start | bytes 11796480 | tf_op jit(solution)/shard_map/all_gather | solution.py:80
  504.9 245.2 %copy-start.116 = (f32[64]{0:T(128)}, f32[64]{0:T(128)S(1)}, u32[]{:S(2)}) copy-start(f32[64]{0:T(128)S(1)} %get-tuple-element.488) | copy-start | bytes 772
  504.9 245.2 %copy-start.153 = (f32[64]{0:T(128)}, f32[64]{0:T(128)S(1)}, u32[]{:S(2)}) copy-start(f32[64]{0:T(128)S(1)} %get-tuple-element.455) | copy-start | bytes 772
  585.7 13.0 collective-permute-start.4
  589.0 9.6 collective-permute-start.5
  758.0 58.4 %all-to-all-start.1 = ((bf16[4,64,4608]{2,1,0:T(8,128)(2,1)}), bf16[4,64,4608]{2,1,0:T(8,128)(2,1)}, u32[]{:S(2)}, u32[]{:S(2)}) async-start(bf16[4,64,4608]{2,1,0:T(8,128)(2,1)} %bitcast.1354), calls=%async_computation.2 | async-start | bytes 4718592 | tf_op jit(solution)/shard_map/all_to_all | solution.py:339
  762.6 415.4 %reduce-scatter.10.cloned.1.call-start = ((), (), s32[]{:S(2)}) async-start(), calls=%async_computation.12 | async-start | bytes 11796480 | tf_op jit(solution)/shard_map/reduce_scatter | solution.py:84
  844.1 13.2 collective-permute-start.6
  847.5 9.8 collective-permute-start.7
  1078.7 16.5 collective-permute-start.8
  1080.7 14.6 collective-permute-start.9
  1101.1 479.3 %reduce-scatter.12.cloned.1.call-start = ((), (), s32[]{:S(2)}) async-start(), calls=%async_computation.13 | async-start | bytes 14008320 | tf_op jit(solution)/shard_map/reduce_scatter | solution.py:84
  1437.7 25.5 %collective-permute-start.10 = (bf16[304,1,128]{2,1,0:T(2,128)(2,1)S(1)}, bf16[304,1,128]{2,1,0:T(2,128)(2,1)S(1)}, u32[]{:S(2)}, u32[]{:S(2)}) collective-permute-start(bf16[304,1,128]{2,1,0:T(2,128)(2,1)S(1)} %get-tuple-element.365), channel_id=1, source_target_pairs={{0,4},{4,8},{8,12},{12,16},{16,20},{20,24},{24,28},{1,5},{5,9},{9,... | collective-permute-start | bytes 233480 | tf_op jit(solution)/shard_map/ppermute | solution.py:22
  1439.0 24.2 %collective-permute-start.11 = (bf16[304,1,128]{2,1,0:T(2,128)(2,1)S(1)}, bf16[304,1,128]{2,1,0:T(2,128)(2,1)S(1)}, u32[]{:S(2)}, u32[]{:S(2)}) collective-permute-start(bf16[304,1,128]{2,1,0:T(2,128)(2,1)S(1)} %get-tuple-element.366), channel_id=1, source_target_pairs={{4,0},{8,4},{12,8},{16,12},{20,16},{24,20},{28,24},{5,1},{9,5},{13... | collective-permute-start | bytes 233480 | tf_op jit(solution)/shard_map/ppermute | solution.py:23
  1491.5 253.3 %reduce-scatter.16.cloned.1.call-start = ((), (), s32[]{:S(2)}) async-start(), calls=%async_computation.16 | async-start | bytes 3686400
  1613.6 12.2 collective-permute-start.12
  1617.1 8.7 collective-permute-start.13
  1660.2 559.3 %all-gather.14.cloned.1.call-start = ((), (), s32[]{:S(2)}) async-start(), calls=%async_computation.15 | async-start | bytes 2211840 | tf_op jit(solution)/shard_map/all_gather | solution.py:80
  1793.9 487.4 %all-reduce.66.cloned.1.call-start = ((), (), s32[]{:S(2)}) async-start(), calls=%async_computation.17 | async-start | bytes 17072128 | tf_op jit(solution)/shard_map/psum | solution.py:434
  1956.0 374.7 %reduce-scatter.14.cloned.1.call-start = ((), (), s32[]{:S(2)}) async-start(), calls=%async_computation.14 | async-start | bytes 5898240 | tf_op jit(solution)/shard_map/reduce_scatter | solution.py:84
  1998.8 111.0 %collective-permute-start.14 = (bf16[2048,18,32]{0,2,1:T(8,128)(2,1)S(1)}, bf16[2048,18,32]{0,2,1:T(8,128)(2,1)S(1)}, u32[]{:S(2)}, u32[]{:S(2)}) collective-permute-start(bf16[2048,18,32]{0,2,1:T(8,128)(2,1)S(1)} %get-tuple-element.371), channel_id=1, source_target_pairs={{0,4},{4,8},{8,12},{12,16},{16,20},{20,24},{24,28},{1,5},{5,9},{9,... | collective-permute-start | bytes 7077896 | tf_op jit(solution)/shard_map/ppermute | solution.py:22
  2002.9 106.9 %collective-permute-start.15 = (bf16[2048,18,32]{0,2,1:T(8,128)(2,1)S(1)}, bf16[2048,18,32]{0,2,1:T(8,128)(2,1)}, u32[]{:S(2)}, u32[]{:S(2)}) collective-permute-start(bf16[2048,18,32]{0,2,1:T(8,128)(2,1)S(1)} %get-tuple-element.372), channel_id=1, source_target_pairs={{4,0},{8,4},{12,8},{16,12},{20,16},{24,20},{28,24},{5,1},{9,5},{13... | collective-permute-start | bytes 7077896 | tf_op jit(solution)/shard_map/ppermute | solution.py:23
  2135.0 33.1 %all-to-all-start = ((bf16[64,4,4608]{2,0,1:T(8,128)(2,1)}), bf16[64,4,4608]{2,0,1:T(8,128)(2,1)}, u32[]{:S(2)}, u32[]{:S(2)}) async-start(bf16[64,4,4608]{2,0,1:T(8,128)(2,1)} %copy.416), calls=%async_computation.1 | async-start | bytes 4718592 | tf_op jit(solution)/shard_map/all_to_all | solution.py:319
  (250 other events, 5119.5 us)
Sparse Core Ops, SparseCore 0:
  14.4 40.1 all-gather.5
  57.2 29.4 reduce-scatter.7
  330.1 68.0 all-gather.7
  499.8 70.9 all-gather.9
  755.9 87.2 all-gather.11
  1101.2 76.7 reduce-scatter.9
  1491.6 88.7 reduce-scatter.11
  1660.3 33.1 reduce-scatter.15
  1794.0 18.7 all-gather.13
  1956.1 325.1 all-reduce.65
  2283.8 46.8 reduce-scatter.13
where the time goes:
time: 2350 us; the launch traced here: 2340 us
  matrix products  602 us (26%)
  waiting for transfers between devices  563 us (24%)
  local copies, waits for them, and re-layouts  472 us (20%)
  blocking collectives  333 us (14%)
  other arithmetic  308 us (13%)
  starting transfers between devices  47.7 us (2%)
    psum x12, blocking collectives, pixel_sums(): return lax.psum(values, 'row')  251 us
    dot_general x45, matrix products, dilated_forward(): jnp.einsum('oc,crw->orw', weight[:, row_tap * 3 + col_tap], window_in, pr...  229 us
    dot_general x45, matrix products, dilated_backward(): jnp.einsum('orw,crw->oc', masked, window_in, preferred_element_type=jnp.f...  208 us
    ppermute x8, waiting for transfers between devices, with_halo(): before = lax.ppermute(last, axis, up)  181 us
    all_gather x5, waiting for transfers between devices, channel_gather(): return lax.all_gather(values, 'ch', axis=0, tiled=True)  168 us
    dot_general x5, matrix products, dilated_backward(): jnp.einsum('otc,torw->crw', weight, jnp.stack(placed), preferred_element_...  124 us
    reduce_scatter x4, waiting for transfers between devices, channel_sum(): lax.psum_scatter(values.astype(jnp.bfloat16), 'ch', scatter_dimension=0,...  113 us
    unnamed x549, local copies, waits for them, and re-layouts  111 us
  transfers between devices with their start and end apart: 29, of which 13 were waited for; matrix products, arithmetic and copies ran while one was open for 28% of the time, Pallas kernels for 0%

commit v1 on v0

v1 whole, which is shorter than its diff:
```python
import jax
import jax.numpy as jnp
from jax import lax
from jax.experimental import pallas as pl
from jax.experimental.pallas import tpu as pltpu
from jax.sharding import PartitionSpec as P

LOWC = 48
WS = 32
WF = 4 * WS
REACH = 18
PAD = 640
EPSILON = 1e-05
HIGHEST = lax.Precision.HIGHEST
BF = jnp.bfloat16
F32 = jnp.float32
BOTH = ("row", "ch")
VMEM_LIMIT = 56 * 1024 * 1024
CHUNKS = (((0, 1, 2), True),)


def params():
    return pltpu.CompilerParams(vmem_limit_bytes=VMEM_LIMIT)


def dot(a, b):
    return jnp.dot(a, b, preferred_element_type=F32)


def dot_nt(a, b):
    return lax.dot_general(a, b, (((1,), (1,)), ((), ())), preferred_element_type=F32)


def tiles(extent, size):
    return [(start, min(size, extent - start)) for start in range(0, extent, size)]


class Images:
    def __init__(self, heights_ref, widths_ref):
        self.ends, self.widths, total = [], [], 0
        for i in range(heights_ref.shape[0]):
            total = total + heights_ref[i]
            self.ends.append(total)
            self.widths.append(widths_ref[i])
        self.total = total

    def image(self, rows, factor=1):
        return sum((rows >= end * factor).astype(jnp.int32) for end in self.ends)

    def same(self, rows, offset, factor=1):
        others = rows + offset
        inside = (rows >= 0) & (rows < self.total * factor) & (others >= 0) & (others < self.total * factor)
        return jnp.where(inside & (self.image(rows, factor) == self.image(others, factor)), 1.0, 0.0)

    def limit(self, rows, factor=1):
        image = self.image(rows, factor)
        value = jnp.zeros(rows.shape, jnp.int32)
        for i, width in enumerate(self.widths):
            value = jnp.where(image == i, width * factor, value)
        return jnp.where(rows >= 0, value, 0)


def iota(shape, axis):
    return lax.broadcasted_iota(jnp.int32, shape, axis)


def split(index, size):
    return jnp.right_shift(index, size.bit_length() - 1), jnp.bitwise_and(index, size - 1)


def tap_rows(images, rows, col):
    masks = [images.same(rows, -a * rate) for rate in (6, 12, 18) for a in (-1, 1)]
    return masks + [jnp.where(col < images.limit(rows), 1.0, 0.0)]


def strip_geometry_kernel(heights, widths, places, rows_ref, member_ref, fine_ref):
    images = Images(heights, widths)
    pixels = rows_ref.shape[1]
    row, col = split(places[0] * pixels + iota((1, pixels), 1), WS)
    values = tap_rows(images, row, col)
    for i, value in enumerate(values):
        rows_ref[i : i + 1] = value
    rows_ref[7:8] = jnp.zeros((1, pixels), F32)
    image = images.image(row)
    number = iota(member_ref.shape, 0)
    member_ref[...] = (jnp.where(number == image, 1.0, 0.0) * values[6]).astype(BF)
    row, col = split(places[0] * 16 * pixels + iota(fine_ref.shape, 1), WF)
    fine_ref[...] = jnp.where(col < images.limit(row, 4), 1.0, 0.0).astype(BF)


def geometry_kernel(
    margin, heights, widths, places,
    canvas_ref, member_ref, strips_ref, shares_ref, fines_ref, mine_ref, window_ref, ext_ref, masks_ref, enlarge_ref,
):
    images = Images(heights, widths)
    groups, _, pixels = canvas_ref.shape
    everyone, share = shares_ref.shape[0], mine_ref.shape[1]
    place = places[1]
    shape = (groups, pixels)
    row, col = split(iota(shape, 0) * pixels + iota(shape, 1), WS)
    values = tap_rows(images, row, col)
    for i, value in enumerate(values):
        canvas_ref[:, i] = value
    canvas_ref[:, 7] = jnp.zeros(shape, F32)
    image = images.image(row)
    for i in range(member_ref.shape[1]):
        member_ref[:, i] = jnp.where(image == i, values[6], 0.0)
    strips_ref[...] = jnp.sum(values[6], axis=1, keepdims=True)

    def counted(pixels, cols, factor):
        row, col = split(iota((everyone, pixels), 0) * pixels + iota((everyone, pixels), 1), cols)
        return jnp.sum(jnp.where(col < images.limit(row, factor), 1.0, 0.0), axis=1, keepdims=True)

    shares_ref[...] = counted(share, WS, 1)
    rows = masks_ref.shape[1] // WF
    number = iota((everyone, rows), 0) * rows + iota((everyone, rows), 1)
    fines_ref[...] = jnp.sum(images.limit(number, 4).astype(F32), axis=1, keepdims=True)

    row, col = split(place * share + iota((1, share), 1), WS)
    valid = jnp.where(col < images.limit(row), 1.0, 0.0)
    image = images.image(row)
    last = mine_ref.shape[0] - 8
    mine_ref[:last] = jnp.where(iota((last, share), 0) == image, 1.0, 0.0) * valid
    mine_ref[last:] = jnp.broadcast_to(valid, (8, share))
    row, col = split(place * share - margin + iota(window_ref.shape, 1), WS)
    window_ref[...] = jnp.where(col < images.limit(row), 1.0, 0.0)

    first = place * rows
    row, col = split(iota((1, masks_ref.shape[1]), 1), WF)
    for i, offset in enumerate((-1, 1)):
        masks_ref[i : i + 1] = images.same(first + row, offset, 4)
    window, ext = enlarge_ref.shape
    at_row, at_col = split(place * share - margin + iota((window, 1), 0), WS)
    for start, size in tiles(ext, 512):
        row, col = split(start + iota((1, size), 1), WF)
        row = first - 1 + row
        valid = jnp.where(col < images.limit(row, 4), 1.0, 0.0)
        ext_ref[:, start : start + size] = valid

        def weights(phase):
            middle = jnp.where((phase == 0) | (phase == 3), 0.625, 0.875)
            before = jnp.where(phase == 0, 0.375, jnp.where(phase == 1, 0.125, 0.0))
            after = jnp.where(phase == 3, 0.375, jnp.where(phase == 2, 0.125, 0.0))
            return middle, before, after

        def part(there, here, middle, before, after):
            apart = there - here
            return jnp.where(apart == 0, middle, jnp.where(apart == -1, before, jnp.where(apart == 1, after, 0.0)))

        q, phase = split(row, 4)
        middle, before, after = weights(phase)
        by_row = part(at_row, q, middle * valid, before * images.same(q, -1) * valid, after * images.same(q, 1) * valid)
        q, phase = split(col, 4)
        enlarge_ref[:, start : start + size] = (by_row * part(at_col, q, *weights(phase))).astype(BF)


def geometry_call(kernel, heights, widths, places, outputs):
    smem = pl.BlockSpec(memory_space=pltpu.SMEM)
    return pl.pallas_call(
        kernel,
        in_specs=[smem] * 3,
        out_specs=[pl.BlockSpec(memory_space=pltpu.VMEM)] * len(outputs),
        out_shape=outputs,
        compiler_params=params(),
        cost_estimate=pl.CostEstimate(flops=20000000, bytes_accessed=6000000, transcendentals=0),
    )(heights, widths, places)


def gather_blocks(x):
    count, me = lax.axis_size("ch"), lax.axis_index("ch")
    if count == 4:
        cross = lambda v, m: lax.ppermute(v, "ch", [(i, i ^ m) for i in range(count)])
        far = cross(x, 2)
        near = cross(x, 1)
        return [x, near, far, cross(far, 1)], [me, me ^ 1, me ^ 2, me ^ 3]
    every = lax.all_gather(x, "ch", axis=0)
    return [every[i] for i in range(count)], [jnp.int32(i) for i in range(count)]


def swap_row(x):
    groups, strip = lax.axis_size("row"), lax.axis_index("row")
    number = jnp.arange(groups, dtype=jnp.int32)
    if groups != 8:
        return lax.all_to_all(x, "row", 0, 0), number
    pick = lambda i: lax.dynamic_index_in_dim(x, i, 0, False)
    blocks = [pick(strip)]
    for m in range(1, groups):
        blocks.append(lax.ppermute(pick(strip ^ m), "row", [(i, i ^ m) for i in range(groups)]))
    return jnp.stack(blocks), number ^ strip


def swap_ch(x):
    count, me = lax.axis_size("ch"), lax.axis_index("ch")
    if count != 4:
        return lax.all_to_all(x, "ch", 0, 0)
    pick = lambda i: lax.dynamic_index_in_dim(x, i, 0, False)
    blocks = [pick(me)]
    for m in (1, 2, 3):
        blocks.append(lax.ppermute(pick(me ^ m), "ch", [(i, i ^ m) for i in range(count)]))
    return jnp.stack(blocks)


def reduce_blocks(blocks):
    count = lax.axis_size("ch")
    if count == 4:
        cross = lambda v, m: lax.ppermute(v, "ch", [(i, i ^ m) for i in range(count)])
        arrived = cross(jnp.stack([blocks[3], blocks[1]]), 1).astype(F32)
        onward = (blocks[2].astype(F32) + arrived[0]).astype(BF)
        return blocks[0].astype(F32) + arrived[1] + cross(onward, 2).astype(F32)
    return lax.psum_scatter(jnp.stack(blocks), "ch", scatter_dimension=0).astype(F32)


def gather_all(top, low):
    groups, count = lax.axis_size("row"), lax.axis_size("ch")
    strip, me = lax.axis_index("row"), lax.axis_index("ch")
    whole = jnp.arange(groups * count, dtype=jnp.int32)
    if groups != 8 or count != 4:
        every = lax.all_gather(jnp.stack([top, low]), BOTH, axis=0)
        top, low = every[:, 0], every[:, 1]
        return (top, top), (low, low), whole, whole
    line = groups // 2

    def around(v, step):
        pairs = [(2 * i + e, 2 * ((i + step) % line) + e) for i in range(line) for e in range(2)]
        return lax.ppermute(v, "row", pairs)

    beside = lambda v: lax.ppermute(v, "row", [(i, i ^ 1) for i in range(groups)])
    across = lambda v: lax.ppermute(v, "ch", [(i, i ^ 2) for i in range(count)])
    core = lambda v: lax.ppermute(v, "ch", [(i, i ^ 1) for i in range(count)])
    top = jnp.stack([top, around(top, 1), around(top, 2), around(top, 3)])
    low = jnp.stack([low, around(low, 1), around(low, 2), around(low, 3)])
    top_beside, low_across = beside(top), across(low)
    top = jnp.concatenate([top, top_beside, across(top), across(top_beside)])
    low = jnp.concatenate([low, low_across, beside(low), beside(low_across)])
    other_strip, other_me = whole // count, whole % count
    z = jnp.mod(strip // 2 - other_strip // 2, line)
    e = (strip ^ other_strip) & 1
    y = ((me ^ other_me) >> 1) & 1
    c = (me ^ other_me) & 1
    return (top, core(top)), (low, core(low)), ((c * 2 + y) * 2 + e) * line + z, ((c * 2 + e) * 2 + y) * line + z


def gather_line(x, rider):
    def along(v, places, step):
        return lax.ppermute(v, "row", [(2 * i + e, 2 * (i + step) + e) for i in places for e in range(2)])

    def beside(v, places):
        return lax.ppermute(v, "row", [(2 * i + e, 2 * i + 1 - e) for i in places for e in range(2)])

    def together(*keys):
        for key, value in zip(keys, lax.optimization_barrier(tuple(got[key] for key in keys))):
            got[key] = value

    got = {(0, 0, 0): x}
    got[-1, 0, 0], got[1, 0, 0] = along(x, (0, 1, 2), 1), along(x, (1, 2, 3), -1)
    got[0, 1, 0] = beside(x, (0, 1, 2, 3))
    together((-1, 0, 0), (1, 0, 0), (0, 1, 0))
    got[-2, 0, 0], got[2, 0, 0] = along(got[-1, 0, 0], (1, 2), 1), along(got[1, 0, 0], (1, 2), -1)
    got[-1, 1, 0], got[1, 1, 0] = beside(got[-1, 0, 0], (1, 2, 3)), beside(got[1, 0, 0], (0,))
    together((-2, 0, 0), (2, 0, 0), (-1, 1, 0), (1, 1, 0), (1, 0, 0))
    got[-3, 0, 0], got[3, 0, 0] = along(got[-2, 0, 0], (2,), 1), along(got[2, 0, 0], (1,), -1)
    got[1, 1, 1] = beside(got[1, 0, 0], (1, 2))
    got[-2, 1, 0], got[2, 1, 0] = beside(got[-2, 0, 0], (3,)), beside(got[2, 0, 0], (0,))
    together((-3, 0, 0), (3, 0, 0), (1, 1, 1), (-2, 1, 0), (2, 1, 0), (-2, 0, 0), (2, 0, 0))
    got[-3, 0, 0], *rider = lax.optimization_barrier((got[-3, 0, 0], *rider))
    got[-2, 1, 1], got[2, 1, 1] = beside(got[-2, 0, 0], (2,)), beside(got[2, 0, 0], (1,))
    got[-3, 1, 0], got[3, 1, 0] = beside(got[-3, 0, 0], (3,)), beside(got[3, 0, 0], (0,))
    return got, rider


def line_part(place, steps, side):
    first = {(1, 1): (0,), (-2, 1): (3,), (2, 1): (0,)}.get((steps, side))
    return (steps, side, 0 if first is None or place in first else 1)


def swap_all(values):
    return lax.all_to_all(values, BOTH, 0, 0)


def tell_all(values):
    count = lax.axis_size("row") * lax.axis_size("ch")
    return swap_all(jnp.broadcast_to(values[None], (count,) + values.shape))


def tell_row(values):
    count = lax.axis_size("row")
    return lax.all_to_all(jnp.broadcast_to(values[None], (count,) + values.shape), "row", 0, 0)


def vector_tile(*vectors):
    rows = [jnp.pad(v, (0, 256 - v.shape[0])).reshape(2, 128) for v in vectors]
    return jnp.pad(jnp.concatenate(rows), ((0, 8 - 2 * len(rows)), (0, 0)))


def to_next(x):
    count = lax.axis_size("row") * lax.axis_size("ch")
    return lax.ppermute(x, BOTH, [(i, i + 1) for i in range(count - 1)])


def to_previous(x):
    count = lax.axis_size("row") * lax.axis_size("ch")
    return lax.ppermute(x, BOTH, [(i + 1, i) for i in range(count - 1)])


def local_moments(x, valid):
    count = jnp.sum(valid)
    mean = jnp.sum(x * valid[None], axis=1) / jnp.maximum(count, 1.0)
    centered = (x - mean[:, None]) * valid[None]
    return mean, jnp.sum(centered * centered, axis=1)


def merge_moments(means, spreads, counts, total):
    mean = jnp.sum(means * counts[:, None], axis=0) / total
    away = means - mean[None]
    var = (jnp.sum(spreads, axis=0) + jnp.sum(counts[:, None] * away * away, axis=0)) / total
    return mean, lax.rsqrt(var + EPSILON)


def silu_slope(y):
    gate = jax.nn.sigmoid(y)
    return gate * (1.0 + y * (1.0 - gate))


def rows_per_step(rows):
    for step in (6, 4, 3, 2):
        if rows % step == 0:
            return step
    return 1


def pack_vectors(out_ref, first, second, more=None):
    more = jnp.zeros((4, 128), F32) if more is None else more
    tile = jnp.concatenate([first[:, :128], first[:, 128:], second[:, :128], second[:, 128:], more], axis=0)
    out_ref[:, :8] = jnp.broadcast_to(tile[None], (out_ref.shape[0], 8, 128))


def as_rows(columns):
    channels = columns[0].shape[0]
    lane = lax.broadcasted_iota(jnp.int32, (channels, 128), 1)
    block = jnp.zeros((channels, 128), F32)
    for i, column in enumerate(columns):
        block = jnp.where(lane == i, column, block)
    turned = block.T
    if channels < 256:
        turned = jnp.concatenate([turned, jnp.zeros((128, 256 - channels), F32)], axis=1)
    return [turned[i : i + 1] for i in range(len(columns))]


def as_columns(rows, channels):
    block = jnp.concatenate(rows + [jnp.zeros((8 - len(rows), rows[0].shape[1]), F32)], axis=0)
    turned = block.T
    return [turned[:channels, i : i + 1] for i in range(len(rows))]


def told_vectors(told):
    return jnp.concatenate([told[:, 0], told[:, 1]], axis=1), jnp.concatenate([told[:, 2], told[:, 3]], axis=1)


def merged(told, counts, inverse):
    means, spreads = told_vectors(told)
    mean = jnp.sum(means * counts, axis=0, keepdims=True) * inverse
    away = means - mean
    var = jnp.sum(spreads + counts * (away * away), axis=0, keepdims=True) * inverse
    return mean, lax.rsqrt(var + EPSILON)


def norm_columns(told_ref, counts_ref, inverse, gain_rows, channels, first=0):
    mean, scale = merged(told_ref[:, first : first + 4], counts_ref[...], inverse)
    return as_columns([mean, scale, gain_rows[0:1], gain_rows[1:2]], channels)


def sums_columns(told_ref, channels):
    first, second = told_vectors(told_ref[...])
    return as_columns([jnp.sum(first, axis=0, keepdims=True), jnp.sum(second, axis=0, keepdims=True)], channels)


def normed_of(pre, cols):
    return (pre - cols[0]) * cols[1]


def activation(pre, cols, valid):
    y = cols[2] * normed_of(pre, cols) + cols[3]
    return (y * jax.nn.sigmoid(y) * valid).astype(BF)


def fold(x):
    total = x[:, :128]
    for at in range(128, x.shape[1], 128):
        total = total + x[:, at : at + 128]
    return total


def moments_step(v, valid, state_ref, first):
    @pl.when(first)
    def _():
        count = jnp.maximum(jnp.sum(valid), 1.0)
        state_ref[0] = jnp.broadcast_to(jnp.sum(v * valid, axis=1, keepdims=True) / count, state_ref.shape[1:])
        state_ref[1] = jnp.zeros(state_ref.shape[1:], F32)
        state_ref[2] = jnp.zeros(state_ref.shape[1:], F32)

    away = (v - state_ref[0, :, 0:1]) * valid
    state_ref[1] += fold(away)
    state_ref[2] += fold(away * away)


def moments_end(state_ref, count, out_ref):
    total = jnp.sum(state_ref[1], axis=1, keepdims=True)
    squares = jnp.sum(state_ref[2], axis=1, keepdims=True)
    mean = state_ref[0, :, 0:1] + total / count
    pack_vectors(out_ref, *as_rows([mean, squares - total * total / count]))


def sums_step(dy, normed, state_ref, first):
    @pl.when(first)
    def _():
        state_ref[...] = jnp.zeros_like(state_ref)

    state_ref[0] += fold(dy)
    state_ref[1] += fold(dy * normed)


def sums_end(state_ref, out_ref):
    pack_vectors(out_ref, *as_rows([jnp.sum(state_ref[i], axis=1, keepdims=True) for i in range(2)]))


def ext_parts(rows_ext, piece):
    own = rows_ext * WF - 2 * WF
    yield 0, slice(0, WF), slice(0, WF)
    for start, size in tiles(own, piece):
        yield 1, slice(start, start + size), slice(WF + start, WF + start + size)
    yield 2, slice(0, WF), slice(WF + own, 2 * WF + own)


def stacked(a_ref, start, lanes, mask_ref, flip, rows):
    first, last = (1, 0) if flip else (0, 1)
    before = a_ref[rows, pl.ds(start, lanes)]
    middle = a_ref[rows, pl.ds(start + WF, lanes)]
    after = a_ref[rows, pl.ds(start + 2 * WF, lanes)]
    before = before * mask_ref[0:1, pl.ds(start, lanes)].astype(BF)
    after = after * mask_ref[1:2, pl.ds(start, lanes)].astype(BF)
    return [after, middle, before] if flip else [before, middle, after]


def columns_joined(acc, outs, flip):
    lanes = acc.shape[1]
    col = lax.broadcasted_iota(jnp.int32, (1, lanes), 1) % WF
    left, right = (acc[2 * outs :], acc[:outs]) if flip else (acc[:outs], acc[2 * outs :])
    left = jnp.where(col > 0, pltpu.roll(left, 1, 1), 0.0)
    right = jnp.where(col < WF - 1, pltpu.roll(right, lanes - 1, 1), 0.0)
    return acc[outs : 2 * outs] + left + right


def forward_weights(w_ref, up, out_ref):
    devices, _, outs, cin = w_ref.shape
    wide, extra = devices * outs, cin - up
    for c in range(devices):
        for b in range(3):
            rows = slice(b * wide + c * outs, b * wide + (c + 1) * outs)
            for a in range(3):
                piece = w_ref[c, 3 * a + b]
                out_ref[rows, a * up : (a + 1) * up] = piece[:, :up]
                if extra:
                    at = 3 * up + a * extra
                    out_ref[rows, at : at + extra] = piece[:, up:]


def backward_weights(w_ref, up, out_ref):
    devices, _, outs, cin = w_ref.shape
    wide, extra = devices * outs, cin - up
    for a in range(3):
        for b in range(3):
            whole = jnp.concatenate([w_ref[c, 3 * a + b] for c in range(devices)], axis=0).astype(F32)
            columns = slice(a * wide, (a + 1) * wide)
            out_ref[b * up : (b + 1) * up, columns] = whole[:, :up].T.astype(BF)
            if extra:
                tail = jnp.concatenate([whole[:, up:], jnp.zeros((wide, 128 - extra), F32)], axis=1).T
                at = 3 * up + b * extra
                out_ref[at : at + extra, columns] = tail[:extra].astype(BF)


def first_kernel(
    lanes,
    proj_prev, proj_own, proj_next, told_proj, counts_c, proj_gain, window_valid,
    enlarge, low_prev, low_own, low_next, told_low, counts_f, low_gain, valid_ext, mask, w_all, scalars,
    a_ref, out_ref, top_ref, bottom_ref, stats_ref, coarse_ref, w_ref, state_ref,
):
    step, last = pl.program_id(0), pl.num_programs(0) - 1
    up = proj_own.shape[0]
    margin, share = proj_prev.shape[1], proj_own.shape[1]

    @pl.when(step == 0)
    def _():
        forward_weights(w_all, up, w_ref)
        cols = norm_columns(told_proj, counts_c, scalars[0], proj_gain, up)
        for ref, start in ((proj_prev, 0), (proj_own, margin), (proj_next, margin + share)):
            part = slice(start, start + ref.shape[1])
            coarse_ref[:, part] = activation(ref[...], cols, window_valid[:, part])
        ext = a_ref.shape[1]
        for start, size in tiles(ext, 512):
            a_ref[:up, start : start + size] = dot(coarse_ref[...], enlarge[:, start : start + size]).astype(BF)
        cols = norm_columns(told_low, counts_f, scalars[1], low_gain, LOWC, 4)
        for which, part, there in ext_parts(ext // WF, 1536):
            a_ref[up:, there] = activation((low_prev, low_own, low_next)[which][:, part], cols, valid_ext[:, there])

    start = pl.multiple_of(step * lanes, 128)
    taps = stacked(a_ref, start, lanes, mask, False, slice(0, up)) + stacked(a_ref, start, lanes, mask, False, slice(up, up + LOWC))
    acc = dot(w_ref[...], jnp.concatenate(taps, axis=0))
    conv_end(acc, False, step, last, start, lanes, valid_ext, out_ref, top_ref, bottom_ref, stats_ref, state_ref)


def conv_end(acc, flip, step, last, start, lanes, valid_ext, out_ref, top_ref, bottom_ref, stats_ref, state_ref):
    outs = out_ref.shape[0]
    v = columns_joined(acc, outs, flip)
    out_ref[...] = v
    moments_step(v, valid_ext[:, pl.ds(start + WF, lanes)], state_ref, step == 0)

    @pl.when(step == 0)
    def _():
        top_ref[...] = v[:, :WF]

    @pl.when(step == last)
    def _():
        bottom_ref[...] = v[:, lanes - WF :]
        count = jnp.maximum(jnp.sum(valid_ext[:, WF : valid_ext.shape[1] - WF]), 1.0)
        moments_end(state_ref, count, stats_ref)


def second_kernel(
    lanes, prev, own, after, told, counts, gain, valid_ext, mask, w_all, scalars,
    a_ref, out_ref, top_ref, bottom_ref, stats_ref, w_ref, state_ref,
):
    step, last = pl.program_id(0), pl.num_programs(0) - 1

    @pl.when(step == 0)
    def _():
        forward_weights(w_all, w_all.shape[3], w_ref)
        cols = norm_columns(told, counts, scalars[1], gain, a_ref.shape[0])
        for which, part, there in ext_parts(a_ref.shape[1] // WF, 768):
            a_ref[:, there] = activation((prev, own, after)[which][:, part], cols, valid_ext[:, there])

    start = pl.multiple_of(step * lanes, 128)
    taps = stacked(a_ref, start, lanes, mask, False, slice(None))
    acc = dot(w_ref[...], jnp.concatenate(taps, axis=0))
    conv_end(acc, False, step, last, start, lanes, valid_ext, out_ref, top_ref, bottom_ref, stats_ref, state_ref)


def class_kernel(
    pre, cotangent, valid, told, counts, gain, w_cls, w_turned, bias, scalars,
    logits_ref, weights_ref, bias_ref, sums_ref, state_ref, cols_ref,
):
    step, last = pl.program_id(0), pl.num_programs(0) - 1
    classes = logits_ref.shape[0]

    @pl.when(step == 0)
    def _():
        for i, col in enumerate(norm_columns(told, counts, scalars[1], gain, pre.shape[0])):
            cols_ref[:, i : i + 1] = col
        weights_ref[...] = jnp.zeros_like(weights_ref)
        bias_ref[...] = jnp.zeros_like(bias_ref)

    cols = [cols_ref[:, i : i + 1] for i in range(4)]
    normed = normed_of(pre[...], cols)
    y = cols[2] * normed + cols[3]
    gate = jax.nn.sigmoid(y)
    act = (y * gate * valid[...]).astype(BF)
    logits_ref[...] = (dot(w_cls[...], act) + bias[...])[:classes]
    weights_ref[...] += dot_nt(cotangent[...], act)
    bias_ref[...] += fold(cotangent[...].astype(F32))
    d = dot(w_turned[...], cotangent[...]).astype(BF).astype(F32)
    dy = d * (gate * (1.0 + y * (1.0 - gate)) * valid[...])
    sums_step(dy, normed, state_ref, step == 0)

    @pl.when(step == last)
    def _():
        sums_end(state_ref, sums_ref)


def back_dz(dy, normed, cols, sums, valid, inverse):
    return ((cols[1] * cols[2]) * (dy - (sums[0] + normed * sums[1]) * (valid * inverse))).astype(BF)


def second_back_kernel(
    lanes,
    prev, own, after, told, counts, gain, sums, cot_prev, cot_own, cot_after, w_turned, valid_ext, mask, w_all,
    first_pre, told_first, gain_first, riders, scalars,
    dz_ref, dy_ref, top_ref, bottom_ref, sums_ref, w_ref, state_ref, cols_ref,
):
    step, last = pl.program_id(0), pl.num_programs(0) - 1

    @pl.when(step == 0)
    def _():
        backward_weights(w_all, w_all.shape[3], w_ref)
        channels = dz_ref.shape[0]
        cols = norm_columns(told, counts, scalars[1], gain, channels)
        totals = sums_columns(sums, channels)
        for which, part, there in ext_parts(dz_ref.shape[1] // WF, 768):
            pre, cot = ((prev, cot_prev), (own, cot_own), (after, cot_after))[which]
            normed = normed_of(pre[:, part], cols)
            valid = valid_ext[:, there]
            d = dot(w_turned[...], cot[:, part]).astype(BF).astype(F32)
            dy = d * silu_slope(cols[2] * normed + cols[3]) * valid
            dz_ref[:, there] = back_dz(dy, normed, cols, totals, valid, scalars[1])
        for i, col in enumerate(norm_columns(told_first, counts, scalars[1], gain_first, channels)):
            cols_ref[:, i : i + 1] = col

    start = pl.multiple_of(step * lanes, 128)
    taps = stacked(dz_ref, start, lanes, mask, True, slice(None))
    acc = dot(w_ref[...], jnp.concatenate(taps, axis=0))
    grad = columns_joined(acc, dy_ref.shape[0], True)
    cols = [cols_ref[:, i : i + 1] for i in range(4)]
    normed = normed_of(first_pre[...], cols)
    dy = grad * silu_slope(cols[2] * normed + cols[3]) * valid_ext[:, pl.ds(start + WF, lanes)]
    dy_ref[...] = dy
    sums_step(dy, normed, state_ref, step == 0)

    @pl.when(step == 0)
    def _():
        top_ref[...] = dy[:, :WF]

    @pl.when(step == last)
    def _():
        bottom_ref[...] = dy[:, lanes - WF :]
        sums_end(state_ref, sums_ref)
        sums_ref[:, 8:] = riders[...]


def first_back_kernel(
    lanes,
    prev, own, after, dy_prev, dy_own, dy_after, told, counts, gain, sums, valid_ext, mask, w_all,
    enlarge, low_pre, told_low, low_gain, scalars,
    dz_ref, window_ref, low_ref, low_sums_ref, w_ref, state_ref, cols_ref,
):
    step, last = pl.program_id(0), pl.num_programs(0) - 1
    up = window_ref.shape[0]

    @pl.when(step == 0)
    def _():
        backward_weights(w_all, up, w_ref)
        channels = dz_ref.shape[0]
        cols = norm_columns(told, counts, scalars[1], gain, channels)
        totals = sums_columns(sums, channels)
        for which, part, there in ext_parts(dz_ref.shape[1] // WF, 768):
            pre, dy = ((prev, dy_prev), (own, dy_own), (after, dy_after))[which]
            normed = normed_of(pre[:, part], cols)
            dz_ref[:, there] = back_dz(dy[:, part], normed, cols, totals, valid_ext[:, there], scalars[1])
        for i, col in enumerate(norm_columns(told_low, counts, scalars[1], low_gain, LOWC, 4)):
            cols_ref[:, i : i + 1] = col
        window_ref[...] = jnp.zeros_like(window_ref)

    start = pl.multiple_of(step * lanes, 128)
    taps = stacked(dz_ref, start, lanes, mask, True, slice(None))
    acc = dot(w_ref[...], jnp.concatenate(taps, axis=0))
    grad = columns_joined(acc[: 3 * up], up, True)
    high = grad.astype(BF)
    rest = (grad - high.astype(F32)).astype(BF)
    part = enlarge[:, pl.ds(start + WF, lanes)]
    window_ref[...] += dot_nt(high, part) + dot_nt(rest, part)
    cols = [cols_ref[:, i : i + 1] for i in range(4)]
    normed = normed_of(low_pre[...], cols)
    dy = columns_joined(acc[3 * up :], LOWC, True)
    dy = dy * silu_slope(cols[2] * normed + cols[3]) * valid_ext[:, pl.ds(start + WF, lanes)]
    low_ref[...] = dy
    sums_step(dy, normed, state_ref, step == 0)

    @pl.when(step == last)
    def _():
        for i in range(2):
            low_sums_ref[i : i + 1] = as_rows([jnp.sum(state_ref[i], axis=1, keepdims=True)])[0]


def decoder_weight_kernel(lanes, outs, dz_ref, a_ref, mask_ref, *refs):
    step = pl.program_id(0)
    start = pl.multiple_of(step * lanes, 128)
    acc_ref = refs[-1]
    wide = dz_ref.shape[0]
    up, extra = wide, a_ref.shape[0] - wide

    @pl.when(step == 0)
    def _():
        acc_ref[...] = jnp.zeros_like(acc_ref)

    taps = stacked(a_ref, start, lanes, mask_ref, False, slice(0, up))
    if a_ref.shape[0] > up:
        taps = taps + stacked(a_ref, start, lanes, mask_ref, False, slice(up, None))
    dz = dz_ref[:, pl.ds(start + WF, lanes)]
    col = lax.broadcasted_iota(jnp.int32, (1, lanes), 1) % WF
    left = pltpu.roll(dz, lanes - 1, 1) * (col < WF - 1).astype(F32).astype(BF)
    right = pltpu.roll(dz, 1, 1) * (col > 0).astype(F32).astype(BF)
    acc_ref[...] += dot_nt(jnp.concatenate([left, dz, right], axis=0), jnp.concatenate(taps, axis=0))

    @pl.when(step == pl.num_programs(0) - 1)
    def _():
        for c in range(wide // outs):
            for b in range(3):
                rows = slice(b * wide + c * outs, b * wide + (c + 1) * outs)
                for a in range(3):
                    refs[0][c, 3 * a + b, :, :up] = acc_ref[rows, a * up : (a + 1) * up].astype(BF)
                    if extra:
                        at = 3 * up + a * extra
                        refs[0][c, 3 * a + b, :, up:] = acc_ref[rows, at : at + extra].astype(BF)


def decoder_weight_grad(dz, a, masks, outs):
    wide, pixels = dz.shape[0], dz.shape[1] - 2 * WF
    cin = a.shape[0]
    lanes = WF * rows_per_step(pixels // WF)
    devices = wide // outs
    whole = pl.BlockSpec(memory_space=pltpu.VMEM)
    return pl.pallas_call(
        lambda *refs: decoder_weight_kernel(lanes, outs, *refs),
        grid=(pixels // lanes,),
        in_specs=[whole] * 3,
        out_specs=whole,
        out_shape=jax.ShapeDtypeStruct((devices, 9, outs, cin), BF),
        scratch_shapes=[pltpu.VMEM((3 * wide, 3 * cin), F32)],
        compiler_params=params(),
        cost_estimate=pl.CostEstimate(flops=18 * cin * wide * pixels, bytes_accessed=2 * (cin + wide) * pixels, transcendentals=0),
    )(dz, a, masks)


def decoder_call(kernel, operands, blocked, smem, outputs, blocked_out, scratch, pixels, flops):
    lanes = WF * rows_per_step(pixels // WF)
    whole = pl.BlockSpec(memory_space=pltpu.VMEM)
    run = lambda channels: pl.BlockSpec((channels, lanes), lambda i: (0, i))
    in_specs = [
        pl.BlockSpec(memory_space=pltpu.SMEM) if i in smem else run(v.shape[0]) if i in blocked else whole
        for i, v in enumerate(operands)
    ]
    out_specs = [run(v.shape[0]) if i in blocked_out else whole for i, v in enumerate(outputs)]
    return pl.pallas_call(
        kernel,
        grid=(pixels // lanes,),
        in_specs=in_specs,
        out_specs=out_specs,
        out_shape=outputs,
        scratch_shapes=scratch,
        compiler_params=params(),
        cost_estimate=pl.CostEstimate(flops=flops, bytes_accessed=16 * 256 * pixels, transcendentals=0),
    )(*operands)


def branch_kernel(centre, from_next, from_prev, valid, out_ref, pieces_ref, stats_ref):
    outs, pixels = centre.shape[1:]
    devices, _, share = pieces_ref.shape
    count = jnp.maximum(jnp.sum(valid[...]), 1.0)
    means, spreads = [], []
    for k in range(4):
        rows = slice(k * outs, (k + 1) * outs)
        v = centre[(k + 3) % 4]
        if k:
            v = v + jnp.concatenate([jnp.zeros((outs, pixels - PAD), F32), from_next[k - 1].astype(F32)], axis=1)
            v = v + jnp.concatenate([from_prev[k - 1].astype(F32), jnp.zeros((outs, pixels - PAD), F32)], axis=1)
        mean = jnp.sum(v * valid[...], axis=1, keepdims=True) / count
        v = (v - mean) * valid[...]
        means.append(mean)
        spreads.append(jnp.sum(v * v, axis=1, keepdims=True))
        out_ref[rows] = v.astype(BF)
        for i in range(devices):
            pieces_ref[i, rows] = v[:, i * share : (i + 1) * share].astype(BF)
    pack_vectors(stats_ref, *as_rows([jnp.concatenate(means, axis=0), jnp.concatenate(spreads, axis=0)]))


def project_kernel(
    swapped, told, counts, gains, w_ref, broad, valid, low_stats, scalars, places, out_ref, left_ref, right_ref, stats_ref
):
    devices, four, share = swapped.shape
    groups = told.shape[0]
    margin = left_ref.shape[1]
    mine = places[0]
    number = lax.broadcasted_iota(jnp.int32, (groups, 1), 0)
    total = broad[...]
    for j in range(devices):
        c = places[1 + j]
        group = told[:, c]
        mean, scale = merged(group, counts[...], scalars[0])
        here = jnp.sum(jnp.where(number == mine, told_vectors(group)[0], 0.0), axis=0, keepdims=True)
        cols = as_columns([mean - here, scale, gains[c, 0:1], gains[c, 1:2]], four)
        total = total + dot(w_ref[c], activation(swapped[j].astype(F32), cols, valid[...]))
    out_ref[...] = total
    left_ref[...] = total[:, :margin]
    right_ref[...] = total[:, share - margin :]
    count = jnp.maximum(jnp.sum(valid[...]), 1.0)
    mean = jnp.sum(total * valid[...], axis=1, keepdims=True) / count
    away = (total - mean) * valid[...]
    pack_vectors(stats_ref, *as_rows([mean, jnp.sum(away * away, axis=1, keepdims=True)]), low_stats[...])


def small_call(kernel, operands, smem, outputs, flops):
    whole = pl.BlockSpec(memory_space=pltpu.VMEM)
    return pl.pallas_call(
        kernel,
        in_specs=[pl.BlockSpec(memory_space=pltpu.SMEM) if i in smem else whole for i in range(len(operands))],
        out_specs=[whole] * len(outputs),
        out_shape=outputs,
        compiler_params=params(),
        cost_estimate=pl.CostEstimate(flops=flops, bytes_accessed=4000000, transcendentals=0),
    )(*operands)


def pyramid_kernel(blocks, outs, perm_ref, *refs):
    x_refs = refs[:blocks]
    w_ref, w_one_ref, mask_ref, centre_ref, up_ref, down_ref, acc_ref = refs[blocks:]
    k = pl.program_id(0)
    rate = 6 * (k + 1)
    depth, pixels = x_refs[0].shape

    def product(weights, width):
        for start, size in tiles(pixels, 512):
            total = None
            for j in range(blocks):
                at = pl.multiple_of(perm_ref[j] * depth, depth)
                part = dot(weights(at, depth), x_refs[j][:, start : start + size])
                total = part if total is None else total + part
            acc_ref[:width, start : start + size] = total

    @pl.when(k == 3)
    def _():
        product(lambda at, n: w_one_ref[:, pl.ds(at, n)], outs)
        centre_ref[0] = acc_ref[:outs]

    @pl.when(k < 3)
    def _():
        product(lambda at, n: w_ref[0, :, pl.ds(at, n)], 9 * outs)
        lane = lax.broadcasted_iota(jnp.int32, (1, pixels), 1)
        col, row = lane % WS, lane // WS
        for a in (0, 1, -1):
            tap = 3 * (a + 1) * outs
            left = pltpu.roll(acc_ref[tap : tap + outs], rate, 1)
            right = pltpu.roll(acc_ref[tap + 2 * outs : tap + 3 * outs], pixels - rate, 1)
            part = acc_ref[tap + outs : tap + 2 * outs] + jnp.where(col >= rate, left, 0.0) + jnp.where(col < WS - rate, right, 0.0)
            if a == 0:
                centre_ref[0] = part
                continue
            part = part * mask_ref[pl.ds(2 * k + (a + 1) // 2, 1)]
            if a == 1:
                moved = pltpu.roll(part, pixels - WS * rate, 1)
                inside = row < pixels // WS - rate
                up_ref[0] = jnp.where(inside, 0.0, moved)[:, pixels - PAD :].astype(BF)
            else:
                moved = pltpu.roll(part, WS * rate, 1)
                inside = row >= rate
                down_ref[0] = jnp.where(inside, 0.0, moved)[:, :PAD].astype(BF)
            centre_ref[0] += jnp.where(inside, moved, 0.0)


def pyramid(x_blocks, perm, w_taps, w_one, masks):
    depth, pixels = x_blocks[0].shape
    outs, cin = w_one.shape
    whole = pl.BlockSpec(memory_space=pltpu.VMEM)
    third = lambda k, p: (jnp.minimum(k, 2), 0, 0)
    return pl.pallas_call(
        lambda *refs: pyramid_kernel(len(x_blocks), outs, *refs),
        grid_spec=pltpu.PrefetchScalarGridSpec(
            num_scalar_prefetch=1,
            grid=(4,),
            in_specs=[whole] * len(x_blocks)
            + [pl.BlockSpec((1, 9 * outs, cin), third), whole, whole],
            out_specs=[
                pl.BlockSpec((1, outs, pixels), lambda k, p: (k, 0, 0)),
                pl.BlockSpec((1, outs, PAD), third),
                pl.BlockSpec((1, outs, PAD), third),
            ],
            scratch_shapes=[pltpu.VMEM((9 * outs, pixels), F32)],
        ),
        out_shape=[
            jax.ShapeDtypeStruct((4, outs, pixels), F32),
            jax.ShapeDtypeStruct((3, outs, PAD), BF),
            jax.ShapeDtypeStruct((3, outs, PAD), BF),
        ],
        compiler_params=params(),
        cost_estimate=pl.CostEstimate(flops=2 * 28 * outs * cin * pixels, bytes_accessed=2 * (28 * outs + pixels) * cin, transcendentals=0),
    )(perm, *x_blocks, w_taps, w_one, masks)


def shifted_taps(read, lanes, rate, masks, store):
    col = lax.broadcasted_iota(jnp.int32, (1, lanes), 1) % WS
    for a in (-1, 0, 1):
        for b in (-1, 0, 1):
            shift = rate * (WS * a + b)
            first = (PAD - shift) // 128 * 128
            rest = PAD - shift - first
            window = read(first, lanes + 128)
            if rest:
                window = pltpu.roll(window, lanes + 128 - rest, 1)
            keep = ((col - b * rate >= 0) & (col - b * rate < WS)).astype(F32)
            if a:
                keep = keep * masks[(a + 1) // 2]
            store(3 * (a + 1) + b + 1, window[:, :lanes] * keep.astype(BF))


def dot_tn(a, b):
    return lax.dot_general(a, b, (((0,), (0,)), ((), ())), preferred_element_type=F32)


def input_grad_kernel(outs, dz_ref, spread_ref, mask_ref, w_ref, one_ref, pool_ref, out_ref, taps_ref):
    pixels = spread_ref.shape[1]

    @pl.when(pl.program_id(0) == 0)
    def _():
        for k in range(3):
            def store(tap, value, k=k):
                at = (9 * k + tap) * outs
                taps_ref[at : at + outs] = value

            masks = (mask_ref[2 * k : 2 * k + 1], mask_ref[2 * k + 1 : 2 * k + 2])
            rows = (k + 1) * outs
            shifted_taps(lambda first, n: dz_ref[rows : rows + outs, first : first + n], pixels, 6 * (k + 1), masks, store)
        taps_ref[27 * outs : 28 * outs] = dz_ref[:outs, PAD : PAD + pixels]
        taps_ref[28 * outs :] = spread_ref[...]

    weights = jnp.concatenate([w_ref[...], one_ref[...], pool_ref[...]], axis=0)
    for start, size in tiles(pixels, 512):
        out_ref[0, :, start : start + size] = dot_tn(weights, taps_ref[:, start : start + size]).astype(BF)


def input_grad(dz, spread, masks, w_taps, w_one, w_pool, perm):
    pixels = spread.shape[1]
    outs, cin = w_one.shape
    blocks = perm.shape[0]
    depth = cin // blocks
    whole = pl.BlockSpec(memory_space=pltpu.VMEM)
    slab = lambda rows: pl.BlockSpec((rows, depth), lambda i, p: (0, p[i]))

    def kernel(perm_ref, *refs):
        input_grad_kernel(outs, *refs)

    return pl.pallas_call(
        kernel,
        grid_spec=pltpu.PrefetchScalarGridSpec(
            num_scalar_prefetch=1,
            grid=(blocks,),
            in_specs=[whole, whole, whole, slab(27 * outs), slab(outs), slab(outs)],
            out_specs=pl.BlockSpec((1, depth, pixels), lambda i, p: (i, 0, 0)),
            scratch_shapes=[pltpu.VMEM((29 * outs, pixels), BF)],
        ),
        out_shape=jax.ShapeDtypeStruct((blocks, depth, pixels), BF),
        compiler_params=params(),
        cost_estimate=pl.CostEstimate(flops=2 * 29 * outs * cin * pixels, bytes_accessed=2 * (29 * outs + pixels) * cin, transcendentals=0),
    )(perm, dz, spread, masks, w_taps.reshape(27 * outs, cin), w_one, w_pool)


def pyramid_weight_kernel(lanes, outs, branches, plain, dz_ref, mask_ref, *refs):
    x_refs, (out_ref, taps_ref, acc_ref) = refs[:-3], refs[-3:]
    step = pl.program_id(0)
    start = pl.multiple_of(step * lanes, 128)

    @pl.when(step == 0)
    def _():
        acc_ref[...] = jnp.zeros_like(acc_ref)

    for n, k in enumerate(branches):
        def store(tap, value, n=n):
            at = (9 * n + tap) * outs
            taps_ref[at : at + outs] = value

        rows = slice((k + 1) * outs, (k + 2) * outs)
        masks = (mask_ref[0, 2 * k : 2 * k + 1], mask_ref[0, 2 * k + 1 : 2 * k + 2])
        shifted_taps(lambda first, n, rows=rows: dz_ref[rows, pl.ds(start + first, n)], lanes, 6 * (k + 1), masks, store)
    if plain:
        taps_ref[9 * len(branches) * outs :] = dz_ref[:outs, pl.ds(start + PAD, lanes)]
    acc_ref[...] += dot_nt(taps_ref[...], jnp.concatenate([x[0] for x in x_refs], axis=0))

    @pl.when(step == pl.num_programs(0) - 1)
    def _():
        out_ref[...] = acc_ref[...].astype(BF)


def pyramid_weight_grad(dz, x_blocks, places, masks, branches, plain):
    groups, slim, lanes = x_blocks[0].shape
    outs, canvas = dz.shape[0] // 4, groups * lanes
    channels = slim * len(x_blocks)
    out_rows = (9 * len(branches) + plain) * outs
    whole = pl.BlockSpec(memory_space=pltpu.VMEM)

    def kernel(places_ref, *refs):
        pyramid_weight_kernel(lanes, outs, branches, plain, *refs)

    return pl.pallas_call(
        kernel,
        grid_spec=pltpu.PrefetchScalarGridSpec(
            num_scalar_prefetch=1,
            grid=(groups,),
            in_specs=[whole, pl.BlockSpec((1, 8, lanes), lambda i, p: (i, 0, 0))]
            + [pl.BlockSpec((1, slim, lanes), lambda i, p: (p[i], 0, 0))] * len(x_blocks),
            out_specs=whole,
            scratch_shapes=[pltpu.VMEM((out_rows, lanes), BF), pltpu.VMEM((out_rows, channels), F32)],
        ),
        out_shape=jax.ShapeDtypeStruct((out_rows, channels), BF),
        compiler_params=params(),
        cost_estimate=pl.CostEstimate(flops=2 * out_rows * channels * canvas, bytes_accessed=2 * (4 * outs + channels) * canvas, transcendentals=0),
    )(places, dz, masks, *x_blocks)


def canvas_kernel(groups, devices, outs, stack_size, count, tab_top, tab_low, *refs):
    piece_refs, refs = refs[: 4 * devices], refs[4 * devices :]
    centred_ref, valid_ref, member_ref, w_ref, cols_ref, offset_ref = refs[:6]
    dz_ref, sums_ref, proj_ref, image_ref, pieces_ref, dy_ref = refs[6:]
    step = pl.program_id(0)
    four = 4 * outs
    half, share = piece_refs[0].shape[1:]
    pixels = share * devices
    group = lax.rem(step, groups)
    gain, shift, scale, mean = (cols_ref[:, i : i + 1] for i in range(4))
    lane = lax.broadcasted_iota(jnp.int32, offset_ref.shape, 1)
    offset = jnp.sum(jnp.where(lane == group, offset_ref[...], 0.0), axis=1, keepdims=True) - mean
    valid = valid_ref[0, 6:7]
    at = pl.multiple_of(group * pixels, 128)

    @pl.when(step == 0)
    def _():
        sums_ref[...] = jnp.zeros_like(sums_ref)
        proj_ref[...] = jnp.zeros_like(proj_ref)
        image_ref[...] = jnp.zeros_like(image_ref)
        dz_ref[:, :PAD] = jnp.zeros((four, PAD), BF)
        dz_ref[:, PAD + groups * pixels :] = jnp.zeros((four, PAD), BF)

    @pl.when(step < groups)
    def _():
        for i in range(devices):
            for h, table in enumerate((tab_top, tab_low)):
                own, near = piece_refs[4 * i + 2 * h], piece_refs[4 * i + 2 * h + 1]
                is_own = table[group * devices + i] < stack_size
                rows, part = slice(h * half, (h + 1) * half), slice(i * share, (i + 1) * share)
                pieces_ref[rows, part] = jnp.where(is_own, own[0], near[0])
        image_ref[...] += dot_nt(pieces_ref[...], member_ref[0].astype(BF))
        total = jnp.zeros((four, 128), F32)
        total_normed = jnp.zeros((four, 128), F32)
        for start, size in tiles(pixels, 384):
            part = slice(start, start + size)
            normed = (centred_ref[0, :, part].astype(F32) + offset) * scale
            y = gain * normed + shift
            gate = jax.nn.sigmoid(y)
            act = (y * gate * valid[:, part]).astype(BF)
            proj_ref[...] += dot_nt(pieces_ref[:, part], act)
            slope = gate * (1.0 + y * (1.0 - gate)) * valid[:, part]
            dy = dot(w_ref[...], pieces_ref[:, part]) * slope
            dy_ref[:, pl.ds(at + start, size)] = dy
            both = dy * normed
            for tile in range(0, size, 128):
                total = total + dy[:, tile : tile + 128]
                total_normed = total_normed + both[:, tile : tile + 128]
        sums_ref[:, 0:1] += jnp.sum(total, axis=1, keepdims=True)
        sums_ref[:, 1:2] += jnp.sum(total_normed, axis=1, keepdims=True)

    @pl.when(step >= groups)
    def _():
        normed = (centred_ref[0].astype(F32) + offset) * scale
        parts = (sums_ref[:, 0:1] + normed * sums_ref[:, 1:2]) * (valid * count[0])
        dz = (scale * gain) * (dy_ref[:, pl.ds(at, pixels)] - parts)
        dz_ref[:, pl.ds(PAD + at, pixels)] = dz.astype(BF)


def canvas_grad(top, low, tables, centred, valid, member, w_turned, cols, offsets, inverse_count):
    groups, four, pixels = centred.shape
    stack_size, half, share = top[0].shape
    devices = tables[0].shape[0] // groups
    wide = 2 * half

    def piece(i, table):
        def index(s, top_table, low_table):
            at = jnp.minimum(s, groups - 1) * devices + i
            return (lax.rem((top_table if table == 0 else low_table)[at], stack_size), 0, 0)

        return pl.BlockSpec((1, half, share), index)

    by_group = lambda s, a, b: (lax.rem(s, groups), 0, 0)
    whole = pl.BlockSpec(memory_space=pltpu.VMEM)

    def kernel(tab_top, tab_low, *refs):
        canvas_kernel(groups, devices, four // 4, stack_size, refs[-7], tab_top, tab_low, *refs[:-7], *refs[-6:])

    return pl.pallas_call(
        kernel,
        grid_spec=pltpu.PrefetchScalarGridSpec(
            num_scalar_prefetch=2,
            grid=(2 * groups,),
            in_specs=[piece(i, table) for i in range(devices) for table in (0, 0, 1, 1)]
            + [
                pl.BlockSpec((1, four, pixels), by_group),
                pl.BlockSpec((1, 8, pixels), by_group),
                pl.BlockSpec((1, member.shape[1], pixels), by_group),
                whole,
                whole,
                whole,
                pl.BlockSpec(memory_space=pltpu.SMEM),
            ],
            out_specs=[whole] * 4,
            scratch_shapes=[pltpu.VMEM((wide, pixels), BF), pltpu.VMEM((four, groups * pixels), F32)],
        ),
        out_shape=[
            jax.ShapeDtypeStruct((four, 2 * PAD + groups * pixels), BF),
            jax.ShapeDtypeStruct((four, 128), F32),
            jax.ShapeDtypeStruct((wide, four), F32),
            jax.ShapeDtypeStruct((wide, member.shape[1]), F32),
        ],
        compiler_params=params(),
        cost_estimate=pl.CostEstimate(flops=4 * wide * four * groups * pixels, bytes_accessed=8 * wide * groups * pixels, transcendentals=four * groups * pixels),
    )(*tables, *([*top, *low] * devices), centred, valid, member, w_turned, cols, offsets, inverse_count)


def assembly_kernel(groups, devices, order, where_ref, perm_ref, pieces, plain, out_ref, one_ref):
    line = groups // 2
    cin = out_ref.shape[1]
    depth = cin // devices
    slim = depth // groups

    def fill(refs, target):
        for r in range(0, groups, 2):
            for j in range(devices):
                part = slice(j * slim, (j + 1) * slim)
                pair = jnp.concatenate([refs[r][:, part], refs[r + 1][:, part]], axis=1)
                at = pl.multiple_of(perm_ref[j] * depth + r * slim, 128)
                target[:, pl.ds(at, 2 * slim)] = pair.astype(F32)

    for z in range(line):
        for e in range(2):
            chosen = [order.index(line_part(z, r // 2 - z, (r ^ e) & 1)) for r in range(groups)]

            @pl.when((where_ref[0] // 2 == z) & (where_ref[0] % 2 == e))
            def _(chosen=chosen):
                fill([pieces[i] for i in chosen], out_ref)
                if one_ref is not None:

                    @pl.when(pl.program_id(0) == 0)
                    def _():
                        fill([plain[i] for i in chosen], one_ref)


def assemble(branches, plain, found, devices, groups, strip, perm, into, outs, cin):
    order = sorted(found)
    pieces = [found[key] for key in order]
    slots, width = len(pieces), pieces[0].shape[1]
    rows = 3 * outs
    smem = pl.BlockSpec(memory_space=pltpu.SMEM)
    operands = [strip[None].astype(jnp.int32), perm] + pieces
    in_specs = [smem, smem] + [pl.BlockSpec((rows, width), lambda i: (i, 0))] * slots
    first = 3 * branches[0]
    out_specs = [pl.BlockSpec((rows, cin), lambda i: (first + i, 0))]
    out_shape = [jax.ShapeDtypeStruct((27 * outs, cin), F32)]
    if plain:
        operands += pieces
        in_specs += [pl.BlockSpec((outs, width), lambda i: (9 * len(branches), 0))] * slots
        out_specs.append(pl.BlockSpec((outs, cin), lambda i: (0, 0)))
        out_shape.append(jax.ShapeDtypeStruct((outs, cin), F32))
    aliases = {}
    if into is not None:
        aliases = {len(operands): 0}
        operands.append(into)
        in_specs.append(pl.BlockSpec(memory_space=pl.ANY))

    def kernel(where_ref, perm_ref, *refs):
        one_ref = refs[-1] if plain else None
        out_ref = refs[-2] if plain else refs[-1]
        assembly_kernel(groups, devices, order, where_ref, perm_ref, refs[:slots], refs[slots : 2 * slots], out_ref, one_ref)

    return pl.pallas_call(
        kernel,
        grid=(3 * len(branches),),
        in_specs=in_specs,
        out_specs=out_specs,
        out_shape=out_shape,
        input_output_aliases=aliases,
        compiler_params=params(),
        cost_estimate=pl.CostEstimate(flops=0, bytes_accessed=9 * len(branches) * outs * cin * 6, transcendentals=0),
    )(*operands)


def local(
    feats,
    lowlevel,
    heights,
    widths,
    w_one,
    w_atrous,
    w_pool,
    w_proj,
    w_low,
    w_dec1,
    w_dec2,
    w_cls,
    b_cls,
    mid_gain,
    mid_shift,
    low_gain,
    low_shift,
    dec_gain,
    dec_shift,
    cotangent,
):
    devices, groups = lax.axis_size("ch"), lax.axis_size("row")
    me, strip = lax.axis_index("ch"), lax.axis_index("row")
    place = strip * devices + me
    everyone = devices * groups
    depth, pixels = feats.shape
    rows = pixels // WS
    canvas = groups * pixels
    outs = w_one.shape[0]
    wide = outs * devices
    images = heights.shape[0]
    share = pixels // devices
    fine = 16 * share
    fine_rows = fine // WF
    margin = WS if fine_rows % 4 == 0 else 2 * WS

    area = (heights * widths).astype(F32)
    count = jnp.sum(area)
    fine_count = 16.0 * count
    scalars = jnp.stack([1.0 / count, 1.0 / fine_count])
    places = jnp.stack([strip, place]).astype(jnp.int32)
    members = -(-images // 16) * 16
    window = share + 2 * margin
    ext = fine + 2 * WF
    shaped = lambda *shape: jax.ShapeDtypeStruct(shape, F32)
    strip_rows, member_strip, valid_fine_strip = geometry_call(
        strip_geometry_kernel,
        heights, widths, places,
        [shaped(8, pixels), jax.ShapeDtypeStruct((members, pixels), BF), jax.ShapeDtypeStruct((1, 16 * pixels), BF)],
    )
    valid_strip = strip_rows[6:7]

    mine = feats * valid_strip.astype(BF)
    x_blocks, origin = gather_blocks(mine)
    perm = jnp.stack(origin).astype(jnp.int32)
    slice_depth = depth // groups
    x_slice = lax.all_to_all(mine.reshape(groups, slice_depth, pixels), "row", 0, 0)

    vectors = jnp.concatenate(
        [
            v.astype(F32).reshape(-1)
            for v in (mid_gain, mid_shift, dec_gain, dec_shift, low_gain, low_shift)
        ]
    )
    sums = dot_nt(mine, member_strip)[:, :images].reshape(-1)
    sums, x_slice = lax.optimization_barrier((jnp.concatenate([sums, vectors]), x_slice))
    told = tell_all(sums).reshape(groups, devices, -1)
    pool_sums = jnp.sum(told[:, :, : depth * images], axis=0).reshape(devices * depth, images)
    vectors = lax.dynamic_index_in_dim(told, strip, 0, False)[:, depth * images :]
    norm_rows = vectors[:, : 16 * outs].reshape(devices, 16, outs)
    gain_rows = [norm_rows[:, k].reshape(-1) for k in range(16)]
    branch_gains = jnp.stack([norm_rows[:, :4].reshape(devices, -1), norm_rows[:, 6:10].reshape(devices, -1)], axis=1)
    branch_gains = jnp.pad(branch_gains, ((0, 0), (0, 0), (0, 256 - 4 * outs)))
    proj_gain = jnp.stack([gain_rows[5], gain_rows[11]])
    first_gain = jnp.stack([gain_rows[12], gain_rows[14]])
    second_gain = jnp.stack([gain_rows[13], gain_rows[15]])
    low_share = LOWC // devices
    low_gain_all = vectors[:, 16 * outs : 16 * outs + low_share].reshape(-1)
    low_shift_all = vectors[:, 16 * outs + low_share : 16 * outs + 2 * low_share].reshape(-1)
    low_gains = jnp.pad(jnp.stack([low_gain_all, low_shift_all]), ((0, 0), (0, 256 - LOWC)))

    low_in = lowlevel * valid_fine_strip
    low_part = dot(w_low, low_in).astype(BF)
    low_pre = lax.psum_scatter(low_part, "ch", scatter_dimension=1, tiled=True).astype(F32)

    first_taps = w_dec1.transpose(1, 0, 2)
    w1 = lax.all_gather(jnp.concatenate([first_taps[:, :, LOWC:], first_taps[:, :, :LOWC]], axis=2), "ch", axis=0)
    proj_taps = w_proj.reshape(outs, 5, wide).transpose(1, 0, 2)
    pool_taps = w_pool.reshape(outs, -1, wide).transpose(1, 0, 2)
    rest = lax.all_gather(jnp.concatenate([w_dec2.transpose(1, 0, 2), proj_taps, pool_taps], axis=0), "ch", axis=0)
    w2, wp, w_pool_all = rest[:, :9], rest[:, 9:14], rest[:, 14:]
    wp_acts = wp[:, :4].reshape(devices, 4, outs, devices, outs).transpose(3, 0, 2, 1, 4).reshape(devices, wide, 4 * outs)
    wp_pool = wp[:, 4].reshape(wide, wide)

    pooled = (pool_sums / area[None]).astype(BF)
    pool_pre = jnp.einsum(
        "ckoi,kin->con", w_pool_all, pooled.reshape(-1, wide, images), preferred_element_type=F32
    ).reshape(wide, images)
    pool_mean = jnp.mean(pool_pre, axis=1)
    pool_scale = lax.rsqrt(jnp.mean(pool_pre * pool_pre, axis=1) - pool_mean * pool_mean + EPSILON)
    pool_normed = (pool_pre - pool_mean[:, None]) * pool_scale[:, None]
    gain_mid, shift_mid = mid_gain.astype(F32), mid_shift.astype(F32)
    pool_shifted = gain_rows[4][:, None] * pool_normed + gain_rows[10][:, None]
    pool_acts = jax.nn.silu(pool_shifted).astype(BF)
    broad_part = dot(wp_pool, pool_acts)
    own_rows = lambda v: lax.dynamic_slice_in_dim(v, me * outs, outs, axis=0)
    pool_act, pool_scale, pool_normed, pool_shifted = map(own_rows, (pool_acts, pool_scale, pool_normed, pool_shifted))

    w_taps = w_atrous.transpose(0, 2, 1, 3).reshape(3, 9 * outs, -1)
    centre, up, down = pyramid(x_blocks, perm, w_taps, w_one, strip_rows)
    up, down, places, low_pre = lax.optimization_barrier((up, down, places, low_pre))
    fwd = [(i, i + 1) for i in range(groups - 1)]
    bwd = [(i + 1, i) for i in range(groups - 1)]
    from_next = lax.ppermute(up, "row", bwd)
    from_prev = lax.ppermute(down, "row", fwd)

    (
        canvas_rows, member_canvas, strip_counts, counts_c, counts_f, mine_rows, window_valid, valid_wide, fine_masks, enlarge,
    ) = geometry_call(
        lambda *refs: geometry_kernel(margin, *refs),
        heights, widths, places,
        [
            shaped(groups, 8, pixels), shaped(groups, members, pixels), shaped(groups, 1), shaped(everyone, 1),
            shaped(everyone, 1), shaped(members + 8, share), shaped(1, window), shaped(1, ext), shaped(2, fine),
            jax.ShapeDtypeStruct((window, ext), BF),
        ],
    )
    member_mine, valid_mine = mine_rows[:images], mine_rows[members : members + 1]
    valid_fine = valid_wide[:, WF:-WF]
    broad_part = jnp.dot(broad_part, member_mine, precision=HIGHEST)
    low_stats = vector_tile(*local_moments(low_pre, valid_fine[0]))[:4]

    order = jnp.argsort(perm)
    x_places = jnp.arange(groups, dtype=jnp.int32)

    def columns(s, lead):
        s = s.reshape((groups,) + lead + (devices, slice_depth))
        s = jnp.take(s, order, axis=len(lead) + 1)
        s = jnp.moveaxis(s, 0, len(lead) + 1)
        return s.reshape(lead + (devices * depth,)).astype(F32)

    tile = jax.ShapeDtypeStruct((everyone, 8, 128), F32)
    centered, pieces, stats = small_call(
        branch_kernel,
        [centre, from_next, from_prev, valid_strip],
        (),
        [
            jax.ShapeDtypeStruct((4 * outs, pixels), BF),
            jax.ShapeDtypeStruct((devices, 4 * outs, share), BF),
            tile,
        ],
        0,
    )
    told_branch = swap_all(stats)
    swapped, x_slice = lax.optimization_barrier((swap_ch(pieces), x_slice))
    slice_blocks, _ = gather_blocks(x_slice)
    proj_pre, proj_left, proj_right, stats = small_call(
        project_kernel,
        [
            swapped, told_branch.reshape(groups, devices, 8, 128), strip_counts, branch_gains, wp_acts, broad_part,
            valid_mine, low_stats, scalars, jnp.concatenate([strip[None].astype(jnp.int32), perm]),
        ],
        (8, 9),
        [
            jax.ShapeDtypeStruct((wide, share), F32),
            jax.ShapeDtypeStruct((wide, margin), F32),
            jax.ShapeDtypeStruct((wide, margin), F32),
            tile,
        ],
        8 * wide * wide * share,
    )
    told_proj = swap_all(stats)
    proj_prev, proj_next = to_next(proj_right), to_previous(proj_left)
    low_prev, low_next = to_next(low_pre[:, -WF:]), to_previous(low_pre[:, :WF])
    canvas_centered = lax.all_gather(centered, "row", axis=0)

    lanes = WF * rows_per_step(fine_rows)
    edge = jax.ShapeDtypeStruct((wide, WF), F32)
    full = jax.ShapeDtypeStruct((wide, fine), F32)
    work = 18 * wide * wide * fine
    state = lambda n, channels: pltpu.VMEM((n, channels, 128), F32)
    decoder_in, first_pre, first_top, first_bottom, stats = decoder_call(
        lambda *refs: first_kernel(lanes, *refs),
        [
            proj_prev, proj_pre, proj_next, told_proj, counts_c, proj_gain, window_valid, enlarge, low_prev, low_pre, low_next,
            told_proj, counts_f, low_gains, valid_wide, fine_masks, w1, scalars,
        ],
        (), (17,),
        [jax.ShapeDtypeStruct((wide + LOWC, ext), BF), full, edge, edge, tile],
        (1,),
        [pltpu.VMEM((wide, window), BF), pltpu.VMEM((3 * wide, 3 * (wide + LOWC)), BF), state(3, wide)],
        fine, work,
    )
    stats, *slice_blocks = lax.optimization_barrier((stats, *slice_blocks))
    told_first = swap_all(stats)
    first_prev, first_next = to_next(first_bottom), to_previous(first_top)
    first_act, second_pre, second_top, second_bottom, stats = decoder_call(
        lambda *refs: second_kernel(lanes, *refs),
        [first_prev, first_pre, first_next, told_first, counts_f, first_gain, valid_wide, fine_masks, w2, scalars],
        (), (9,),
        [jax.ShapeDtypeStruct((wide, ext), BF), full, edge, edge, tile],
        (1,),
        [pltpu.VMEM((3 * wide, 3 * wide), BF), state(3, wide)],
        fine, work,
    )
    told_second = swap_all(stats)
    second_prev, second_next = to_next(second_bottom), to_previous(second_top)

    classes = w_cls.shape[0]
    cot = jnp.pad(cotangent, ((0, -classes % 32), (0, 0)))
    cot_prev, cot_next = to_next(cot[:, -WF:]), to_previous(cot[:, :WF])
    w_cls_wide = jnp.pad(w_cls, ((0, -classes % 32), (0, 0)))
    bias = jnp.pad(b_cls.astype(F32), (0, -classes % 32))[:, None]
    logits, class_part, bias_part, sums = decoder_call(
        class_kernel,
        [
            second_pre, cot, valid_fine, told_second, counts_f, second_gain, w_cls_wide, w_cls_wide.T, bias, scalars,
        ],
        (0, 1, 2), (9,),
        [
            jax.ShapeDtypeStruct((classes, fine), F32),
            jax.ShapeDtypeStruct((w_cls_wide.shape[0], wide), F32),
            jax.ShapeDtypeStruct((w_cls_wide.shape[0], 128), F32),
            tile,
        ],
        (0,),
        [state(2, wide), pltpu.VMEM((wide, 128), F32)],
        fine, work // 8,
    )
    told_sums = swap_all(sums)
    class_part = jnp.concatenate([class_part[:classes].reshape(-1), jnp.sum(bias_part[:classes], axis=1)])
    class_rows = -(-class_part.shape[0] // (128 * everyone))
    class_part = jnp.pad(class_part, (0, class_rows * 128 * everyone - class_part.shape[0])).reshape(everyone, class_rows, 128)
    class_part = jnp.pad(class_part, ((0, 0), (0, 8 - class_rows), (0, 0)))
    second_dz, first_dy, dy_top, dy_bottom, sums = decoder_call(
        lambda *refs: second_back_kernel(lanes, *refs),
        [
            second_prev, second_pre, second_next, told_second, counts_f, second_gain, told_sums, cot_prev, cot, cot_next,
            w_cls_wide.T, valid_wide, fine_masks, w2, first_pre, told_first, first_gain, class_part, scalars,
        ],
        (14,), (18,),
        [jax.ShapeDtypeStruct((wide, ext), BF), full, edge, edge, jax.ShapeDtypeStruct((everyone, 16, 128), F32)],
        (1,),
        [pltpu.VMEM((3 * wide, 3 * wide), BF), state(2, wide), pltpu.VMEM((wide, 128), F32)],
        fine, work,
    )
    second_sums = jnp.sum(told_sums, axis=0)
    told_first_sums = swap_all(sums)
    first_sums = jnp.sum(told_first_sums, axis=0)
    class_share = first_sums[8 : 8 + class_rows]
    first_sums = first_sums[:8]
    dy_prev, dy_next = to_next(dy_bottom), to_previous(dy_top)
    g_dec2 = decoder_weight_grad(second_dz, first_act, fine_masks, outs)
    told_first_sums, g_dec2, canvas_centered = lax.optimization_barrier((told_first_sums, g_dec2, canvas_centered))
    part_dec2 = lax.psum_scatter(g_dec2, "ch", scatter_dimension=0)
    first_dz, grad_window, dy_low, low_part_sums = decoder_call(
        lambda *refs: first_back_kernel(lanes, *refs),
        [
            first_prev, first_pre, first_next, dy_prev, first_dy, dy_next, told_first, counts_f, first_gain, told_first_sums,
            valid_wide, fine_masks, w1, enlarge, low_pre, told_proj, low_gains, scalars,
        ],
        (14,), (17,),
        [
            jax.ShapeDtypeStruct((wide, ext), BF),
            jax.ShapeDtypeStruct((wide, window), F32),
            jax.ShapeDtypeStruct((LOWC, fine), F32),
            jax.ShapeDtypeStruct((2, 256), F32),
        ],
        (2,),
        [pltpu.VMEM((3 * (wide + LOWC), 3 * wide), BF), state(2, LOWC), pltpu.VMEM((LOWC, 128), F32)],
        fine, work,
    )
    g_dec1 = decoder_weight_grad(first_dz, decoder_in, fine_masks, outs)

    def norm_back(dy, normed, scale, gain, totals, valid, total):
        parts = (totals[0][:, None] + normed * totals[1][:, None]) * (valid / total)
        return (scale * gain)[:, None] * (dy - parts)

    grad_coarse = grad_window[:, margin : margin + share]
    grad_coarse = grad_coarse.at[:, :margin].add(to_next(grad_window[:, margin + share :]))
    grad_coarse = grad_coarse.at[:, share - margin :].add(to_previous(grad_window[:, :margin]))
    proj_told = told_proj.reshape(everyone, 8 * 128)
    proj_mean, proj_scale = merge_moments(proj_told[:, :wide], proj_told[:, 256 : 256 + wide], counts_c[:, 0], count)
    proj_normed = (proj_pre - proj_mean[:, None]) * proj_scale[:, None]
    dy = grad_coarse * silu_slope(proj_gain[0][:, None] * proj_normed + proj_gain[1][:, None]) * valid_mine
    both = vector_tile(jnp.sum(dy, axis=1), jnp.sum(dy * proj_normed, axis=1), low_part_sums[0], low_part_sums[1])
    both = jnp.concatenate([both, jnp.pad(class_share, ((0, 8 - class_rows), (0, 0)))])
    told_both, g_dec1, part_dec2 = lax.optimization_barrier((tell_all(both), g_dec1, part_dec2))
    both = jnp.sum(told_both[:, :8], axis=0).reshape(4, 256)
    class_sums = told_both[:, 8 : 8 + class_rows].reshape(-1)
    bias_sums = class_sums[classes * wide : classes * wide + classes]
    class_sums = class_sums[: classes * wide].reshape(classes, wide)
    proj_sums, low_sums = both[:2], both[2:, :LOWC]
    proj_dz = norm_back(dy, proj_normed, proj_scale, proj_gain[0], proj_sums, valid_mine, count).astype(BF)

    part_dec1 = lax.psum_scatter(g_dec1, "ch", scatter_dimension=0)

    low_mean, low_scale = merge_moments(proj_told[:, 512 : 512 + LOWC], proj_told[:, 768 : 768 + LOWC], counts_f[:, 0], fine_count)
    low_normed = (low_pre - low_mean[:, None]) * low_scale[:, None]
    low_dz = norm_back(dy_low, low_normed, low_scale, low_gain_all, low_sums, valid_fine, fine_count).astype(BF)
    low_dz_all = lax.all_gather(low_dz, "ch", axis=1, tiled=True)

    top, low, top_table, low_table = gather_all(proj_dz[: wide // 2], proj_dz[wide // 2 :])
    wp_own = lax.dynamic_index_in_dim(wp_acts, me, 0, False)
    wp_pool_own = lax.dynamic_slice_in_dim(wp_pool, me * outs, outs, axis=1)
    own_told = lax.dynamic_index_in_dim(told_branch.reshape(groups, devices, 8 * 128), me, 1, False)
    own_mean, own_scale = merge_moments(own_told[:, : 4 * outs], own_told[:, 256 : 256 + 4 * outs], strip_counts[:, 0], count)
    cols = jnp.stack([gain_mid[:4].reshape(-1), shift_mid[:4].reshape(-1), own_scale, own_mean], axis=1)
    padded_dz, branch_sums, g_proj_acts, image_dz = canvas_grad(
        top,
        low,
        (top_table, low_table),
        canvas_centered,
        canvas_rows,
        member_canvas,
        wp_own.T,
        cols,
        own_told[:, : 4 * outs].T,
        1.0 / count[None],
    )
    branch_sums = branch_sums[:, :2].T
    image_dz = image_dz[:, :images]

    g_lowlevel = lax.dot_general(w_low, low_dz_all, (((0,), (0,)), ((), ())), preferred_element_type=F32) * valid_fine_strip.astype(F32)
    g_low = dot_nt(low_dz_all, low_in).astype(BF)
    low_columns = g_low.shape[1]
    g_low = jnp.pad(g_low, ((0, -LOWC % outs), (0, wide - low_columns))).reshape(-1, outs, wide)
    padded_dz, g_low, part_dec1, part_dec2 = lax.optimization_barrier((padded_dz, g_low, part_dec1, part_dec2))
    g_dec1, g_rest = lax.psum((part_dec1, jnp.concatenate([part_dec2, g_low])), "row")

    into, g_w_one = None, None
    if groups == 8 and 2 * slice_depth == 128:
        for branches, plain in CHUNKS:
            part = pyramid_weight_grad(padded_dz, slice_blocks, x_places, canvas_rows, branches, plain)
            part, padded_dz = lax.optimization_barrier((part, padded_dz))
            found, (g_dec1, g_rest) = gather_line(part, (g_dec1, g_rest))
            got = assemble(branches, plain, found, devices, groups, strip, perm, into, outs, devices * depth)
            into = got[0]
            if plain:
                g_w_one = got[1]
    else:
        part = pyramid_weight_grad(padded_dz, slice_blocks, x_places, canvas_rows, (0, 1, 2), True)
        found = columns(lax.all_gather(part, "row", axis=0), (28 * outs,))
        into, g_w_one = found[: 27 * outs], found[27 * outs :]
    g_w_atrous = into.reshape(3, 9, outs, devices * depth).transpose(0, 2, 1, 3)

    g_proj_pool = jnp.dot(image_dz, pool_act.astype(F32).T, precision=HIGHEST)
    g_proj_part = jnp.concatenate([g_proj_acts, g_proj_pool], axis=1).astype(BF)
    g_proj = swap_ch(g_proj_part.reshape(devices, outs, 5 * outs))
    g_proj = jnp.take(g_proj, order, axis=0)
    g_w_proj = g_proj.reshape(devices, outs, 5, outs).transpose(1, 2, 0, 3).reshape(outs, -1).astype(F32)

    grad_pool_act = lax.dot_general(wp_pool_own.astype(F32), image_dz, (((0,), (0,)), ((), ())), precision=HIGHEST)
    dy_pool = grad_pool_act * silu_slope(pool_shifted)
    pool_gain_sum = jnp.sum(dy_pool * pool_normed, axis=1)
    pool_shift_sum = jnp.sum(dy_pool, axis=1)
    pool_dz = (
        (pool_scale * gain_mid[4])[:, None]
        * (dy_pool - (pool_shift_sum[:, None] + pool_normed * pool_gain_sum[:, None]) / images)
    ).astype(BF)
    g_w_pool = dot_nt(pool_dz, pooled)
    spread = jnp.dot(pool_dz.astype(F32) / area[None], member_strip[:images].astype(F32), precision=HIGHEST).astype(BF)

    strip_pad = lax.dynamic_slice_in_dim(padded_dz, strip * pixels, pixels + 2 * PAD, axis=1)
    parts = input_grad(strip_pad, spread, strip_rows, w_taps, w_one, w_pool, perm)
    g_feats = reduce_blocks([parts[i] for i in range(devices)]) * valid_strip

    g_dec1, g_rest = g_dec1.astype(F32), g_rest.astype(F32)
    g_dec2, g_low = g_rest[:9], g_rest[9:].reshape(-1, wide)[:LOWC, :low_columns]
    g_w_dec1 = jnp.concatenate([g_dec1[:, :, wide:], g_dec1[:, :, :wide]], axis=2).transpose(1, 0, 2)
    g_w_dec2 = g_dec2.transpose(1, 0, 2)

    def my(v, n):
        return lax.dynamic_slice_in_dim(v, me * n, n, axis=-1)

    second_sums, first_sums = second_sums.reshape(4, 256), first_sums.reshape(4, 256)
    g_mid_gain = jnp.concatenate([branch_sums[1].reshape(4, outs), pool_gain_sum[None], my(proj_sums[1], outs)[None]])
    g_mid_shift = jnp.concatenate([branch_sums[0].reshape(4, outs), pool_shift_sum[None], my(proj_sums[0], outs)[None]])
    return (
        logits,
        g_feats,
        g_lowlevel,
        g_w_one,
        g_w_atrous,
        g_w_pool,
        g_w_proj,
        g_low,
        g_w_dec1,
        g_w_dec2,
        class_sums,
        bias_sums,
        g_mid_gain,
        g_mid_shift,
        my(low_sums[1], low_share),
        my(low_sums[0], low_share),
        jnp.stack([my(first_sums[1], outs), my(second_sums[1], outs)]),
        jnp.stack([my(first_sums[0], outs), my(second_sums[0], outs)]),
    )


def solution(mesh):
    placed = (
        P("ch", "row"),
        P("ch", "row"),
        P(),
        P(),
        P("ch", None),
        P(None, "ch", None, None),
        P("ch", None),
        P("ch", None),
        P(None, "ch"),
        P("ch", None, None),
        P("ch", None, None),
        P(),
        P(),
        P(None, "ch"),
        P(None, "ch"),
        P("ch"),
        P("ch"),
        P(None, "ch"),
        P(None, "ch"),
        P(None, ("row", "ch")),
    )
    return jax.shard_map(
        local,
        mesh=mesh,
        in_specs=placed,
        out_specs=(
            P(None, ("row", "ch")),
            P("ch", "row"),
            P("ch", "row"),
            P("ch", None),
            P(None, "ch", None, None),
            P("ch", None),
            P("ch", None),
            P(None, "ch"),
            P("ch", None, None),
            P("ch", None, None),
            P(),
            P(),
            P(None, "ch"),
            P(None, "ch"),
            P("ch"),
            P("ch"),
            P(None, "ch"),
            P(None, "ch"),
        ),
        check_vma=False,
    )
```

time: 2350 us -> 733 us (0.31)
  matrix products: 602 us -> 18.6 us
  local copies, waits for them, and re-layouts: 472 us -> 73.6 us
  waiting for transfers between devices: 563 us -> 170 us
  blocking collectives: 333 us -> 0 us
  other arithmetic: 308 us -> 52.2 us
  Pallas kernels: 0 us -> 229 us
  starting transfers between devices: 47.7 us -> 159 us
    dot_general x114 -> x10, matrix products: 602 us -> 16.5 us  [the longest x2 4.68 us: dot_nt(): lax.dot_general(a, b, (((1,), (1,)), ((), ())), preferred_element_type=F32)]
    psum x14 -> x0, blocking collectives: 333 us -> none  [the longest x12 251 us: pixel_sums(): return lax.psum(values, 'row')]
    pallas_call x0 -> x16, Pallas kernels: none -> 229 us  [the longest x5 88.3 us: decoder_call(): pl.pallas_call(kernel, grid=(pixels // lanes,), in_specs=in_specs, out_sp...]
    all_gather x5 -> x4, waiting for transfers between devices: 168 us -> 0.04 us  [the longest x1 0.02 us: local(): lax.all_gather(jnp.concatenate([first_taps[:, :, LOWC:], first_taps[:, :,...]
    reduce_scatter x4 -> x3, waiting for transfers between devices: 113 us -> 0.04 us  [the longest x1 0.02 us: local(): part_dec1 = lax.psum_scatter(g_dec1, 'ch', scatter_dimension=0)]
    unnamed x549 -> x230, local copies, waits for them, and re-layouts: 111 us -> 16.2 us
    another operation x10 -> x19, local copies, waits for them, and re-layouts: 97.2 us -> 2.99 us  [the longest x3 0.96 us: local(): jnp.stack([gain_mid[:4].reshape(-1), shift_mid[:4].reshape(-1), own_scale...]
    ppermute x16 -> x60, waiting for transfers between devices: 184 us -> 112 us  [the longest x6 36 us: gather_blocks(): lax.ppermute(v, 'ch', [(i, i ^ m) for i in range(count)])]
  transfers between devices with their start and end apart: 29 -> 77, of which waited for: 13 -> 18; matrix products, arithmetic and copies ran while one was open for 28% -> 18% of each run, Pallas kernels for 0% -> 27%
where the time goes in v1:
time: 733 us; the launch traced here: 722 us
  Pallas kernels  229 us (31%)
  waiting for transfers between devices  170 us (23%)
  starting transfers between devices  159 us (22%)
  local copies, waits for them, and re-layouts  73.6 us (10%)
  other arithmetic  52.2 us (7%)
  between operations  18.8 us (3%)
  matrix products  18.6 us (3%)
    pallas_call x5, Pallas kernels, decoder_call(): pl.pallas_call(kernel, grid=(pixels // lanes,), in_specs=in_specs, out_sp...  88.3 us
    all_to_all x8, starting transfers between devices, swap_all(): return lax.all_to_all(values, BOTH, 0, 0)  52.5 us
    psum x1, waiting for transfers between devices, local(): lax.psum((part_dec1, jnp.concatenate([part_dec2, g_low])), 'row')  40.1 us
    ppermute x6, waiting for transfers between devices, gather_blocks(): lax.ppermute(v, 'ch', [(i, i ^ m) for i in range(count)])  36 us
    ppermute x6, waiting for transfers between devices, along(): lax.ppermute(v, 'row', [(2 * i + e, 2 * (i + step) + e) for i in places f...  33.8 us
    pallas_call x1, Pallas kernels, canvas_grad(): pl.pallas_call(kernel, grid_spec=pltpu.PrefetchScalarGridSpec(num_scalar_...  30 us
    pallas_call x2, Pallas kernels, decoder_weight_grad(): pl.pallas_call(lambda *refs: decoder_weight_kernel(lanes, outs, *refs), g...  24.1 us
    ppermute x7, starting transfers between devices, to_next(): return lax.ppermute(x, BOTH, [(i, i + 1) for i in range(count - 1)])  21.3 us
  transfers between devices with their start and end apart: 77, of which 18 were waited for; matrix products, arithmetic and copies ran while one was open for 18% of the time, Pallas kernels for 27%

profile of v1, /device:TPU:0, one launch (start us, length us, event | category | flops | bytes accessed | tf_op | source)
XLA Modules:
  0.0 721.5 jit_solution(7178188435333114779)
XLA Ops:
  22.0 5.8 all-to-all-start
  29.2 28.5 %collective-permute-done.1.refs_3_ = bf16[512,1152]{1,0:T(8,128)(2,1)S(1)} collective-permute-done((bf16[512,1152]{1,0:T(8,128)(2,1)}, bf16[512,1152]{1,0:T(8,128)(2,1)S(1)}, u32[]{:S(2)}, u32[]{:S(2)}) %collective-permute-start.1) | collective-permute-done | bytes 1179680 | tf_op jit(solution)/shard_map/ppermute | solution.py:172
  65.2 6.1 all-to-all-start.2
  78.4 18.0 %shard_map.332 = (f32[4,64,1152]{2,1,0:T(8,128)}, bf16[3,64,640]{2,1,0:T(8,128)(2,1)}, bf16[3,64,640]{2,1,0:T(8,128)(2,1)}) custom-call(s32[4]{0:T(128)} %pad_add_fusion.refs_0_.perm_ref, bf16[512,1152]{1,0:T(8,128)(2,1)} %broadcast_multiply_fusion.refs_1_, bf16[512,1152]{1,0:T(8,128)(2,1)} %copy-done.86, bf16[512,1152]{1,0:T(8,128)(2,1)} %copy-done.85, ...), custom_call_target="tpu_custom_call" | custom-call | flops 8455716864 | bytes 12058624 | tf_op jit(solution)/shard_map/pallas_call | solution.py:851
  109.2 5.3 collective-permute-done.4.from_prev
  124.0 10.1 %shard_map.334 = (f32[8,8,1152]{2,1,0:T(8,128)}, f32[8,16,1152]{2,1,0:T(8,128)}, f32[8,1]{1,0:T(8,128)}, f32[32,1]{1,0:T(8,128)}, f32[32,1]{1,0:T(8,128)}, /*ind...) custom-call(s32[6]{0:T(128)} %refs_0_.1, ...), custom_call_target="tpu_custom_call" | custom-call | flops 20000000 | bytes 6000000 | tf_op jit(solution)/shard_map/pallas_call | solution.py:159
  141.8 5.5 all-to-all-start.1
  171.9 5.5 all-to-all-start.3
  177.4 7.4 %collective-permute-done.15.refs_4_ = bf16[8,64,1152]{2,1,0:T(8,128)(2,1)} collective-permute-done((bf16[8,64,1152]{2,1,0:T(8,128)(2,1)}, bf16[8,64,1152]{2,1,0:T(8,128)(2,1)}, u32[]{:S(2)}, u32[]{:S(2)}) %collective-permute-start.15) | collective-permute-done | bytes 1179680 | tf_op jit(solution)/shard_map/ppermute | solution.py:172
  198.1 19.0 %shard_map.336 = (bf16[304,4864]{1,0:T(8,128)(2,1)}, f32[256,4608]{1,0:T(8,128)}, f32[256,128]{1,0:T(8,128)}, f32[256,128]{1,0:T(8,128)}, f32[32,8,128]{2,1,0:T(8,128)}) custom-call(f32[256,32]{1,0:T(8,128)} %copy-done.95, f32[256,288]{1,0:T(8,128)} %get-tuple-element.157.refs_1_, f32[256,32]{1,0:T(8,128)} %copy-done.96, f32[32,8,128]{2,1,0:T(8,128)} %copy-done.31, ...), custom_call_target="tpu_custom_call" | custom-call | flops 5435817984 | bytes 18874368 | tf_op jit(solution)/shard_map/pallas_call | solution.py:730
  225.1 14.1 %all-to-all-start.4 = ((f32[32,8,128]{2,1,0:T(8,128)}), f32[32,8,128]{2,1,0:T(8,128)S(1)}, u32[]{:S(2)}, u32[]{:S(2)}) async-start(f32[32,8,128]{2,1,0:T(8,128)} %get-tuple-element.170), calls=%async_computation.5 | async-start | bytes 262144 | tf_op jit(solution)/shard_map/all_to_all | solution.py:277
  239.3 8.1 %all-to-all-done.4.refs_3_.refs_15_.refs_6_ = f32[32,8,128]{2,1,0:T(8,128)S(1)} async-done(((f32[32,8,128]{2,1,0:T(8,128)}), f32[32,8,128]{2,1,0:T(8,128)S(1)}, u32[]{:S(2)}, u32[]{:S(2)}) %all-to-all-start.4) | async-done | bytes 131104 | tf_op jit(solution)/shard_map/all_to_all | solution.py:277
  248.1 15.9 %shard_map.337 = (bf16[256,4864]{1,0:T(8,128)(2,1)}, f32[256,4608]{1,0:T(8,128)}, f32[256,128]{1,0:T(8,128)}, f32[256,128]{1,0:T(8,128)}, f32[32,8,128]{2,1,0:T(8,128)}) custom-call(f32[256,128]{1,0:T(8,128)} %copy-done.89, f32[256,4608]{1,0:T(8,128)} %get-tuple-element.166.refs_1_.refs_14_, f32[256,128]{1,0:T(8,128)} %copy-done.90, ...), custom_call_target="tpu_custom_call" | custom-call | flops 5435817984 | bytes 18874368 | tf_op jit(solution)/shard_map/pallas_call | solution.py:730
  267.4 7.4 %all-to-all-done.5.told.refs_3_ = f32[32,8,128]{2,1,0:T(8,128)S(1)} async-done(((f32[32,8,128]{2,1,0:T(8,128)}), f32[32,8,128]{2,1,0:T(8,128)S(1)}, u32[]{:S(2)}, u32[]{:S(2)}) %all-to-all-start.5) | async-done | bytes 131104 | tf_op jit(solution)/shard_map/all_to_all | solution.py:277
  275.5 8.5 %shard_map.338 = (f32[21,4608]{1,0:T(8,128)}, f32[32,256]{1,0:T(8,128)}, f32[32,128]{1,0:T(8,128)}, f32[32,8,128]{2,1,0:T(8,128)}) custom-call(f32[256,4608]{1,0:T(8,128)} %get-tuple-element.171.pre.refs_1_, bf16[32,4608]{1,0:T(8,128)(2,1)} %pad.49.cotangent.refs_8_, f32[1,4608]{1,0:T(1,128)} %get-tuple-element.306.valid, f32[32,8,128]{2,1,0:T(8,128)} %copy-done.28, ...), custom_call_target="tpu_custom_call" | custom-call | flops 679477248 | bytes 18874368 | tf_op jit(solution)/shard_map/pallas_call | solution.py:730
  295.5 19.4 %shard_map.339 = (bf16[256,4864]{1,0:T(8,128)(2,1)}, f32[256,4608]{1,0:T(8,128)}, f32[256,128]{1,0:T(8,128)}, f32[256,128]{1,0:T(8,128)}, f32[32,16,128]{2,1,0:T(8,128)}) custom-call(f32[256,128]{1,0:T(8,128)} %copy-done.97, f32[256,4608]{1,0:T(8,128)} %get-tuple-element.171.pre.refs_1_, f32[256,128]{1,0:T(8,128)} %copy-done.98, f32[32,8,128]{2,1,0:T(8,128)} %copy-done.28, ...), custom_call_target="tpu_custom_call" | custom-call | flops 5435817984 | bytes 18874368 | tf_op jit(solution)/shard_map/pallas_call | solution.py:730
  320.5 8.2 %all-to-all-start.7 = ((f32[32,16,128]{2,1,0:T(8,128)}), f32[32,16,128]{2,1,0:T(8,128)S(1)}, u32[]{:S(2)}, u32[]{:S(2)}) async-start(f32[32,16,128]{2,1,0:T(8,128)} %get-tuple-element.182), calls=%async_computation.8 | async-start | bytes 524288 | tf_op jit(solution)/shard_map/all_to_all | solution.py:277
  329.0 10.8 %shard_map.340 = bf16[4,9,64,256]{3,2,1,0:T(8,128)(2,1)} custom-call(bf16[256,4864]{1,0:T(8,128)(2,1)} %get-tuple-element.183.refs_0_, bf16[256,4864]{1,0:T(8,128)(2,1)} %get-tuple-element.184.refs_1_, f32[2,4608]{1,0:T(2,128)} %get-tuple-element.164.refs_15_.refs_7_.refs_12_.refs_2_.refs_11_), custom_call_target="tpu_custom_call" | custom-call | flops 5435817984 | bytes 4718592 | tf_op jit(solution)/shard_map/pallas_call | solution.py:709
  341.2 25.4 %shard_map.341 = (bf16[256,4864]{1,0:T(8,128)(2,1)}, f32[256,352]{1,0:T(8,128)}, f32[48,4608]{1,0:T(8,128)}, f32[2,256]{1,0:T(2,128)}) custom-call(f32[256,128]{1,0:T(8,128)} %copy-done.89, f32[256,4608]{1,0:T(8,128)} %get-tuple-element.166.refs_1_.refs_14_, f32[256,128]{1,0:T(8,128)} %copy-done.90, f32[256,128]{1,0:T(8,128)} %copy-done.93, ...), custom_call_target="tpu_custom_call" | custom-call | flops 5435817984 | bytes 18874368 | tf_op jit(solution)/shard_map/pallas_call | solution.py:730
  377.1 8.0 %all-to-all-start.8 = ((f32[32,16,128]{2,1,0:T(8,128)}), f32[32,16,128]{2,1,0:T(8,128)S(1)}, u32[]{:S(2)}, u32[]{:S(2)}) async-start(f32[32,16,128]{2,1,0:T(8,128)} %broadcast_in_dim.31), calls=%async_computation.9 | async-start | bytes 524288 | tf_op jit(solution)/shard_map/all_to_all | solution.py:277
  385.1 13.3 %shard_map.342 = bf16[4,9,64,304]{3,2,1,0:T(8,128)(2,1)} custom-call(bf16[256,4864]{1,0:T(8,128)(2,1)} %get-tuple-element.189.refs_0_, bf16[304,4864]{1,0:T(8,128)(2,1)} %get-tuple-element.190.refs_1_, f32[2,4608]{1,0:T(2,128)} %get-tuple-element.164.refs_15_.refs_7_.refs_12_.refs_2_.refs_11_), custom_call_target="tpu_custom_call" | custom-call | flops 6455033856 | bytes 5160960 | tf_op jit(solution)/shard_map/pallas_call | solution.py:709
  411.2 5.0 collective-permute-done.26
  430.7 8.9 %collective-permute-done.35 = bf16[4,128,288]{2,1,0:T(8,128)(2,1)} collective-permute-done((bf16[4,128,288]{2,1,0:T(8,128)(2,1)S(1)}, bf16[4,128,288]{2,1,0:T(8,128)(2,1)}, u32[]{:S(2)}, u32[]{:S(2)}) %collective-permute-start.35) | collective-permute-done | bytes 294944 | tf_op jit(solution)/shard_map/ppermute | solution.py:228
  466.5 30.0 %shard_map.343 = (bf16[256,10496]{1,0:T(8,128)(2,1)}, f32[256,128]{1,0:T(8,128)}, f32[256,256]{1,0:T(8,128)}, f32[256,16]{1,0:T(8,128)}) custom-call(s32[32]{0:T(128)} %get-tuple-element.325.tab_top, s32[32]{0:T(128)} %get-tuple-element.324.tab_low, bf16[16,128,288]{2,1,0:T(8,128)(2,1)} %copy-done.2, ...), custom_call_target="tpu_custom_call" | custom-call | flops 2415919104 | bytes 18874368 | tf_op jit(solution)/shard_map/pallas_call | solution.py:1072
  501.8 17.5 %shard_map.344.refs_7_.refs_24_ = bf16[1792,256]{1,0:T(8,128)(2,1)} custom-call(s32[8]{0:T(128)} %iota.18.places_ref, bf16[256,10496]{1,0:T(8,128)(2,1)} %get-tuple-element.205.refs_0_, f32[8,8,1152]{2,1,0:T(8,128)} %get-tuple-element.194.refs_17_.refs_1_, bf16[8,64,1152]{2,1,0:T(8,128)(2,1)} %all-to-all-done.refs_2_, ...), custom_call_target="tpu_custom_call" | custom-call | flops 8455716864 | bytes 9437184 | tf_op jit(solution)/shard_map/pallas_call | solution.py:978
  519.3 8.9 %collective-permute-start.41 = (bf16[1792,256]{1,0:T(8,128)(2,1)}, bf16[1792,256]{1,0:T(8,128)(2,1)S(1)}, u32[]{:S(2)}, u32[]{:S(2)}) collective-permute-start(bf16[1792,256]{1,0:T(8,128)(2,1)} %shard_map.344.refs_7_.refs_24_), channel_id=1, source_target_pairs={{0,8},{4,12},{8,16},{12,20},{16,24},{20,28},{1,9},{5,13},{9,17},{1... | collective-permute-start | bytes 2752520 | tf_op jit(solution)/shard_map/ppermute | solution.py:245
  532.3 16.4 %shard_map.345 = bf16[4,512,1152]{2,1,0:T(8,128)(2,1)} custom-call(s32[4]{0:T(128)} %pad_add_fusion.refs_0_.perm_ref, bf16[256,2432]{1,0:T(8,128)(2,1)} %constant_dynamic-slice_fusion.5.refs_0_, bf16[64,1152]{1,0:T(8,128)(2,1)} %convolution_convert_fusion.1.refs_1_, f32[8,1152]{1,0:T(8,128)} %get-tuple-element.138.refs_7_.refs_2_, ...), custom_call_target="tpu_custom_call" | custom-call | flops 8757706752 | bytes 12320768 | tf_op jit(solution)/shard_map/pallas_call | solution.py:927
  570.7 18.3 %collective-permute-done.45.refs_12_.refs_29_ = bf16[1792,256]{1,0:T(8,128)(2,1)} collective-permute-done((bf16[1792,256]{1,0:T(8,128)(2,1)}, bf16[1792,256]{1,0:T(8,128)(2,1)}, u32[]{:S(2)}, u32[]{:S(2)}) %collective-permute-start.45) | collective-permute-done | bytes 917536 | tf_op jit(solution)/shard_map/ppermute | solution.py:245
  616.6 15.5 %collective-permute-done.49.refs_15_.refs_32_ = bf16[1792,256]{1,0:T(8,128)(2,1)} collective-permute-done((bf16[1792,256]{1,0:T(8,128)(2,1)}, bf16[1792,256]{1,0:T(8,128)(2,1)}, u32[]{:S(2)}, u32[]{:S(2)}) %collective-permute-start.49) | collective-permute-done | bytes 917536 | tf_op jit(solution)/shard_map/ppermute | solution.py:245
  632.0 40.1 %all-reduce.13.cloned.1.call-done = (bf16[9,64,304]{2,1,0:T(8,128)(2,1)}, bf16[10,64,256]{2,1,0:T(8,128)(2,1)}) async-done(((bf16[9,64,304]{2,1,0:T(8,128)(2,1)}, bf16[10,64,256]{2,1,0:T(8,128)(2,1)}), (bf16[9,64,304]{2,1,0:T(8,128)(2,1)}, bf16[10,64,256]{2,1,0:T(8,128)(2,1)})) %all-reduce.13.cloned.1.call-update) | async-done | bytes 677904 | tf_op jit(solution)/shard_map/psum | solution.py:1497
  685.3 12.2 %collective-permute-done.56.refs_16_.refs_33_ = bf16[1792,256]{1,0:T(8,128)(2,1)S(1)} collective-permute-done((bf16[1792,256]{1,0:T(8,128)(2,1)}, bf16[1792,256]{1,0:T(8,128)(2,1)S(1)}, u32[]{:S(2)}, u32[]{:S(2)}) %collective-permute-start.56) | collective-permute-done | bytes 917536 | tf_op jit(solution)/shard_map/ppermute | solution.py:248
  698.5 15.7 %shard_map.346 = (f32[1728,2048]{1,0:T(8,128)}, f32[64,2048]{1,0:T(8,128)}) custom-call(s32[1]{0:T(128)} %bitcast.4.where_ref, s32[4]{0:T(128)} %pad_add_fusion.refs_0_.perm_ref, bf16[1792,256]{1,0:T(8,128)(2,1)} %copy-done.10, bf16[1792,256]{1,0:T(8,128)(2,1)} %copy-done.11, bf16[1792,256]{1,0:T(8,128)(2,1)} %collective-permute-done.44.refs_2_.refs_19_, ...), custom_call_target="tpu_custom_call" | custom-call | bytes 21233664 | tf_op jit(solution)/shard_map/pallas_call | solution.py:1156
  (582 shorter events, 263.8 us)
Async XLA Ops:
  7.2 90.9 %reduce-scatter.4.cloned.1.call-start = ((), (), s32[]{:S(2)}) async-start(), calls=%async_computation.12 | async-start | bytes 2211840 | tf_op jit(solution)/shard_map/reduce_scatter | solution.py:1252
  14.9 143.2 %all-gather.10.cloned.1.call-start = ((), (), s32[]{:S(2)}) async-start(), calls=%async_computation.16 | async-start | bytes 3604480 | tf_op jit(solution)/shard_map/all_gather | solution.py:1258
  19.1 38.6 %collective-permute-start.1 = (bf16[512,1152]{1,0:T(8,128)(2,1)}, bf16[512,1152]{1,0:T(8,128)(2,1)S(1)}, u32[]{:S(2)}, u32[]{:S(2)}) collective-permute-start(bf16[512,1152]{1,0:T(8,128)(2,1)} %broadcast_multiply_fusion.refs_1_), channel_id=1, source_target_pairs={{0,2},{1,3},{2,0},{3,1},{4,6},{5,7},{6,4},{7,5},{8,10},{9,11},{10,... | collective-permute-start | bytes 3538952 | tf_op jit(solution)/shard_map/ppermute | solution.py:172
  22.0 42.1 %all-to-all-start = ((bf16[8,64,1152]{2,1,0:T(8,128)(2,1)}), bf16[8,64,1152]{2,1,0:T(8,128)(2,1)}, u32[]{:S(2)}, u32[]{:S(2)}) async-start(bf16[8,64,1152]{2,1,0:T(8,128)(2,1)} %bitcast.15), calls=%async_computation.1 | async-start | bytes 2359296 | tf_op jit(solution)/shard_map/all_to_all | solution.py:1225
  27.9 169.5 %all-gather.12.cloned.1.call-start = ((), (), s32[]{:S(2)}) async-start(), calls=%async_computation.17 | async-start | bytes 2211840 | tf_op jit(solution)/shard_map/all_gather | solution.py:1255
  27.9 49.4 %collective-permute-start = (bf16[512,1152]{1,0:T(8,128)(2,1)}, bf16[512,1152]{1,0:T(8,128)(2,1)S(1)}, u32[]{:S(2)}, u32[]{:S(2)}) collective-permute-start(bf16[512,1152]{1,0:T(8,128)(2,1)} %broadcast_multiply_fusion.refs_1_), channel_id=1, source_target_pairs={{0,1},{1,0},{2,3},{3,2},{4,5},{5,4},{6,7},{7,6},{8,9},{9,8},{10,11... | collective-permute-start | bytes 3538952 | tf_op jit(solution)/shard_map/ppermute | solution.py:172
  65.2 31.2 %all-to-all-start.2 = ((f32[32,1,4120]{2,1,0:T(1,128)}), f32[32,1,4120]{2,1,0:T(1,128)S(1)}, u32[]{:S(2)}, u32[]{:S(2)}) async-start(f32[32,1,4120]{2,1,0:T(1,128)} %broadcast_in_dim.25), calls=%async_computation.3 | async-start | bytes 1081344 | tf_op jit(solution)/shard_map/all_to_all | solution.py:277
  71.3 268.6 %all-gather.14.cloned.1.call-start = ((), (), s32[]{:S(2)}) async-start(), calls=%async_computation.18 | async-start | bytes 5308416 | tf_op jit(solution)/shard_map/all_gather | solution.py:1343
  147.4 40.6 %collective-permute-start.10 = (f32[48,128]{1,0:T(8,128)S(1)}, f32[48,128]{1,0:T(8,128)S(1)}, u32[]{:S(2)}, u32[]{:S(2)}) collective-permute-start(f32[48,128]{1,0:T(8,128)S(1)} %get-tuple-element.270), channel_id=1, source_target_pairs={{0,1},{1,2},{2,3},{3,4},{4,5},{5,6},{6,7},{7,8},{8,9},{9,10},{10,1... | collective-permute-start | bytes 73736 | tf_op jit(solution)/shard_map/ppermute | solution.py:297
  149.6 42.4 %collective-permute-start.11 = (f32[48,128]{1,0:T(8,128)S(1)}, f32[48,128]{1,0:T(8,128)S(1)}, u32[]{:S(2)}, u32[]{:S(2)}) collective-permute-start(f32[48,128]{1,0:T(8,128)S(1)} %get-tuple-element.269), channel_id=1, source_target_pairs={{1,0},{2,1},{3,2},{4,3},{5,4},{6,5},{7,6},{8,7},{9,8},{10,9},{11,1... | collective-permute-start | bytes 73736 | tf_op jit(solution)/shard_map/ppermute | solution.py:302
  153.1 70.7 %collective-permute-start.14 = (bf16[8,64,1152]{2,1,0:T(8,128)(2,1)}, bf16[8,64,1152]{2,1,0:T(8,128)(2,1)}, u32[]{:S(2)}, u32[]{:S(2)}) collective-permute-start(bf16[8,64,1152]{2,1,0:T(8,128)(2,1)} %all-to-all-done.refs_2_), channel_id=1, source_target_pairs={{0,1},{1,0},{2,3},{3,2},{4,5},{5,4},{6,7},{7,6},{8,9},{9,8},{10,11... | collective-permute-start | bytes 3538952 | tf_op jit(solution)/shard_map/ppermute | solution.py:172
  155.4 29.4 %collective-permute-start.15 = (bf16[8,64,1152]{2,1,0:T(8,128)(2,1)}, bf16[8,64,1152]{2,1,0:T(8,128)(2,1)}, u32[]{:S(2)}, u32[]{:S(2)}) collective-permute-start(bf16[8,64,1152]{2,1,0:T(8,128)(2,1)} %all-to-all-done.refs_2_), channel_id=1, source_target_pairs={{0,2},{1,3},{2,0},{3,1},{4,6},{5,7},{6,4},{7,5},{8,10},{9,11},{10,... | collective-permute-start | bytes 3538952 | tf_op jit(solution)/shard_map/ppermute | solution.py:172
  184.8 40.2 %collective-permute-start.16 = (bf16[8,64,1152]{2,1,0:T(8,128)(2,1)}, bf16[8,64,1152]{2,1,0:T(8,128)(2,1)S(1)}, u32[]{:S(2)}, u32[]{:S(2)}) collective-permute-start(bf16[8,64,1152]{2,1,0:T(8,128)(2,1)} %collective-permute-done.15.refs_4_), channel_id=1, source_target_pairs={{0,1},{1,0},{2,3},{3,2},{4,5},{5,4},{6,7},{7,6},{8,9},{9,8},{10,11... | collective-permute-start | bytes 3538952 | tf_op jit(solution)/shard_map/ppermute | solution.py:172
  191.9 100.2 %collective-permute-start.19 = (bf16[32,128]{1,0:T(8,128)(2,1)S(1)}, bf16[32,128]{1,0:T(8,128)(2,1)S(1)}, u32[]{:S(2)}, u32[]{:S(2)}) collective-permute-start(bf16[32,128]{1,0:T(8,128)(2,1)S(1)} %get-tuple-element.280), channel_id=1, source_target_pairs={{0,1},{1,2},{2,3},{3,4},{4,5},{5,6},{6,7},{7,8},{8,9},{9,10},{10,1... | collective-permute-start | bytes 24584 | tf_op jit(solution)/shard_map/ppermute | solution.py:297
  196.0 96.2 %collective-permute-start.20 = (bf16[32,128]{1,0:T(8,128)(2,1)S(1)}, bf16[32,128]{1,0:T(8,128)(2,1)S(1)}, u32[]{:S(2)}, u32[]{:S(2)}) collective-permute-start(bf16[32,128]{1,0:T(8,128)(2,1)S(1)} %get-tuple-element.279), channel_id=1, source_target_pairs={{1,0},{2,1},{3,2},{4,3},{5,4},{6,5},{7,6},{8,7},{9,8},{10,9},{11,1... | collective-permute-start | bytes 24584 | tf_op jit(solution)/shard_map/ppermute | solution.py:302
  314.9 25.6 %collective-permute-start.21 = (f32[256,128]{1,0:T(8,128)}, f32[256,128]{1,0:T(8,128)S(1)}, u32[]{:S(2)}, u32[]{:S(2)}) collective-permute-start(f32[256,128]{1,0:T(8,128)} %get-tuple-element.179), channel_id=1, source_target_pairs={{0,1},{1,2},{2,3},{3,4},{4,5},{5,6},{6,7},{7,8},{8,9},{9,10},{10,1... | collective-permute-start | bytes 393224 | tf_op jit(solution)/shard_map/ppermute | solution.py:297
  328.7 69.6 %reduce-scatter.6.cloned.1.call-start = ((), (), s32[]{:S(2)}) async-start(), calls=%async_computation.13 | async-start | bytes 1474560 | tf_op jit(solution)/shard_map/reduce_scatter | solution.py:1423
  385.0 113.9 %all-gather.8.cloned.1.call-start = ((), (), s32[]{:S(2)}) async-start(), calls=%async_computation.14 | async-start | bytes 2211840 | tf_op jit(solution)/shard_map/all_gather | solution.py:1469
  400.1 101.2 %reduce-scatter.8.cloned.1.call-start = ((), (), s32[]{:S(2)}) async-start(), calls=%async_computation.15 | async-start | bytes 2211840 | tf_op jit(solution)/shard_map/reduce_scatter | solution.py:1464
  408.1 264.0 %all-reduce.13.cloned.1.call-start = ((), (), s32[]{:S(2)}) async-start(), calls=%async_computation.19 | async-start | bytes 1540096 | tf_op jit(solution)/shard_map/psum | solution.py:1497
  519.3 36.7 %collective-permute-start.41 = (bf16[1792,256]{1,0:T(8,128)(2,1)}, bf16[1792,256]{1,0:T(8,128)(2,1)S(1)}, u32[]{:S(2)}, u32[]{:S(2)}) collective-permute-start(bf16[1792,256]{1,0:T(8,128)(2,1)} %shard_map.344.refs_7_.refs_24_), channel_id=1, source_target_pairs={{0,8},{4,12},{8,16},{12,20},{16,24},{20,28},{1,9},{5,13},{9,17},{1... | collective-permute-start | bytes 2752520 | tf_op jit(solution)/shard_map/ppermute | solution.py:245
  528.2 27.8 %collective-permute-start.42 = (bf16[1792,256]{1,0:T(8,128)(2,1)}, bf16[1792,256]{1,0:T(8,128)(2,1)}, u32[]{:S(2)}, u32[]{:S(2)}) collective-permute-start(bf16[1792,256]{1,0:T(8,128)(2,1)} %shard_map.344.refs_7_.refs_24_), channel_id=1, source_target_pairs={{8,0},{12,4},{16,8},{20,12},{24,16},{28,20},{9,1},{13,5},{17,9},{2... | collective-permute-start | bytes 2752520 | tf_op jit(solution)/shard_map/ppermute | solution.py:245
  529.8 26.3 %collective-permute-start.43 = (bf16[1792,256]{1,0:T(8,128)(2,1)}, bf16[1792,256]{1,0:T(8,128)(2,1)S(1)}, u32[]{:S(2)}, u32[]{:S(2)}) collective-permute-start(bf16[1792,256]{1,0:T(8,128)(2,1)} %shard_map.344.refs_7_.refs_24_), channel_id=1, source_target_pairs={{0,4},{4,0},{8,12},{12,8},{16,20},{20,16},{24,28},{28,24},{1,5},{5... | collective-permute-start | bytes 2752520 | tf_op jit(solution)/shard_map/ppermute | solution.py:248
  552.2 48.7 %collective-permute-start.39 = (bf16[2,512,1152]{2,1,0:T(8,128)(2,1)}, bf16[2,512,1152]{2,1,0:T(8,128)(2,1)}, u32[]{:S(2)}, u32[]{:S(2)}) collective-permute-start(bf16[2,512,1152]{2,1,0:T(8,128)(2,1)} %pad_maximum_fusion), channel_id=1, source_target_pairs={{0,1},{1,0},{2,3},{3,2},{4,5},{5,4},{6,7},{7,6},{8,9},{9,8},{10,11... | collective-permute-start | bytes 7077896 | tf_op jit(solution)/shard_map/ppermute | solution.py:206
  558.6 32.8 %collective-permute-start.46 = (bf16[1792,256]{1,0:T(8,128)(2,1)S(1)}, bf16[1792,256]{1,0:T(8,128)(2,1)S(1)}, u32[]{:S(2)}, u32[]{:S(2)}) collective-permute-start(bf16[1792,256]{1,0:T(8,128)(2,1)S(1)} %collective-permute-done.41.refs_5_.refs_22_), channel_id=1, source_target_pairs={{8,12},{12,8},{16,20},{20,16},{24,28},{28,24},{9,13},{13,9},{17,21... | collective-permute-start | bytes 2752520 | tf_op jit(solution)/shard_map/ppermute | solution.py:248
  559.3 29.7 %collective-permute-start.45 = (bf16[1792,256]{1,0:T(8,128)(2,1)}, bf16[1792,256]{1,0:T(8,128)(2,1)}, u32[]{:S(2)}, u32[]{:S(2)}) collective-permute-start(bf16[1792,256]{1,0:T(8,128)(2,1)} %collective-permute-done.42.refs_9_.refs_26_), channel_id=1, source_target_pairs={{8,0},{12,4},{16,8},{20,12},{9,1},{13,5},{17,9},{21,13},{10,2},{14... | collective-permute-start | bytes 2752520 | tf_op jit(solution)/shard_map/ppermute | solution.py:245
  560.6 30.8 %collective-permute-start.47 = (bf16[1792,256]{1,0:T(8,128)(2,1)}, bf16[1792,256]{1,0:T(8,128)(2,1)}, u32[]{:S(2)}, u32[]{:S(2)}) collective-permute-start(bf16[1792,256]{1,0:T(8,128)(2,1)} %collective-permute-done.42.refs_9_.refs_26_), channel_id=1, source_target_pairs={{0,4},{4,0},{1,5},{5,1},{2,6},{6,2},{3,7},{7,3}} | collective-permute-start | bytes 2752520 | tf_op jit(solution)/shard_map/ppermute | solution.py:248
  595.8 36.2 %collective-permute-start.51 = (bf16[1792,256]{1,0:T(8,128)(2,1)}, bf16[1792,256]{1,0:T(8,128)(2,1)}, u32[]{:S(2)}, u32[]{:S(2)}) collective-permute-start(bf16[1792,256]{1,0:T(8,128)(2,1)} %collective-permute-done.44.refs_2_.refs_19_), channel_id=1, source_target_pairs={{24,28},{28,24},{25,29},{29,25},{26,30},{30,26},{27,31},{31,27}} | collective-permute-start | bytes 2752520 | tf_op jit(solution)/shard_map/ppermute | solution.py:248
  597.4 34.6 %collective-permute-start.49 = (bf16[1792,256]{1,0:T(8,128)(2,1)}, bf16[1792,256]{1,0:T(8,128)(2,1)}, u32[]{:S(2)}, u32[]{:S(2)}) collective-permute-start(bf16[1792,256]{1,0:T(8,128)(2,1)} %collective-permute-done.45.refs_12_.refs_29_), channel_id=1, source_target_pairs={{8,0},{12,4},{9,1},{13,5},{10,2},{14,6},{11,3},{15,7}} | collective-permute-start | bytes 2752520 | tf_op jit(solution)/shard_map/ppermute | solution.py:245
  598.7 33.3 %collective-permute-start.52 = (bf16[1792,256]{1,0:T(8,128)(2,1)}, bf16[1792,256]{1,0:T(8,128)(2,1)}, u32[]{:S(2)}, u32[]{:S(2)}) collective-permute-start(bf16[1792,256]{1,0:T(8,128)(2,1)} %collective-permute-done.45.refs_12_.refs_29_), channel_id=1, source_target_pairs={{0,4},{4,0},{1,5},{5,1},{2,6},{6,2},{3,7},{7,3}} | collective-permute-start | bytes 2752520 | tf_op jit(solution)/shard_map/ppermute | solution.py:248
  600.9 31.1 %collective-permute-start.50 = (bf16[1792,256]{1,0:T(8,128)(2,1)}, bf16[1792,256]{1,0:T(8,128)(2,1)}, u32[]{:S(2)}, u32[]{:S(2)}) collective-permute-start(bf16[1792,256]{1,0:T(8,128)(2,1)} %collective-permute-done.42.refs_9_.refs_26_), channel_id=1, source_target_pairs={{8,12},{12,8},{16,20},{20,16},{9,13},{13,9},{17,21},{21,17},{10,14... | collective-permute-start | bytes 2752520 | tf_op jit(solution)/shard_map/ppermute | solution.py:248
  608.1 73.1 %collective-permute-start.40 = (bf16[512,1152]{1,0:T(8,128)(2,1)}, bf16[512,1152]{1,0:T(8,128)(2,1)}, u32[]{:S(2)}, u32[]{:S(2)}) collective-permute-start(bf16[512,1152]{1,0:T(8,128)(2,1)} %fusion.9), channel_id=1, source_target_pairs={{0,2},{1,3},{2,0},{3,1},{4,6},{5,7},{6,4},{7,5},{8,10},{9,11},{10,... | collective-permute-start | bytes 3538952 | tf_op jit(solution)/shard_map/ppermute | solution.py:206
  (151 other events, 2052.5 us)
Sparse Core Ops, SparseCore 0:
  15.0 41.6 reduce-scatter.3
  58.4 32.8 all-gather.9
  93.5 20.7 all-gather.11
  118.6 81.5 all-gather.13
  340.0 26.9 reduce-scatter.5
  400.2 23.2 all-gather.7
  426.7 30.3 reduce-scatter.7
  595.9 76.1 all-reduce.12

commit v2 on v1

--- a/solution.py
+++ b/solution.py
@@ -1,3 +1,5 @@
+import math
+
 import jax
 import jax.numpy as jnp
 from jax import lax
@@ -15,8 +17,8 @@
 BF = jnp.bfloat16
 F32 = jnp.float32
 BOTH = ("row", "ch")
+BRIEF = pl.CostEstimate(flops=1, bytes_accessed=1, transcendentals=0)
 VMEM_LIMIT = 56 * 1024 * 1024
-CHUNKS = (((0, 1, 2), True),)
 
 
 def params():
@@ -166,27 +168,17 @@
     )(heights, widths, places)
 
 
-def gather_blocks(x):
+def gather_blocks(x, meanwhile=()):
     count, me = lax.axis_size("ch"), lax.axis_index("ch")
     if count == 4:
         cross = lambda v, m: lax.ppermute(v, "ch", [(i, i ^ m) for i in range(count)])
         far = cross(x, 2)
         near = cross(x, 1)
-        return [x, near, far, cross(far, 1)], [me, me ^ 1, me ^ 2, me ^ 3]
+        if meanwhile:
+            far, *meanwhile = lax.optimization_barrier((far, *meanwhile))
+        return [x, near, far, cross(far, 1)], [me, me ^ 1, me ^ 2, me ^ 3], meanwhile
     every = lax.all_gather(x, "ch", axis=0)
-    return [every[i] for i in range(count)], [jnp.int32(i) for i in range(count)]
-
-
-def swap_row(x):
-    groups, strip = lax.axis_size("row"), lax.axis_index("row")
-    number = jnp.arange(groups, dtype=jnp.int32)
-    if groups != 8:
-        return lax.all_to_all(x, "row", 0, 0), number
-    pick = lambda i: lax.dynamic_index_in_dim(x, i, 0, False)
-    blocks = [pick(strip)]
-    for m in range(1, groups):
-        blocks.append(lax.ppermute(pick(strip ^ m), "row", [(i, i ^ m) for i in range(groups)]))
-    return jnp.stack(blocks), number ^ strip
+    return [every[i] for i in range(count)], [jnp.int32(i) for i in range(count)], meanwhile
 
 
 def swap_ch(x):
@@ -210,37 +202,7 @@
     return lax.psum_scatter(jnp.stack(blocks), "ch", scatter_dimension=0).astype(F32)
 
 
-def gather_all(top, low):
-    groups, count = lax.axis_size("row"), lax.axis_size("ch")
-    strip, me = lax.axis_index("row"), lax.axis_index("ch")
-    whole = jnp.arange(groups * count, dtype=jnp.int32)
-    if groups != 8 or count != 4:
-        every = lax.all_gather(jnp.stack([top, low]), BOTH, axis=0)
-        top, low = every[:, 0], every[:, 1]
-        return (top, top), (low, low), whole, whole
-    line = groups // 2
-
-    def around(v, step):
-        pairs = [(2 * i + e, 2 * ((i + step) % line) + e) for i in range(line) for e in range(2)]
-        return lax.ppermute(v, "row", pairs)
-
-    beside = lambda v: lax.ppermute(v, "row", [(i, i ^ 1) for i in range(groups)])
-    across = lambda v: lax.ppermute(v, "ch", [(i, i ^ 2) for i in range(count)])
-    core = lambda v: lax.ppermute(v, "ch", [(i, i ^ 1) for i in range(count)])
-    top = jnp.stack([top, around(top, 1), around(top, 2), around(top, 3)])
-    low = jnp.stack([low, around(low, 1), around(low, 2), around(low, 3)])
-    top_beside, low_across = beside(top), across(low)
-    top = jnp.concatenate([top, top_beside, across(top), across(top_beside)])
-    low = jnp.concatenate([low, low_across, beside(low), beside(low_across)])
-    other_strip, other_me = whole // count, whole % count
-    z = jnp.mod(strip // 2 - other_strip // 2, line)
-    e = (strip ^ other_strip) & 1
-    y = ((me ^ other_me) >> 1) & 1
-    c = (me ^ other_me) & 1
-    return (top, core(top)), (low, core(low)), ((c * 2 + y) * 2 + e) * line + z, ((c * 2 + e) * 2 + y) * line + z
-
-
-def gather_line(x, rider):
+def gather_line(x):
     def along(v, places, step):
         return lax.ppermute(v, "row", [(2 * i + e, 2 * (i + step) + e) for i in places for e in range(2)])
 
@@ -248,8 +210,7 @@
         return lax.ppermute(v, "row", [(2 * i + e, 2 * i + 1 - e) for i in places for e in range(2)])
 
     def together(*keys):
-        for key, value in zip(keys, lax.optimization_barrier(tuple(got[key] for key in keys))):
-            got[key] = value
+        got.update(zip(keys, lax.optimization_barrier(tuple(got[key] for key in keys))))
 
     got = {(0, 0, 0): x}
     got[-1, 0, 0], got[1, 0, 0] = along(x, (0, 1, 2), 1), along(x, (1, 2, 3), -1)
@@ -262,10 +223,9 @@
     got[1, 1, 1] = beside(got[1, 0, 0], (1, 2))
     got[-2, 1, 0], got[2, 1, 0] = beside(got[-2, 0, 0], (3,)), beside(got[2, 0, 0], (0,))
     together((-3, 0, 0), (3, 0, 0), (1, 1, 1), (-2, 1, 0), (2, 1, 0), (-2, 0, 0), (2, 0, 0))
-    got[-3, 0, 0], *rider = lax.optimization_barrier((got[-3, 0, 0], *rider))
     got[-2, 1, 1], got[2, 1, 1] = beside(got[-2, 0, 0], (2,)), beside(got[2, 0, 0], (1,))
     got[-3, 1, 0], got[3, 1, 0] = beside(got[-3, 0, 0], (3,)), beside(got[3, 0, 0], (0,))
-    return got, rider
+    return got
 
 
 def line_part(place, steps, side):
@@ -285,6 +245,11 @@
 def tell_row(values):
     count = lax.axis_size("row")
     return lax.all_to_all(jnp.broadcast_to(values[None], (count,) + values.shape), "row", 0, 0)
+
+
+def tell_group(values):
+    count = lax.axis_size("ch")
+    return lax.all_to_all(jnp.broadcast_to(values[None], (count,) + values.shape), "ch", 0, 0)
 
 
 def vector_tile(*vectors):
@@ -714,7 +679,7 @@
         out_shape=jax.ShapeDtypeStruct((devices, 9, outs, cin), BF),
         scratch_shapes=[pltpu.VMEM((3 * wide, 3 * cin), F32)],
         compiler_params=params(),
-        cost_estimate=pl.CostEstimate(flops=18 * cin * wide * pixels, bytes_accessed=2 * (cin + wide) * pixels, transcendentals=0),
+        cost_estimate=BRIEF,
     )(dz, a, masks)
 
 
@@ -735,7 +700,7 @@
         out_shape=outputs,
         scratch_shapes=scratch,
         compiler_params=params(),
-        cost_estimate=pl.CostEstimate(flops=flops, bytes_accessed=16 * 256 * pixels, transcendentals=0),
+        cost_estimate=BRIEF,
     )(*operands)
 
 
@@ -760,15 +725,59 @@
     pack_vectors(stats_ref, *as_rows([jnp.concatenate(means, axis=0), jnp.concatenate(spreads, axis=0)]))
 
 
+def parameter_kernel(
+    depth, told_ref, w_pool_ref, w_proj_ref, area_ref, branch_ref, proj_ref, first_ref, second_ref, low_ref, pooled_ref
+):
+    devices, rows, _ = told_ref.shape
+    _, taps, outs, wide = w_pool_ref.shape
+    low_share = LOWC // devices
+    proj_ref[...] = jnp.zeros_like(proj_ref)
+    low_ref[...] = jnp.zeros_like(low_ref)
+    branch_ref[...] = jnp.zeros_like(branch_ref)
+
+    def over(row, place):
+        pieces = [told_ref[c, row : row + 1, depth + place * outs : depth + (place + 1) * outs] for c in range(devices)]
+        return jnp.concatenate(pieces, axis=1)
+
+    for c in range(devices):
+        for i in range(2):
+            branch_ref[c, i : i + 1, : 4 * outs] = told_ref[c, i : i + 1, depth : depth + 4 * outs]
+            at = depth + 128 * i
+            low_ref[i : i + 1, c * low_share : (c + 1) * low_share] = told_ref[c, 4:5, at : at + low_share]
+    for i in range(2):
+        proj_ref[i : i + 1] = over(2, 1 + 2 * i)
+        first_ref[i : i + 1] = over(3, 2 * i)
+        second_ref[i : i + 1] = over(3, 1 + 2 * i)
+    gain, shift = over(2, 0), over(2, 2)
+    pre = jnp.zeros((rows, wide), F32)
+    means = []
+    for c in range(devices):
+        means.append((told_ref[c, :, :depth] / area_ref[...]).astype(BF))
+    means = jnp.concatenate(means, axis=1)
+    for k in range(taps):
+        part = means[:, k * wide : (k + 1) * wide]
+        pre = pre + jnp.concatenate([dot_nt(part, w_pool_ref[c, k]) for c in range(devices)], axis=1)
+    number = iota((rows, 1), 0)
+    real = jnp.where(number < pooled_ref.shape[2], 1.0, 0.0)
+    images = pooled_ref.shape[2]
+    mean = jnp.sum(pre * real, axis=0, keepdims=True) / images
+    var = jnp.sum(pre * pre * real, axis=0, keepdims=True) / images - mean * mean
+    y = gain * ((pre - mean) * lax.rsqrt(var + EPSILON)) + shift
+    act = (y * jax.nn.sigmoid(y)).astype(BF)
+    pooled_ref[0] = dot_nt(w_proj_ref[...], act)[:, :images]
+
+
 def project_kernel(
-    swapped, told, counts, gains, w_ref, broad, valid, low_stats, scalars, places, out_ref, left_ref, right_ref, stats_ref
+    swapped, told, counts, gains, w_ref, broad, member, valid, low_stats, scalars, places, out_ref, left_ref, right_ref, stats_ref
 ):
     devices, four, share = swapped.shape
     groups = told.shape[0]
     margin = left_ref.shape[1]
     mine = places[0]
     number = lax.broadcasted_iota(jnp.int32, (groups, 1), 0)
-    total = broad[...]
+    total = jnp.zeros(out_ref.shape, F32)
+    for i in range(broad.shape[2]):
+        total = total + broad[0, :, i : i + 1] * member[i : i + 1]
     for j in range(devices):
         c = places[1 + j]
         group = told[:, c]
@@ -958,58 +967,93 @@
         shifted_taps(lambda first, n, rows=rows: dz_ref[rows, pl.ds(start + first, n)], lanes, 6 * (k + 1), masks, store)
     if plain:
         taps_ref[9 * len(branches) * outs :] = dz_ref[:outs, pl.ds(start + PAD, lanes)]
-    acc_ref[...] += dot_nt(taps_ref[...], jnp.concatenate([x[0] for x in x_refs], axis=0))
+    acc_ref[...] += dot_nt(taps_ref[...], jnp.concatenate([x[0, 0] for x in x_refs], axis=0))
 
     @pl.when(step == pl.num_programs(0) - 1)
     def _():
-        out_ref[...] = acc_ref[...].astype(BF)
-
-
-def pyramid_weight_grad(dz, x_blocks, places, masks, branches, plain):
-    groups, slim, lanes = x_blocks[0].shape
+        rows = 9 * len(branches) * outs
+        out_ref[:rows] = acc_ref[:rows].astype(BF)
+        spare = out_ref.shape[0] - acc_ref.shape[0]
+        if spare:
+            out_ref[rows : rows + spare] = jnp.zeros((spare, out_ref.shape[1]), BF)
+        if plain:
+            out_ref[rows + spare :] = acc_ref[rows:].astype(BF)
+
+
+def pyramid_weight_grad(dz, x, masks, branches, plain, spare=0):
+    devices, groups, slim, lanes = x.shape
     outs, canvas = dz.shape[0] // 4, groups * lanes
-    channels = slim * len(x_blocks)
+    channels = slim * devices
     out_rows = (9 * len(branches) + plain) * outs
     whole = pl.BlockSpec(memory_space=pltpu.VMEM)
-
-    def kernel(places_ref, *refs):
-        pyramid_weight_kernel(lanes, outs, branches, plain, *refs)
-
+    block = lambda j: pl.BlockSpec((1, 1, slim, lanes), lambda i: (j, i, 0, 0))
     return pl.pallas_call(
-        kernel,
-        grid_spec=pltpu.PrefetchScalarGridSpec(
-            num_scalar_prefetch=1,
-            grid=(groups,),
-            in_specs=[whole, pl.BlockSpec((1, 8, lanes), lambda i, p: (i, 0, 0))]
-            + [pl.BlockSpec((1, slim, lanes), lambda i, p: (p[i], 0, 0))] * len(x_blocks),
-            out_specs=whole,
-            scratch_shapes=[pltpu.VMEM((out_rows, lanes), BF), pltpu.VMEM((out_rows, channels), F32)],
-        ),
-        out_shape=jax.ShapeDtypeStruct((out_rows, channels), BF),
+        lambda *refs: pyramid_weight_kernel(lanes, outs, branches, plain, *refs),
+        grid=(groups,),
+        in_specs=[whole, pl.BlockSpec((1, 8, lanes), lambda i: (i, 0, 0))] + [block(j) for j in range(devices)],
+        out_specs=whole,
+        out_shape=jax.ShapeDtypeStruct((out_rows + spare, channels), BF),
+        scratch_shapes=[pltpu.VMEM((out_rows, lanes), BF), pltpu.VMEM((out_rows, channels), F32)],
         compiler_params=params(),
         cost_estimate=pl.CostEstimate(flops=2 * out_rows * channels * canvas, bytes_accessed=2 * (4 * outs + channels) * canvas, transcendentals=0),
-    )(places, dz, masks, *x_blocks)
-
-
-def canvas_kernel(groups, devices, outs, stack_size, count, tab_top, tab_low, *refs):
-    piece_refs, refs = refs[: 4 * devices], refs[4 * devices :]
-    centred_ref, valid_ref, member_ref, w_ref, cols_ref, offset_ref = refs[:6]
-    dz_ref, sums_ref, proj_ref, image_ref, pieces_ref, dy_ref = refs[6:]
+    )(dz, masks, *([x] * devices))
+
+
+def slope_kernel(first, centred_ref, valid_ref, cols_ref, offset_ref, slope_ref, act_ref):
+    lane = iota(offset_ref.shape, 1)
+    gain, shift, scale, mean = (cols_ref[:, i : i + 1] for i in range(4))
+    group = first + pl.program_id(0)
+    offset = jnp.sum(jnp.where(lane == group, offset_ref[...], 0.0), axis=1, keepdims=True) - mean
+    slant, level = gain * scale, gain * scale * offset + shift
+    y = centred_ref[0].astype(F32) * slant + level
+    gate = 0.5 + 0.5 * jnp.tanh(0.5 * y)
+    valid = valid_ref[0, 6:7]
+    through = gate * valid
+    act_ref[0] = (y * through).astype(BF)
+    slope_ref[0] = (through * (1.0 + y * (1.0 - gate))).astype(BF)
+
+
+def slopes(first, number, centred, canvas_rows, cols, offsets, into=None):
+    groups, four, pixels = centred.shape
+    whole = pl.BlockSpec(memory_space=pltpu.VMEM)
+    take = lambda rows: pl.BlockSpec((1, rows, pixels), lambda i: (first + i, 0, 0))
+    shape = jax.ShapeDtypeStruct((groups, four, pixels), BF)
+    operands = [centred, canvas_rows, cols, offsets]
+    in_specs = [take(four), take(8), whole, whole]
+    aliases = {}
+    if into is not None:
+        aliases = {4: 0, 5: 1}
+        operands += into
+        in_specs += [pl.BlockSpec(memory_space=pl.ANY)] * 2
+    return pl.pallas_call(
+        lambda *refs: slope_kernel(first, *refs[:4], *refs[-2:]),
+        grid=(number,),
+        in_specs=in_specs,
+        out_specs=[take(four), take(four)],
+        out_shape=[shape, shape],
+        input_output_aliases=aliases,
+        compiler_params=params(),
+        cost_estimate=BRIEF,
+    )(*operands)
+
+
+def canvas_kernel(groups, devices, *refs):
+    dz_refs, refs = refs[:devices], refs[devices:]
+    centred_ref, slope_ref, rows_ref, member_ref, w_ref, cols_ref, offset_ref, count = refs[:8]
+    dz_ref, proj_ref, sums_ref, image_ref, pieces_ref, dy_ref = refs[8:]
     step = pl.program_id(0)
-    four = 4 * outs
-    half, share = piece_refs[0].shape[1:]
-    pixels = share * devices
-    group = lax.rem(step, groups)
-    gain, shift, scale, mean = (cols_ref[:, i : i + 1] for i in range(4))
-    lane = lax.broadcasted_iota(jnp.int32, offset_ref.shape, 1)
-    offset = jnp.sum(jnp.where(lane == group, offset_ref[...], 0.0), axis=1, keepdims=True) - mean
-    valid = valid_ref[0, 6:7]
+    four, pixels = centred_ref.shape[1:]
+    share = dz_refs[0].shape[2]
+    group = jnp.where(step < groups, step, step - groups)
+    gain, scale, mean = (cols_ref[:, i : i + 1] for i in (0, 2, 3))
+    offset = jnp.sum(jnp.where(iota(offset_ref.shape, 1) == group, offset_ref[...], 0.0), axis=1, keepdims=True) - mean
+    level = offset * scale
+    valid = rows_ref[0, 6:7]
     at = pl.multiple_of(group * pixels, 128)
 
     @pl.when(step == 0)
     def _():
         sums_ref[...] = jnp.zeros_like(sums_ref)
-        proj_ref[...] = jnp.zeros_like(proj_ref)
         image_ref[...] = jnp.zeros_like(image_ref)
         dz_ref[:, :PAD] = jnp.zeros((four, PAD), BF)
         dz_ref[:, PAD + groups * pixels :] = jnp.zeros((four, PAD), BF)
@@ -1017,88 +1061,58 @@
     @pl.when(step < groups)
     def _():
         for i in range(devices):
-            for h, table in enumerate((tab_top, tab_low)):
-                own, near = piece_refs[4 * i + 2 * h], piece_refs[4 * i + 2 * h + 1]
-                is_own = table[group * devices + i] < stack_size
-                rows, part = slice(h * half, (h + 1) * half), slice(i * share, (i + 1) * share)
-                pieces_ref[rows, part] = jnp.where(is_own, own[0], near[0])
+            pieces_ref[:, i * share : (i + 1) * share] = dz_refs[i][0]
+        proj_ref[0] = pieces_ref[...]
         image_ref[...] += dot_nt(pieces_ref[...], member_ref[0].astype(BF))
         total = jnp.zeros((four, 128), F32)
         total_normed = jnp.zeros((four, 128), F32)
-        for start, size in tiles(pixels, 384):
+        for start, size in tiles(pixels, 512):
             part = slice(start, start + size)
-            normed = (centred_ref[0, :, part].astype(F32) + offset) * scale
-            y = gain * normed + shift
-            gate = jax.nn.sigmoid(y)
-            act = (y * gate * valid[:, part]).astype(BF)
-            proj_ref[...] += dot_nt(pieces_ref[:, part], act)
-            slope = gate * (1.0 + y * (1.0 - gate)) * valid[:, part]
-            dy = dot(w_ref[...], pieces_ref[:, part]) * slope
+            dy = dot(w_ref[...], pieces_ref[:, part]) * slope_ref[0, :, part].astype(F32)
             dy_ref[:, pl.ds(at + start, size)] = dy
-            both = dy * normed
-            for tile in range(0, size, 128):
-                total = total + dy[:, tile : tile + 128]
-                total_normed = total_normed + both[:, tile : tile + 128]
+            total = total + fold(dy)
+            total_normed = total_normed + fold(dy * (centred_ref[0, :, part].astype(F32) * scale + level))
         sums_ref[:, 0:1] += jnp.sum(total, axis=1, keepdims=True)
         sums_ref[:, 1:2] += jnp.sum(total_normed, axis=1, keepdims=True)
 
     @pl.when(step >= groups)
     def _():
-        normed = (centred_ref[0].astype(F32) + offset) * scale
-        parts = (sums_ref[:, 0:1] + normed * sums_ref[:, 1:2]) * (valid * count[0])
-        dz = (scale * gain) * (dy_ref[:, pl.ds(at, pixels)] - parts)
-        dz_ref[:, pl.ds(PAD + at, pixels)] = dz.astype(BF)
-
-
-def canvas_grad(top, low, tables, centred, valid, member, w_turned, cols, offsets, inverse_count):
+        steep = scale * gain
+        rise = steep * count[0] * sums_ref[:, 1:2] * scale
+        constant = steep * count[0] * (sums_ref[:, 0:1] + level * sums_ref[:, 1:2])
+        parts = centred_ref[0].astype(F32) * rise + constant
+        dz_ref[:, pl.ds(PAD + at, pixels)] = (steep * dy_ref[:, pl.ds(at, pixels)] - valid * parts).astype(BF)
+
+
+def canvas_grad(proj_dz, slope, centred, canvas_rows, member, w_turned, cols, offsets, scalars):
     groups, four, pixels = centred.shape
-    stack_size, half, share = top[0].shape
-    devices = tables[0].shape[0] // groups
-    wide = 2 * half
-
-    def piece(i, table):
-        def index(s, top_table, low_table):
-            at = jnp.minimum(s, groups - 1) * devices + i
-            return (lax.rem((top_table if table == 0 else low_table)[at], stack_size), 0, 0)
-
-        return pl.BlockSpec((1, half, share), index)
-
-    by_group = lambda s, a, b: (lax.rem(s, groups), 0, 0)
+    everyone, wide, share = proj_dz.shape
+    devices = everyone // groups
+    ahead = lambda s: jnp.minimum(s, groups - 1)
+    by_group = lambda rows: pl.BlockSpec((1, rows, pixels), lambda s: (jnp.where(s < groups, s, s - groups), 0, 0))
+    near = lambda rows: pl.BlockSpec((1, rows, pixels), lambda s: (ahead(s), 0, 0))
+    piece = lambda i: pl.BlockSpec((1, wide, share), lambda s: (ahead(s) * devices + i, 0, 0))
     whole = pl.BlockSpec(memory_space=pltpu.VMEM)
-
-    def kernel(tab_top, tab_low, *refs):
-        canvas_kernel(groups, devices, four // 4, stack_size, refs[-7], tab_top, tab_low, *refs[:-7], *refs[-6:])
-
     return pl.pallas_call(
-        kernel,
-        grid_spec=pltpu.PrefetchScalarGridSpec(
-            num_scalar_prefetch=2,
-            grid=(2 * groups,),
-            in_specs=[piece(i, table) for i in range(devices) for table in (0, 0, 1, 1)]
-            + [
-                pl.BlockSpec((1, four, pixels), by_group),
-                pl.BlockSpec((1, 8, pixels), by_group),
-                pl.BlockSpec((1, member.shape[1], pixels), by_group),
-                whole,
-                whole,
-                whole,
-                pl.BlockSpec(memory_space=pltpu.SMEM),
-            ],
-            out_specs=[whole] * 4,
-            scratch_shapes=[pltpu.VMEM((wide, pixels), BF), pltpu.VMEM((four, groups * pixels), F32)],
-        ),
+        lambda *refs: canvas_kernel(groups, devices, *refs),
+        grid=(2 * groups,),
+        in_specs=[piece(i) for i in range(devices)]
+        + [by_group(four), near(four), by_group(8), near(member.shape[1]), whole, whole, whole]
+        + [pl.BlockSpec(memory_space=pltpu.SMEM)],
+        out_specs=[whole, near(wide), whole, whole],
         out_shape=[
             jax.ShapeDtypeStruct((four, 2 * PAD + groups * pixels), BF),
+            jax.ShapeDtypeStruct((groups, wide, pixels), BF),
             jax.ShapeDtypeStruct((four, 128), F32),
-            jax.ShapeDtypeStruct((wide, four), F32),
             jax.ShapeDtypeStruct((wide, member.shape[1]), F32),
         ],
+        scratch_shapes=[pltpu.VMEM((wide, pixels), BF), pltpu.VMEM((four, groups * pixels), F32)],
         compiler_params=params(),
-        cost_estimate=pl.CostEstimate(flops=4 * wide * four * groups * pixels, bytes_accessed=8 * wide * groups * pixels, transcendentals=four * groups * pixels),
-    )(*tables, *([*top, *low] * devices), centred, valid, member, w_turned, cols, offsets, inverse_count)
-
-
-def assembly_kernel(groups, devices, order, where_ref, perm_ref, pieces, plain, out_ref, one_ref):
+        cost_estimate=pl.CostEstimate(flops=2 * wide * four * groups * pixels, bytes_accessed=8 * wide * groups * pixels, transcendentals=0),
+    )(*([proj_dz] * devices), centred, slope, canvas_rows, member, w_turned, cols, offsets, scalars)
+
+
+def assembly_kernel(groups, devices, order, where_ref, pieces, spare, plain, out_ref, one_ref, rest_ref):
     line = groups // 2
     cin = out_ref.shape[1]
     depth = cin // devices
@@ -1109,8 +1123,8 @@
             for j in range(devices):
                 part = slice(j * slim, (j + 1) * slim)
                 pair = jnp.concatenate([refs[r][:, part], refs[r + 1][:, part]], axis=1)
-                at = pl.multiple_of(perm_ref[j] * depth + r * slim, 128)
-                target[:, pl.ds(at, 2 * slim)] = pair.astype(F32)
+                at = j * depth + r * slim
+                target[:, at : at + 2 * slim] = pair.astype(F32)
 
     for z in range(line):
         for e in range(2):
@@ -1119,50 +1133,45 @@
             @pl.when((where_ref[0] // 2 == z) & (where_ref[0] % 2 == e))
             def _(chosen=chosen):
                 fill([pieces[i] for i in chosen], out_ref)
-                if one_ref is not None:
-
-                    @pl.when(pl.program_id(0) == 0)
-                    def _():
-                        fill([plain[i] for i in chosen], one_ref)
-
-
-def assemble(branches, plain, found, devices, groups, strip, perm, into, outs, cin):
+
+                @pl.when(pl.program_id(0) == 0)
+                def _():
+                    fill([plain[i] for i in chosen], one_ref)
+                    for r, i in enumerate(chosen):
+                        rest_ref[r] = spare[i][...]
+
+
+def assemble(found, devices, groups, strip, outs, cin):
     order = sorted(found)
     pieces = [found[key] for key in order]
     slots, width = len(pieces), pieces[0].shape[1]
-    rows = 3 * outs
+    rows, spare = 9 * outs, 3 * outs
     smem = pl.BlockSpec(memory_space=pltpu.SMEM)
-    operands = [strip[None].astype(jnp.int32), perm] + pieces
-    in_specs = [smem, smem] + [pl.BlockSpec((rows, width), lambda i: (i, 0))] * slots
-    first = 3 * branches[0]
-    out_specs = [pl.BlockSpec((rows, cin), lambda i: (first + i, 0))]
-    out_shape = [jax.ShapeDtypeStruct((27 * outs, cin), F32)]
-    if plain:
-        operands += pieces
-        in_specs += [pl.BlockSpec((outs, width), lambda i: (9 * len(branches), 0))] * slots
-        out_specs.append(pl.BlockSpec((outs, cin), lambda i: (0, 0)))
-        out_shape.append(jax.ShapeDtypeStruct((outs, cin), F32))
-    aliases = {}
-    if into is not None:
-        aliases = {len(operands): 0}
-        operands.append(into)
-        in_specs.append(pl.BlockSpec(memory_space=pl.ANY))
-
-    def kernel(where_ref, perm_ref, *refs):
-        one_ref = refs[-1] if plain else None
-        out_ref = refs[-2] if plain else refs[-1]
-        assembly_kernel(groups, devices, order, where_ref, perm_ref, refs[:slots], refs[slots : 2 * slots], out_ref, one_ref)
+
+    def kernel(where_ref, *refs):
+        parts = [refs[i * slots : (i + 1) * slots] for i in range(3)]
+        assembly_kernel(groups, devices, order, where_ref, *parts, *refs[3 * slots :])
 
     return pl.pallas_call(
         kernel,
-        grid=(3 * len(branches),),
-        in_specs=in_specs,
-        out_specs=out_specs,
-        out_shape=out_shape,
-        input_output_aliases=aliases,
+        grid=(3,),
+        in_specs=[smem]
+        + [pl.BlockSpec((rows, width), lambda i: (i, 0))] * slots
+        + [pl.BlockSpec((spare, width), lambda i: (9, 0))] * slots
+        + [pl.BlockSpec((outs, width), lambda i: (30, 0))] * slots,
+        out_specs=[
+            pl.BlockSpec((rows, cin), lambda i: (i, 0)),
+            pl.BlockSpec((outs, cin), lambda i: (0, 0)),
+            pl.BlockSpec((groups, spare, width), lambda i: (0, 0, 0)),
+        ],
+        out_shape=[
+            jax.ShapeDtypeStruct((27 * outs, cin), F32),
+            jax.ShapeDtypeStruct((outs, cin), F32),
+            jax.ShapeDtypeStruct((groups, spare, width), BF),
+        ],
         compiler_params=params(),
-        cost_estimate=pl.CostEstimate(flops=0, bytes_accessed=9 * len(branches) * outs * cin * 6, transcendentals=0),
-    )(*operands)
+        cost_estimate=pl.CostEstimate(flops=0, bytes_accessed=27 * outs * cin * 6, transcendentals=0),
+    )(strip[None].astype(jnp.int32), *pieces, *pieces, *pieces)
 
 
 def local(
@@ -1219,72 +1228,26 @@
     valid_strip = strip_rows[6:7]
 
     mine = feats * valid_strip.astype(BF)
-    x_blocks, origin = gather_blocks(mine)
-    perm = jnp.stack(origin).astype(jnp.int32)
     slice_depth = depth // groups
-    x_slice = lax.all_to_all(mine.reshape(groups, slice_depth, pixels), "row", 0, 0)
-
-    vectors = jnp.concatenate(
+
+    line = lambda *parts: jnp.concatenate([jnp.pad(v.astype(F32), (0, size - v.shape[0])) for v, size in parts])
+    rank = lambda v: line((v.astype(F32).reshape(-1), 256))
+    low_share = LOWC // devices
+    vectors = jnp.stack(
         [
-            v.astype(F32).reshape(-1)
-            for v in (mid_gain, mid_shift, dec_gain, dec_shift, low_gain, low_shift)
+            rank(mid_gain[:4]),
+            rank(mid_shift[:4]),
+            rank(jnp.concatenate([mid_gain[4:], mid_shift[4:]])),
+            rank(jnp.concatenate([dec_gain, dec_shift])),
+            line((low_gain, 128), (low_shift, 128)),
         ]
     )
-    sums = dot_nt(mine, member_strip)[:, :images].reshape(-1)
-    sums, x_slice = lax.optimization_barrier((jnp.concatenate([sums, vectors]), x_slice))
-    told = tell_all(sums).reshape(groups, devices, -1)
-    pool_sums = jnp.sum(told[:, :, : depth * images], axis=0).reshape(devices * depth, images)
-    vectors = lax.dynamic_index_in_dim(told, strip, 0, False)[:, depth * images :]
-    norm_rows = vectors[:, : 16 * outs].reshape(devices, 16, outs)
-    gain_rows = [norm_rows[:, k].reshape(-1) for k in range(16)]
-    branch_gains = jnp.stack([norm_rows[:, :4].reshape(devices, -1), norm_rows[:, 6:10].reshape(devices, -1)], axis=1)
-    branch_gains = jnp.pad(branch_gains, ((0, 0), (0, 0), (0, 256 - 4 * outs)))
-    proj_gain = jnp.stack([gain_rows[5], gain_rows[11]])
-    first_gain = jnp.stack([gain_rows[12], gain_rows[14]])
-    second_gain = jnp.stack([gain_rows[13], gain_rows[15]])
-    low_share = LOWC // devices
-    low_gain_all = vectors[:, 16 * outs : 16 * outs + low_share].reshape(-1)
-    low_shift_all = vectors[:, 16 * outs + low_share : 16 * outs + 2 * low_share].reshape(-1)
-    low_gains = jnp.pad(jnp.stack([low_gain_all, low_shift_all]), ((0, 0), (0, 256 - LOWC)))
-
-    low_in = lowlevel * valid_fine_strip
-    low_part = dot(w_low, low_in).astype(BF)
-    low_pre = lax.psum_scatter(low_part, "ch", scatter_dimension=1, tiled=True).astype(F32)
-
-    first_taps = w_dec1.transpose(1, 0, 2)
-    w1 = lax.all_gather(jnp.concatenate([first_taps[:, :, LOWC:], first_taps[:, :, :LOWC]], axis=2), "ch", axis=0)
-    proj_taps = w_proj.reshape(outs, 5, wide).transpose(1, 0, 2)
-    pool_taps = w_pool.reshape(outs, -1, wide).transpose(1, 0, 2)
-    rest = lax.all_gather(jnp.concatenate([w_dec2.transpose(1, 0, 2), proj_taps, pool_taps], axis=0), "ch", axis=0)
-    w2, wp, w_pool_all = rest[:, :9], rest[:, 9:14], rest[:, 14:]
-    wp_acts = wp[:, :4].reshape(devices, 4, outs, devices, outs).transpose(3, 0, 2, 1, 4).reshape(devices, wide, 4 * outs)
-    wp_pool = wp[:, 4].reshape(wide, wide)
-
-    pooled = (pool_sums / area[None]).astype(BF)
-    pool_pre = jnp.einsum(
-        "ckoi,kin->con", w_pool_all, pooled.reshape(-1, wide, images), preferred_element_type=F32
-    ).reshape(wide, images)
-    pool_mean = jnp.mean(pool_pre, axis=1)
-    pool_scale = lax.rsqrt(jnp.mean(pool_pre * pool_pre, axis=1) - pool_mean * pool_mean + EPSILON)
-    pool_normed = (pool_pre - pool_mean[:, None]) * pool_scale[:, None]
-    gain_mid, shift_mid = mid_gain.astype(F32), mid_shift.astype(F32)
-    pool_shifted = gain_rows[4][:, None] * pool_normed + gain_rows[10][:, None]
-    pool_acts = jax.nn.silu(pool_shifted).astype(BF)
-    broad_part = dot(wp_pool, pool_acts)
-    own_rows = lambda v: lax.dynamic_slice_in_dim(v, me * outs, outs, axis=0)
-    pool_act, pool_scale, pool_normed, pool_shifted = map(own_rows, (pool_acts, pool_scale, pool_normed, pool_shifted))
-
-    w_taps = w_atrous.transpose(0, 2, 1, 3).reshape(3, 9 * outs, -1)
-    centre, up, down = pyramid(x_blocks, perm, w_taps, w_one, strip_rows)
-    up, down, places, low_pre = lax.optimization_barrier((up, down, places, low_pre))
-    fwd = [(i, i + 1) for i in range(groups - 1)]
-    bwd = [(i + 1, i) for i in range(groups - 1)]
-    from_next = lax.ppermute(up, "row", bwd)
-    from_prev = lax.ppermute(down, "row", fwd)
-
-    (
-        canvas_rows, member_canvas, strip_counts, counts_c, counts_f, mine_rows, window_valid, valid_wide, fine_masks, enlarge,
-    ) = geometry_call(
+    message_rows = -(-images // 8) * 8
+    sums = dot_nt(member_strip, mine)[:message_rows]
+    told = tell_row(sums)
+    told = tell_group(jnp.concatenate([jnp.sum(told, axis=0), jnp.pad(vectors, ((0, message_rows - 5), (0, 0)))], axis=1))
+
+    geometry = geometry_call(
         lambda *refs: geometry_kernel(margin, *refs),
         heights, widths, places,
         [
@@ -1293,24 +1256,69 @@
             jax.ShapeDtypeStruct((window, ext), BF),
         ],
     )
+
+    x_blocks, origin, (told, late_low, late_w1, late_w2, late_proj, late_pool, *geometry) = gather_blocks(
+        mine, (told, lowlevel, w_dec1, w_dec2, w_proj, w_pool, *geometry)
+    )
+    (
+        canvas_rows, member_canvas, strip_counts, counts_c, counts_f, mine_rows, window_valid, valid_wide, fine_masks, enlarge,
+    ) = geometry
+    perm = jnp.stack(origin).astype(jnp.int32)
+    mine, told = lax.optimization_barrier((mine, told))
+    x_slice = lax.all_to_all(mine.reshape(groups, slice_depth, pixels), "row", 0, 0)
+    first_told = told
+
+    proj_taps = late_proj.reshape(outs, 5, wide).transpose(1, 0, 2)
+    pool_taps = late_pool.reshape(outs, -1, wide).transpose(1, 0, 2)
+    rest = lax.all_gather(jnp.concatenate([late_w2.transpose(1, 0, 2), proj_taps, pool_taps], axis=0), "ch", axis=0)
+    w2, wp, w_pool_all = rest[:, :9], rest[:, 9:14], rest[:, 14:]
+    wp_acts = wp[:, :4].reshape(devices, 4, outs, devices, outs).transpose(3, 0, 2, 1, 4).reshape(devices, wide, 4 * outs)
+    wp_pool = wp[:, 4].reshape(wide, wide)
+
+    low_in = late_low * valid_fine_strip
+    low_part = dot(w_low, low_in).astype(BF)
+    low_pre = lax.psum_scatter(low_part, "ch", scatter_dimension=1, tiled=True).astype(F32)
+    first_taps = late_w1.transpose(1, 0, 2)
+    w1 = lax.all_gather(jnp.concatenate([first_taps[:, :, LOWC:], first_taps[:, :, :LOWC]], axis=2), "ch", axis=0)
+
+    area_rows = jnp.pad(area, (0, message_rows - images), constant_values=1.0)[:, None]
+    pair = shaped(2, 256)
+    branch_gains, proj_gain, first_gain, second_gain, low_gains, broad_part = small_call(
+        lambda *refs: parameter_kernel(depth, *refs),
+        [first_told, w_pool_all, wp_pool, area_rows],
+        (),
+        [shaped(devices, 2, 256), pair, pair, pair, pair, shaped(1, wide, images)],
+        0,
+    )
+
+    w_taps = w_atrous.transpose(0, 2, 1, 3).reshape(3, 9 * outs, -1)
+    centre, up, down = pyramid(x_blocks, perm, w_taps, w_one, strip_rows)
+    up, down, x_slice = lax.optimization_barrier((up, down, x_slice))
+    x_canvas = lax.all_gather(x_slice, "ch", axis=0)
+    fwd = [(i, i + 1) for i in range(groups - 1)]
+    bwd = [(i + 1, i) for i in range(groups - 1)]
+    from_next = lax.ppermute(up, "row", bwd)
+    from_prev = lax.ppermute(down, "row", fwd)
+
     member_mine, valid_mine = mine_rows[:images], mine_rows[members : members + 1]
     valid_fine = valid_wide[:, WF:-WF]
-    broad_part = jnp.dot(broad_part, member_mine, precision=HIGHEST)
     low_stats = vector_tile(*local_moments(low_pre, valid_fine[0]))[:4]
 
     order = jnp.argsort(perm)
-    x_places = jnp.arange(groups, dtype=jnp.int32)
 
     def columns(s, lead):
         s = s.reshape((groups,) + lead + (devices, slice_depth))
-        s = jnp.take(s, order, axis=len(lead) + 1)
         s = jnp.moveaxis(s, 0, len(lead) + 1)
         return s.reshape(lead + (devices * depth,)).astype(F32)
+
+    gain_mid, shift_mid = mid_gain.astype(F32), mid_shift.astype(F32)
+
+    branch_valid, branch_gains, wp_acts, broad_part = lax.optimization_barrier((valid_strip, branch_gains, wp_acts, broad_part))
 
     tile = jax.ShapeDtypeStruct((everyone, 8, 128), F32)
     centered, pieces, stats = small_call(
         branch_kernel,
-        [centre, from_next, from_prev, valid_strip],
+        [centre, from_next, from_prev, branch_valid],
         (),
         [
             jax.ShapeDtypeStruct((4 * outs, pixels), BF),
@@ -1320,15 +1328,14 @@
         0,
     )
     told_branch = swap_all(stats)
-    swapped, x_slice = lax.optimization_barrier((swap_ch(pieces), x_slice))
-    slice_blocks, _ = gather_blocks(x_slice)
+    swapped = swap_ch(pieces)
     proj_pre, proj_left, proj_right, stats = small_call(
         project_kernel,
         [
-            swapped, told_branch.reshape(groups, devices, 8, 128), strip_counts, branch_gains, wp_acts, broad_part,
+            swapped, told_branch.reshape(groups, devices, 8, 128), strip_counts, branch_gains, wp_acts, broad_part, member_mine,
             valid_mine, low_stats, scalars, jnp.concatenate([strip[None].astype(jnp.int32), perm]),
         ],
-        (8, 9),
+        (9, 10),
         [
             jax.ShapeDtypeStruct((wide, share), F32),
             jax.ShapeDtypeStruct((wide, margin), F32),
@@ -1337,10 +1344,16 @@
         ],
         8 * wide * wide * share,
     )
-    told_proj = swap_all(stats)
     proj_prev, proj_next = to_next(proj_right), to_previous(proj_left)
     low_prev, low_next = to_next(low_pre[:, -WF:]), to_previous(low_pre[:, :WF])
+    told_proj, proj_prev, proj_next, low_prev, low_next = lax.optimization_barrier(
+        (swap_all(stats), proj_prev, proj_next, low_prev, low_next)
+    )
     canvas_centered = lax.all_gather(centered, "row", axis=0)
+    own_told = lax.dynamic_index_in_dim(told_branch.reshape(groups, devices, 8 * 128), me, 1, False)
+    own_mean, own_scale = merge_moments(own_told[:, : 4 * outs], own_told[:, 256 : 256 + 4 * outs], strip_counts[:, 0], count)
+    cols = jnp.stack([gain_mid[:4].reshape(-1), shift_mid[:4].reshape(-1), own_scale, own_mean], axis=1)
+    offsets = own_told[:, : 4 * outs].T
 
     lanes = WF * rows_per_step(fine_rows)
     edge = jax.ShapeDtypeStruct((wide, WF), F32)
@@ -1359,9 +1372,11 @@
         [pltpu.VMEM((wide, window), BF), pltpu.VMEM((3 * wide, 3 * (wide + LOWC)), BF), state(3, wide)],
         fine, work,
     )
-    stats, *slice_blocks = lax.optimization_barrier((stats, *slice_blocks))
-    told_first = swap_all(stats)
     first_prev, first_next = to_next(first_bottom), to_previous(first_top)
+    told_first, first_prev, first_next, told_proj = lax.optimization_barrier((swap_all(stats), first_prev, first_next, told_proj))
+    proj_told = told_proj.reshape(everyone, 8 * 128)
+    proj_mean, proj_scale = merge_moments(proj_told[:, :wide], proj_told[:, 256 : 256 + wide], counts_c[:, 0], count)
+    proj_normed = (proj_pre - proj_mean[:, None]) * proj_scale[:, None]
     first_act, second_pre, second_top, second_bottom, stats = decoder_call(
         lambda *refs: second_kernel(lanes, *refs),
         [first_prev, first_pre, first_next, told_first, counts_f, first_gain, valid_wide, fine_masks, w2, scalars],
@@ -1373,6 +1388,9 @@
     )
     told_second = swap_all(stats)
     second_prev, second_next = to_next(second_bottom), to_previous(second_top)
+    told_second, second_prev, second_next, x_canvas = lax.optimization_barrier(
+        (told_second, second_prev, second_next, x_canvas)
+    )
 
     classes = w_cls.shape[0]
     cot = jnp.pad(cotangent, ((0, -classes % 32), (0, 0)))
@@ -1413,14 +1431,13 @@
         fine, work,
     )
     second_sums = jnp.sum(told_sums, axis=0)
-    told_first_sums = swap_all(sums)
+    dy_prev, dy_next = to_next(dy_bottom), to_previous(dy_top)
+    told_first_sums, dy_prev, dy_next = lax.optimization_barrier((swap_all(sums), dy_prev, dy_next))
     first_sums = jnp.sum(told_first_sums, axis=0)
     class_share = first_sums[8 : 8 + class_rows]
     first_sums = first_sums[:8]
-    dy_prev, dy_next = to_next(dy_bottom), to_previous(dy_top)
     g_dec2 = decoder_weight_grad(second_dz, first_act, fine_masks, outs)
-    told_first_sums, g_dec2, canvas_centered = lax.optimization_barrier((told_first_sums, g_dec2, canvas_centered))
-    part_dec2 = lax.psum_scatter(g_dec2, "ch", scatter_dimension=0)
+    told_first_sums, g_dec2 = lax.optimization_barrier((told_first_sums, g_dec2))
     first_dz, grad_window, dy_low, low_part_sums = decoder_call(
         lambda *refs: first_back_kernel(lanes, *refs),
         [
@@ -1447,76 +1464,63 @@
     grad_coarse = grad_window[:, margin : margin + share]
     grad_coarse = grad_coarse.at[:, :margin].add(to_next(grad_window[:, margin + share :]))
     grad_coarse = grad_coarse.at[:, share - margin :].add(to_previous(grad_window[:, :margin]))
-    proj_told = told_proj.reshape(everyone, 8 * 128)
-    proj_mean, proj_scale = merge_moments(proj_told[:, :wide], proj_told[:, 256 : 256 + wide], counts_c[:, 0], count)
-    proj_normed = (proj_pre - proj_mean[:, None]) * proj_scale[:, None]
     dy = grad_coarse * silu_slope(proj_gain[0][:, None] * proj_normed + proj_gain[1][:, None]) * valid_mine
     both = vector_tile(jnp.sum(dy, axis=1), jnp.sum(dy * proj_normed, axis=1), low_part_sums[0], low_part_sums[1])
     both = jnp.concatenate([both, jnp.pad(class_share, ((0, 8 - class_rows), (0, 0)))])
-    told_both, g_dec1, part_dec2 = lax.optimization_barrier((tell_all(both), g_dec1, part_dec2))
+    told_both, g_dec1 = lax.optimization_barrier((tell_all(both), g_dec1))
+    part_dec = lax.psum_scatter(jnp.concatenate([g_dec2, g_dec1], axis=3), "ch", scatter_dimension=0)
     both = jnp.sum(told_both[:, :8], axis=0).reshape(4, 256)
     class_sums = told_both[:, 8 : 8 + class_rows].reshape(-1)
     bias_sums = class_sums[classes * wide : classes * wide + classes]
     class_sums = class_sums[: classes * wide].reshape(classes, wide)
     proj_sums, low_sums = both[:2], both[2:, :LOWC]
+
     proj_dz = norm_back(dy, proj_normed, proj_scale, proj_gain[0], proj_sums, valid_mine, count).astype(BF)
-
-    part_dec1 = lax.psum_scatter(g_dec1, "ch", scatter_dimension=0)
+    canvas_dz = lax.all_gather(proj_dz, BOTH, axis=0)
+    slope = slopes(0, groups, canvas_centered, canvas_rows, cols, offsets)
+    canvas_dz, *slope = lax.optimization_barrier((canvas_dz, *slope))
+
+    wp_own = lax.dynamic_index_in_dim(wp_acts, me, 0, False)
+    wp_pool_own = lax.dynamic_slice_in_dim(wp_pool, me * outs, outs, axis=1)
+    padded_dz, strips_dz, branch_sums, image_dz = canvas_grad(
+        canvas_dz, slope[0], canvas_centered, canvas_rows, member_canvas, wp_own.T, cols, offsets, 1.0 / count[None],
+    )
+    branch_sums = branch_sums[:, :2].T
+    image_dz = image_dz[:, :images]
+
+    padded_dz, part_dec = lax.optimization_barrier((padded_dz, part_dec))
+
+    def by_row(v):
+        v = v.reshape(groups, -1)
+        return jnp.pad(v, ((0, 0), (0, -v.shape[1] % wide))).reshape(groups, -1, wide)
+
+    shares = [by_row(part_dec[..., :wide]), by_row(part_dec[..., wide : 2 * wide]), by_row(part_dec[..., 2 * wide :])]
+    share_rows, split_at = shares[0].shape[1], 2 * shares[0].shape[1]
+    shares = lax.all_to_all(jnp.concatenate(shares, axis=1), "row", 0, 0)
+    shares = jnp.sum(shares.astype(F32), axis=0).astype(BF)
+
+    lined = groups == 8 and 2 * slice_depth == 128 and shares.shape[0] <= 3 * outs
+    part = pyramid_weight_grad(padded_dz, x_canvas, canvas_rows, (0, 1, 2), True, 3 * outs if lined else 0)
+    if lined:
+        part = part.at[27 * outs : 27 * outs + shares.shape[0]].set(shares)
+    part, padded_dz, first_told, image_dz, strips_dz, dy_low = lax.optimization_barrier(
+        (part, padded_dz, first_told, image_dz, strips_dz, dy_low)
+    )
 
     low_mean, low_scale = merge_moments(proj_told[:, 512 : 512 + LOWC], proj_told[:, 768 : 768 + LOWC], counts_f[:, 0], fine_count)
     low_normed = (low_pre - low_mean[:, None]) * low_scale[:, None]
-    low_dz = norm_back(dy_low, low_normed, low_scale, low_gain_all, low_sums, valid_fine, fine_count).astype(BF)
-    low_dz_all = lax.all_gather(low_dz, "ch", axis=1, tiled=True)
-
-    top, low, top_table, low_table = gather_all(proj_dz[: wide // 2], proj_dz[wide // 2 :])
-    wp_own = lax.dynamic_index_in_dim(wp_acts, me, 0, False)
-    wp_pool_own = lax.dynamic_slice_in_dim(wp_pool, me * outs, outs, axis=1)
-    own_told = lax.dynamic_index_in_dim(told_branch.reshape(groups, devices, 8 * 128), me, 1, False)
-    own_mean, own_scale = merge_moments(own_told[:, : 4 * outs], own_told[:, 256 : 256 + 4 * outs], strip_counts[:, 0], count)
-    cols = jnp.stack([gain_mid[:4].reshape(-1), shift_mid[:4].reshape(-1), own_scale, own_mean], axis=1)
-    padded_dz, branch_sums, g_proj_acts, image_dz = canvas_grad(
-        top,
-        low,
-        (top_table, low_table),
-        canvas_centered,
-        canvas_rows,
-        member_canvas,
-        wp_own.T,
-        cols,
-        own_told[:, : 4 * outs].T,
-        1.0 / count[None],
-    )
-    branch_sums = branch_sums[:, :2].T
-    image_dz = image_dz[:, :images]
-
-    g_lowlevel = lax.dot_general(w_low, low_dz_all, (((0,), (0,)), ((), ())), preferred_element_type=F32) * valid_fine_strip.astype(F32)
-    g_low = dot_nt(low_dz_all, low_in).astype(BF)
-    low_columns = g_low.shape[1]
-    g_low = jnp.pad(g_low, ((0, -LOWC % outs), (0, wide - low_columns))).reshape(-1, outs, wide)
-    padded_dz, g_low, part_dec1, part_dec2 = lax.optimization_barrier((padded_dz, g_low, part_dec1, part_dec2))
-    g_dec1, g_rest = lax.psum((part_dec1, jnp.concatenate([part_dec2, g_low])), "row")
-
-    into, g_w_one = None, None
-    if groups == 8 and 2 * slice_depth == 128:
-        for branches, plain in CHUNKS:
-            part = pyramid_weight_grad(padded_dz, slice_blocks, x_places, canvas_rows, branches, plain)
-            part, padded_dz = lax.optimization_barrier((part, padded_dz))
-            found, (g_dec1, g_rest) = gather_line(part, (g_dec1, g_rest))
-            got = assemble(branches, plain, found, devices, groups, strip, perm, into, outs, devices * depth)
-            into = got[0]
-            if plain:
-                g_w_one = got[1]
-    else:
-        part = pyramid_weight_grad(padded_dz, slice_blocks, x_places, canvas_rows, (0, 1, 2), True)
-        found = columns(lax.all_gather(part, "row", axis=0), (28 * outs,))
-        into, g_w_one = found[: 27 * outs], found[27 * outs :]
-    g_w_atrous = into.reshape(3, 9, outs, devices * depth).transpose(0, 2, 1, 3)
+    low_dz = norm_back(dy_low, low_normed, low_scale, low_gains[0, :LOWC], low_sums, valid_fine, fine_count).astype(BF)
+
+    pool_sums = first_told[:, :images, :depth].transpose(0, 2, 1).reshape(devices * depth, images)
+    pooled = (pool_sums / area[None]).astype(BF)
+    pool_pre = dot(w_pool, pooled)
+    pool_mean = jnp.mean(pool_pre, axis=1)
+    pool_scale = lax.rsqrt(jnp.mean(pool_pre * pool_pre, axis=1) - pool_mean * pool_mean + EPSILON)
+    pool_normed = (pool_pre - pool_mean[:, None]) * pool_scale[:, None]
+    pool_shifted = gain_mid[4][:, None] * pool_normed + shift_mid[4][:, None]
+    pool_act = jax.nn.silu(pool_shifted).astype(BF)
 
     g_proj_pool = jnp.dot(image_dz, pool_act.astype(F32).T, precision=HIGHEST)
-    g_proj_part = jnp.concatenate([g_proj_acts, g_proj_pool], axis=1).astype(BF)
-    g_proj = swap_ch(g_proj_part.reshape(devices, outs, 5 * outs))
-    g_proj = jnp.take(g_proj, order, axis=0)
-    g_w_proj = g_proj.reshape(devices, outs, 5, outs).transpose(1, 2, 0, 3).reshape(outs, -1).astype(F32)
 
     grad_pool_act = lax.dot_general(wp_pool_own.astype(F32), image_dz, (((0,), (0,)), ((), ())), precision=HIGHEST)
     dy_pool = grad_pool_act * silu_slope(pool_shifted)
@@ -1530,11 +1534,32 @@
     spread = jnp.dot(pool_dz.astype(F32) / area[None], member_strip[:images].astype(F32), precision=HIGHEST).astype(BF)
 
     strip_pad = lax.dynamic_slice_in_dim(padded_dz, strip * pixels, pixels + 2 * PAD, axis=1)
-    parts = input_grad(strip_pad, spread, strip_rows, w_taps, w_one, w_pool, perm)
-    g_feats = reduce_blocks([parts[i] for i in range(devices)]) * valid_strip
-
-    g_dec1, g_rest = g_dec1.astype(F32), g_rest.astype(F32)
-    g_dec2, g_low = g_rest[:9], g_rest[9:].reshape(-1, wide)[:LOWC, :low_columns]
+
+    parts = input_grad(strip_pad, spread, strip_rows, w_taps, w_one, w_pool, jnp.arange(devices, dtype=jnp.int32))
+    g_feats = lax.psum_scatter(parts, "ch", scatter_dimension=0).astype(F32) * valid_strip
+    low_dz_all = lax.all_gather(low_dz, "ch", axis=1, tiled=True)
+    g_lowlevel = lax.dot_general(w_low, low_dz_all, (((0,), (0,)), ((), ())), preferred_element_type=F32)
+    g_lowlevel = g_lowlevel * valid_fine_strip.astype(F32)
+    g_low = jnp.sum(tell_row(dot_nt(low_dz_all, low_in)), axis=0)
+    g_proj_acts = jnp.einsum("gop,gcp->oc", strips_dz, slope[1], preferred_element_type=F32)
+    g_proj_part = jnp.concatenate([g_proj_acts, g_proj_pool], axis=1).astype(BF)
+    g_proj = jnp.take(swap_ch(g_proj_part.reshape(devices, outs, 5 * outs)), order, axis=0)
+    g_w_proj = g_proj.reshape(devices, outs, 5, outs).transpose(1, 2, 0, 3).reshape(outs, -1).astype(F32)
+
+    if lined:
+        into, g_w_one, rest = assemble(gather_line(part), devices, groups, strip, outs, devices * depth)
+    else:
+        found = columns(lax.all_gather(part, "row", axis=0), (28 * outs,))
+        into, g_w_one = found[: 27 * outs], found[27 * outs :]
+        rest = lax.all_gather(shares, "row", axis=0)
+    g_w_atrous = into.reshape(3, 9, outs, devices * depth).transpose(0, 2, 1, 3)
+
+    rest = rest[:, : shares.shape[0]].astype(F32)
+    back = lambda v, shape: v.reshape(groups, -1)[:, : math.prod(shape) // groups].reshape(shape)
+    g_dec2 = back(rest[:, :share_rows], (9, outs, wide))
+    g_dec1 = jnp.concatenate(
+        [back(rest[:, share_rows:split_at], (9, outs, wide)), back(rest[:, split_at:], (9, outs, LOWC))], axis=2
+    )
     g_w_dec1 = jnp.concatenate([g_dec1[:, :, wide:], g_dec1[:, :, :wide]], axis=2).transpose(1, 0, 2)
     g_w_dec2 = g_dec2.transpose(1, 0, 2)
 

time: 733 us -> 696 us (0.950)
  waiting for transfers between devices: 170 us -> 156 us
  local copies, waits for them, and re-layouts: 73.6 us -> 61.9 us
  starting transfers between devices: 159 us -> 148 us
    all_gather x1 -> x3, waiting for transfers between devices: 0.01 us -> 50.2 us  [the longest x1 50.2 us: local(): canvas_dz = lax.all_gather(proj_dz, BOTH, axis=0)]
    psum x1 -> x0, waiting for transfers between devices: 40.1 us -> none  [local(): lax.psum((part_dec1, jnp.concatenate([part_dec2, g_low])), 'row')]
    ppermute x6 -> x3, waiting for transfers between devices: 36 us -> 3.96 us  [gather_blocks(): lax.ppermute(v, 'ch', [(i, i ^ m) for i in range(count)])]
    ppermute x6, waiting for transfers between devices: 33.8 us -> 13.1 us  [along(): lax.ppermute(v, 'row', [(2 * i + e, 2 * (i + step) + e) for i in places f...]
    ppermute x10, waiting for transfers between devices: 12.2 us -> 32.1 us  [beside(): lax.ppermute(v, 'row', [(2 * i + e, 2 * i + 1 - e) for i in places for e...]
    ppermute x16 -> x0, waiting for transfers between devices: 19.8 us -> none  [the longest x3 13.1 us: gather_all(): across = lambda v: lax.ppermute(v, 'ch', [(i, i ^ 2) for i in range(count)])]
    ppermute x16 -> x0, starting transfers between devices: 19.4 us -> none  [the longest x6 8.95 us: around(): return lax.ppermute(v, 'row', pairs)]
    all_to_all x0 -> x4, starting transfers between devices: none -> 18.1 us  [the longest x2 9.17 us: tell_row(): lax.all_to_all(jnp.broadcast_to(values[None], (count,) + values.shape), '...]
  transfers between devices with their start and end apart: 77 -> 62, of which waited for: 18 -> 20; matrix products, arithmetic and copies ran while one was open for 18% -> 15% of each run, Pallas kernels for 27% -> 34%
where the time goes in v2:
time: 696 us; the launch traced here: 684 us
  Pallas kernels  234 us (34%)
  waiting for transfers between devices  156 us (22%)
  starting transfers between devices  148 us (21%)
  local copies, waits for them, and re-layouts  61.9 us (9%)
  other arithmetic  46.1 us (7%)
  matrix products  20 us (3%)
  between operations  17.7 us (3%)
    pallas_call x5, Pallas kernels, decoder_call(): pl.pallas_call(kernel, grid=(pixels // lanes,), in_specs=in_specs, out_sp...  88.3 us
    all_to_all x7, starting transfers between devices, swap_all(): return lax.all_to_all(values, BOTH, 0, 0)  51.9 us
    all_gather x1, waiting for transfers between devices, local(): canvas_dz = lax.all_gather(proj_dz, BOTH, axis=0)  50.2 us
    ppermute x10, waiting for transfers between devices, beside(): lax.ppermute(v, 'row', [(2 * i + e, 2 * i + 1 - e) for i in places for e...  32.1 us
    pallas_call x2, Pallas kernels, decoder_weight_grad(): pl.pallas_call(lambda *refs: decoder_weight_kernel(lanes, outs, *refs), g...  24 us
    pallas_call x1, Pallas kernels, canvas_grad(): pl.pallas_call(lambda *refs: canvas_kernel(groups, devices, *refs), grid=...  23.5 us
    ppermute x7, starting transfers between devices, to_next(): return lax.ppermute(x, BOTH, [(i, i + 1) for i in range(count - 1)])  22.7 us
    pallas_call x1, Pallas kernels, pyramid(): pl.pallas_call(lambda *refs: pyramid_kernel(len(x_blocks), outs, *refs),...  18.1 us
  transfers between devices with their start and end apart: 62, of which 20 were waited for; matrix products, arithmetic and copies ran while one was open for 15% of the time, Pallas kernels for 34%

profile of v2, /device:TPU:0, one launch (start us, length us, event | category | flops | bytes accessed | tf_op | source)
XLA Modules:
  0.0 684.0 jit_solution(1549795745093969123)
XLA Ops:
  19.0 5.8 all-to-all-start
  25.3 6.8 all-to-all-done
  36.3 10.0 %shard_map.332 = (f32[8,8,1152]{2,1,0:T(8,128)}, f32[8,16,1152]{2,1,0:T(8,128)}, f32[8,1]{1,0:T(8,128)}, f32[32,1]{1,0:T(8,128)}, f32[32,1]{1,0:T(8,128)}, /*ind...) custom-call(s32[6]{0:T(128)} %refs_0_.1, ...), custom_call_target="tpu_custom_call" | custom-call | flops 20000000 | bytes 6000000 | tf_op jit(solution)/shard_map/pallas_call | solution.py:161
  60.0 18.1 %shard_map.333 = (f32[4,64,1152]{2,1,0:T(8,128)}, bf16[3,64,640]{2,1,0:T(8,128)(2,1)}, bf16[3,64,640]{2,1,0:T(8,128)(2,1)}) custom-call(s32[4]{0:T(128)} %pad_add_fusion.refs_0_, bf16[512,1152]{1,0:T(8,128)(2,1)} %broadcast_multiply_fusion.refs_1_, bf16[512,1152]{1,0:T(8,128)(2,1)} %copy-done.78, bf16[512,1152]{1,0:T(8,128)(2,1)} %collective-permute-done.1.refs_3_, ...), custom_call_target="tpu_custom_call" | custom-call | flops 8455716864 | bytes 12058624 | tf_op jit(solution)/shard_map/pallas_call | solution.py:860
  78.2 6.0 all-to-all-done.2
  124.7 8.7 %collective-permute-done.7 = bf16[256,288]{1,0:T(8,128)(2,1)S(1)} collective-permute-done((bf16[256,288]{1,0:T(8,128)(2,1)S(1)}, bf16[256,288]{1,0:T(8,128)(2,1)S(1)}, u32[]{:S(2)}, u32[]{:S(2)}) %collective-permute-start.7) | collective-permute-done | bytes 147488 | tf_op jit(solution)/shard_map/ppermute | solution.py:191
  153.0 5.2 collective-permute-start.10
  159.9 19.1 %shard_map.337 = (bf16[304,4864]{1,0:T(8,128)(2,1)}, f32[256,4608]{1,0:T(8,128)}, f32[256,128]{1,0:T(8,128)}, f32[256,128]{1,0:T(8,128)}, f32[32,8,128]{2,1,0:T(8,128)}) custom-call(f32[256,32]{1,0:T(8,128)} %copy-done.46, f32[256,288]{1,0:T(8,128)} %get-tuple-element.229.refs_1_, f32[256,32]{1,0:T(8,128)} %copy-done.47, f32[32,8,128]{2,1,0:T(8,128)} %copy-done.12, ...), custom_call_target="tpu_custom_call" | custom-call | flops 1 | bytes 1 | tf_op jit(solution)/shard_map/pallas_call | solution.py:695
  179.0 9.4 %all-to-all-start.5 = ((f32[32,8,128]{2,1,0:T(8,128)}), f32[32,8,128]{2,1,0:T(8,128)S(1)}, u32[]{:S(2)}, u32[]{:S(2)}) async-start(f32[32,8,128]{2,1,0:T(8,128)} %get-tuple-element.242), calls=%async_computation.6 | async-start | bytes 262144 | tf_op jit(solution)/shard_map/all_to_all | solution.py:237
  202.1 16.0 %shard_map.338 = (bf16[256,4864]{1,0:T(8,128)(2,1)}, f32[256,4608]{1,0:T(8,128)}, f32[256,128]{1,0:T(8,128)}, f32[256,128]{1,0:T(8,128)}, f32[32,8,128]{2,1,0:T(8,128)}) custom-call(f32[256,128]{1,0:T(8,128)} %copy-done.29, f32[256,4608]{1,0:T(8,128)} %get-tuple-element.246.refs_1_.refs_14_, f32[256,128]{1,0:T(8,128)} %copy-done.30, ...), custom_call_target="tpu_custom_call" | custom-call | flops 1 | bytes 1 | tf_op jit(solution)/shard_map/pallas_call | solution.py:695
  218.1 8.3 %all-to-all-start.6 = ((f32[32,8,128]{2,1,0:T(8,128)}), f32[32,8,128]{2,1,0:T(8,128)S(1)}, u32[]{:S(2)}, u32[]{:S(2)}) async-start(f32[32,8,128]{2,1,0:T(8,128)} %get-tuple-element.251), calls=%async_computation.7 | async-start | bytes 262144 | tf_op jit(solution)/shard_map/all_to_all | solution.py:237
  238.5 8.3 %shard_map.339 = (f32[21,4608]{1,0:T(8,128)}, f32[32,256]{1,0:T(8,128)}, f32[32,128]{1,0:T(8,128)}, f32[32,8,128]{2,1,0:T(8,128)}) custom-call(f32[256,4608]{1,0:T(8,128)} %get-tuple-element.250.pre.refs_1_, bf16[32,4608]{1,0:T(8,128)(2,1)} %pad.71.cotangent.refs_8_, f32[1,4608]{1,0:T(1,128)} %get-tuple-element.371.valid, f32[32,8,128]{2,1,0:T(8,128)} %copy-done.17, ...), custom_call_target="tpu_custom_call" | custom-call | flops 1 | bytes 1 | tf_op jit(solution)/shard_map/pallas_call | solution.py:695
  246.9 11.7 %all-to-all-start.7 = ((f32[32,8,128]{2,1,0:T(8,128)}), f32[32,8,128]{2,1,0:T(8,128)S(1)}, u32[]{:S(2)}, u32[]{:S(2)}) async-start(f32[32,8,128]{2,1,0:T(8,128)} %get-tuple-element.261), calls=%async_computation.8 | async-start | bytes 262144 | tf_op jit(solution)/shard_map/all_to_all | solution.py:237
  260.9 8.4 %all-to-all-done.7.refs_6_ = f32[32,8,128]{2,1,0:T(8,128)S(1)} async-done(((f32[32,8,128]{2,1,0:T(8,128)}), f32[32,8,128]{2,1,0:T(8,128)S(1)}, u32[]{:S(2)}, u32[]{:S(2)}) %all-to-all-start.7) | async-done | bytes 131104 | tf_op jit(solution)/shard_map/all_to_all | solution.py:237
  270.0 19.4 %shard_map.340 = (bf16[256,4864]{1,0:T(8,128)(2,1)}, f32[256,4608]{1,0:T(8,128)}, f32[256,128]{1,0:T(8,128)}, f32[256,128]{1,0:T(8,128)}, f32[32,16,128]{2,1,0:T(8,128)}) custom-call(f32[256,128]{1,0:T(8,128)} %copy-done.44, f32[256,4608]{1,0:T(8,128)} %get-tuple-element.250.pre.refs_1_, f32[256,128]{1,0:T(8,128)} %copy-done.45, f32[32,8,128]{2,1,0:T(8,128)} %copy-done.17, ...), custom_call_target="tpu_custom_call" | custom-call | flops 1 | bytes 1 | tf_op jit(solution)/shard_map/pallas_call | solution.py:695
  296.8 10.8 %shard_map.341 = bf16[4,9,64,256]{3,2,1,0:T(8,128)(2,1)} custom-call(bf16[256,4864]{1,0:T(8,128)(2,1)} %get-tuple-element.271.refs_0_, bf16[256,4864]{1,0:T(8,128)(2,1)} %get-tuple-element.272.refs_1_, f32[2,4608]{1,0:T(2,128)} %get-tuple-element.240.refs_15_.refs_7_.refs_12_.refs_2_.refs_11_), custom_call_target="tpu_custom_call" | custom-call | flops 1 | bytes 1 | tf_op jit(solution)/shard_map/pallas_call | solution.py:674
  308.4 25.3 %shard_map.342 = (bf16[256,4864]{1,0:T(8,128)(2,1)}, f32[256,352]{1,0:T(8,128)}, f32[48,4608]{1,0:T(8,128)}, f32[2,256]{1,0:T(2,128)}) custom-call(f32[256,128]{1,0:T(8,128)} %copy-done.29, f32[256,4608]{1,0:T(8,128)} %get-tuple-element.246.refs_1_.refs_14_, f32[256,128]{1,0:T(8,128)} %copy-done.30, f32[256,128]{1,0:T(8,128)} %copy-done.48, ...), custom_call_target="tpu_custom_call" | custom-call | flops 1 | bytes 1 | tf_op jit(solution)/shard_map/pallas_call | solution.py:695
  348.2 11.4 %all-to-all-start.9 = ((f32[32,16,128]{2,1,0:T(8,128)}), f32[32,16,128]{2,1,0:T(8,128)S(1)}, u32[]{:S(2)}, u32[]{:S(2)}) async-start(f32[32,16,128]{2,1,0:T(8,128)} %broadcast_in_dim.36), calls=%async_computation.10 | async-start | bytes 524288 | tf_op jit(solution)/shard_map/all_to_all | solution.py:237
  359.7 13.2 %shard_map.343 = bf16[4,9,64,304]{3,2,1,0:T(8,128)(2,1)} custom-call(bf16[256,4864]{1,0:T(8,128)(2,1)} %get-tuple-element.276.refs_0_, bf16[304,4864]{1,0:T(8,128)(2,1)} %get-tuple-element.277.refs_1_, f32[2,4608]{1,0:T(2,128)} %get-tuple-element.240.refs_15_.refs_7_.refs_12_.refs_2_.refs_11_), custom_call_target="tpu_custom_call" | custom-call | flops 1 | bytes 1 | tf_op jit(solution)/shard_map/pallas_call | solution.py:674
  383.9 11.0 %shard_map.344 = (bf16[8,256,1152]{2,1,0:T(8,128)(2,1)}, bf16[8,256,1152]{2,1,0:T(8,128)(2,1)}) custom-call(bf16[8,256,1152]{2,1,0:T(8,128)(2,1)} %bitcast.201, f32[8,8,1152]{2,1,0:T(8,128)} %get-tuple-element.280.refs_1_.refs_6_, f32[256,4]{1,0:T(8,128)} %copy.120.refs_2_.refs_9_, f32[256,8]{1,0:T(8,128)} %get-tuple-element.356.refs_3_.refs_10_), custom_call_target="tpu_custom_call" | custom-call | flops 1 | bytes 1 | tf_op jit(solution)/shard_map/pallas_call | solution.py:1028
  394.8 50.2 %all-gather.20.cloned.1.call-done = bf16[8192,288]{1,0:T(8,128)(2,1)} async-done(((bf16[256,288]{1,0:T(8,128)(2,1)}), bf16[8192,288]{1,0:T(8,128)(2,1)}) %all-gather.20.cloned.1.call-update) | async-done | bytes 4718608 | tf_op jit(solution)/shard_map/all_gather | solution.py:1479
  445.0 23.5 %shard_map.345 = (bf16[256,10496]{1,0:T(8,128)(2,1)}, bf16[8,256,1152]{2,1,0:T(8,128)(2,1)}, f32[256,128]{1,0:T(8,128)}, f32[256,16]{1,0:T(8,128)}) custom-call(bf16[32,256,288]{2,1,0:T(8,128)(2,1)} %bitcast.197, bf16[32,256,288]{2,1,0:T(8,128)(2,1)} %bitcast.198, bf16[32,256,288]{2,1,0:T(8,128)(2,1)} %bitcast.199, bf16[32,256,288]{2,1,0:T(8,128)(2,1)} %bitcast.200, ...), custom_call_target="tpu_custom_call" | custom-call | flops 1207959552 | bytes 18874368 | tf_op jit(solution)/shard_map/pallas_call | solution.py:1096
  468.6 14.5 %reduce-scatter.6.cloned.1.call-done = bf16[1,9,64,560]{3,2,1,0:T(8,128)(2,1)} async-done(((bf16[4,9,64,560]{3,2,1,0:T(8,128)(2,1)}), bf16[1,9,64,560]{3,2,1,0:T(8,128)(2,1)}) %reduce-scatter.6.cloned.1.call-update) | async-done | bytes 645136 | tf_op jit(solution)/shard_map/reduce_scatter | solution.py:1471
  486.1 5.5 all-to-all-start.10
  492.8 16.6 %shard_map.346 = bf16[1984,256]{1,0:T(8,128)(2,1)} custom-call(bf16[256,10496]{1,0:T(8,128)(2,1)} %get-tuple-element.295.refs_0_, f32[8,8,1152]{2,1,0:T(8,128)} %get-tuple-element.280.refs_1_.refs_6_, bf16[4,8,64,1152]{3,2,1,0:T(8,128)(2,1)} %bitcast.266, bf16[4,8,64,1152]{3,2,1,0:T(8,128)(2,1)} %bitcast.267, bf16[4,8,64,1152]{3,2,1,0:T(8,128)(2,1)} %bitcast.268, ...), custom_call_target="tpu_custom_call" | custom-call | flops 8455716864 | bytes 9437184 | tf_op jit(solution)/shard_map/pallas_call | solution.py:990
  517.3 16.6 %shard_map.347 = bf16[4,512,1152]{2,1,0:T(8,128)(2,1)} custom-call(s32[4]{0:T(128)} %iota.11.perm_ref, bf16[256,2432]{1,0:T(8,128)(2,1)} %constant_dynamic-slice_fusion.2.refs_0_, bf16[64,1152]{1,0:T(8,128)(2,1)} %convolution_convert_fusion.1.refs_1_, f32[8,1152]{1,0:T(8,128)} %get-tuple-element.188.refs_7_.refs_2_, bf16[1728,2048]{1,0:T(8,128)(2,1)} %bitcast.265, ...), custom_call_target="tpu_custom_call" | custom-call | flops 8757706752 | bytes 12320768 | tf_op jit(solution)/shard_map/pallas_call | solution.py:936
  547.9 10.1 %collective-permute-done.24.refs_8_.refs_25_.refs_42_ = bf16[1984,256]{1,0:T(8,128)(2,1)S(1)} collective-permute-done((bf16[1984,256]{1,0:T(8,128)(2,1)}, bf16[1984,256]{1,0:T(8,128)(2,1)S(1)}, u32[]{:S(2)}, u32[]{:S(2)}) %collective-permute-start.24) | collective-permute-done | bytes 1015840 | tf_op jit(solution)/shard_map/ppermute | solution.py:210
  576.3 13.5 %collective-permute-done.28.refs_10_.refs_27_.refs_44_ = bf16[1984,256]{1,0:T(8,128)(2,1)} collective-permute-done((bf16[1984,256]{1,0:T(8,128)(2,1)S(1)}, bf16[1984,256]{1,0:T(8,128)(2,1)}, u32[]{:S(2)}, u32[]{:S(2)}) %collective-permute-start.28) | collective-permute-done | bytes 1015840 | tf_op jit(solution)/shard_map/ppermute | solution.py:210
  589.8 5.4 collective-permute-done.26.refs_12_.refs_29_.refs_46_
  605.5 5.2 fusion.7
  615.3 8.5 %collective-permute-done.33.refs_13_.refs_30_.refs_47_ = bf16[1984,256]{1,0:T(8,128)(2,1)} collective-permute-done((bf16[1984,256]{1,0:T(8,128)(2,1)}, bf16[1984,256]{1,0:T(8,128)(2,1)}, u32[]{:S(2)}, u32[]{:S(2)}) %collective-permute-start.33) | collective-permute-done | bytes 1015840 | tf_op jit(solution)/shard_map/ppermute | solution.py:210
  657.5 13.3 %shard_map.348 = (f32[1728,2048]{1,0:T(8,128)}, f32[64,2048]{1,0:T(8,128)}, bf16[8,192,256]{2,1,0:T(8,128)(2,1)}) custom-call(s32[1]{0:T(128)} %bitcast.4.where_ref, bf16[1984,256]{1,0:T(8,128)(2,1)} %collective-permute-done.29.refs_0_.refs_17_.refs_34_, bf16[1984,256]{1,0:T(8,128)(2,1)} %copy-done.5, ...), custom_call_target="tpu_custom_call" | custom-call | bytes 21233664 | tf_op jit(solution)/shard_map/pallas_call | solution.py:1155
  (476 shorter events, 250.2 us)
Async XLA Ops:
  13.7 32.7 %collective-permute-start.1 = (bf16[512,1152]{1,0:T(8,128)(2,1)}, bf16[512,1152]{1,0:T(8,128)(2,1)}, u32[]{:S(2)}, u32[]{:S(2)}) collective-permute-start(bf16[512,1152]{1,0:T(8,128)(2,1)} %broadcast_multiply_fusion.refs_1_), channel_id=1, source_target_pairs={{0,2},{1,3},{2,0},{3,1},{4,6},{5,7},{6,4},{7,5},{8,10},{9,11},{10,... | collective-permute-start | bytes 3538952 | tf_op jit(solution)/shard_map/ppermute | solution.py:174
  36.3 57.5 %all-gather.14.cloned.1.call-start = ((), (), s32[]{:S(2)}) async-start(), calls=%async_computation.19 | async-start | bytes 3604480 | tf_op jit(solution)/shard_map/all_gather | solution.py:1273
  47.7 67.9 %reduce-scatter.4.cloned.1.call-start = ((), (), s32[]{:S(2)}) async-start(), calls=%async_computation.15 | async-start | bytes 2211840 | tf_op jit(solution)/shard_map/reduce_scatter | solution.py:1280
  49.9 109.4 %all-gather.16.cloned.1.call-start = ((), (), s32[]{:S(2)}) async-start(), calls=%async_computation.20 | async-start | bytes 2211840 | tf_op jit(solution)/shard_map/all_gather | solution.py:1282
  51.0 33.2 %all-to-all-start.2 = ((bf16[8,64,1152]{2,1,0:T(8,128)(2,1)}), bf16[8,64,1152]{2,1,0:T(8,128)(2,1)S(1)}, u32[]{:S(2)}, u32[]{:S(2)}) async-start(bf16[8,64,1152]{2,1,0:T(8,128)(2,1)} %bitcast.8), calls=%async_computation.2 | async-start | bytes 2359296 | tf_op jit(solution)/shard_map/all_to_all | solution.py:1268
  54.8 183.1 %all-gather.18.cloned.1.call-start = ((), (), s32[]{:S(2)}) async-start(), calls=%async_computation.21 | async-start | bytes 5898240 | tf_op jit(solution)/shard_map/all_gather | solution.py:1297
  85.2 298.6 %all-gather.22.cloned.1.call-start = ((), (), s32[]{:S(2)}) async-start(), calls=%async_computation.23 | async-start | bytes 5308416 | tf_op jit(solution)/shard_map/all_gather | solution.py:1352
  85.9 18.2 %collective-permute-start.3 = (bf16[3,64,640]{2,1,0:T(8,128)(2,1)}, bf16[3,64,640]{2,1,0:T(8,128)(2,1)S(1)}, u32[]{:S(2)}, u32[]{:S(2)}) collective-permute-start(bf16[3,64,640]{2,1,0:T(8,128)(2,1)} %get-tuple-element.206), channel_id=1, source_target_pairs={{4,0},{8,4},{12,8},{16,12},{20,16},{24,20},{28,24},{5,1},{9,5},{13... | collective-permute-start | bytes 737288 | tf_op jit(solution)/shard_map/ppermute | solution.py:1300
  118.2 20.7 %all-to-all-start.3 = ((f32[32,8,128]{2,1,0:T(8,128)}), f32[32,8,128]{2,1,0:T(8,128)S(1)}, u32[]{:S(2)}, u32[]{:S(2)}) async-start(f32[32,8,128]{2,1,0:T(8,128)} %get-tuple-element.216), calls=%async_computation.3 | async-start | bytes 262144 | tf_op jit(solution)/shard_map/all_to_all | solution.py:237
  179.0 22.3 %all-to-all-start.5 = ((f32[32,8,128]{2,1,0:T(8,128)}), f32[32,8,128]{2,1,0:T(8,128)S(1)}, u32[]{:S(2)}, u32[]{:S(2)}) async-start(f32[32,8,128]{2,1,0:T(8,128)} %get-tuple-element.242), calls=%async_computation.6 | async-start | bytes 262144 | tf_op jit(solution)/shard_map/all_to_all | solution.py:237
  192.0 69.0 %collective-permute-start.17 = (bf16[32,128]{1,0:T(8,128)(2,1)S(1)}, bf16[32,128]{1,0:T(8,128)(2,1)S(1)}, u32[]{:S(2)}, u32[]{:S(2)}) collective-permute-start(bf16[32,128]{1,0:T(8,128)(2,1)S(1)} %get-tuple-element.362), channel_id=1, source_target_pairs={{1,0},{2,1},{3,2},{4,3},{5,4},{6,5},{7,6},{8,7},{9,8},{10,9},{11,1... | collective-permute-start | bytes 24584 | tf_op jit(solution)/shard_map/ppermute | solution.py:267
  193.3 67.7 %collective-permute-start.16 = (bf16[32,128]{1,0:T(8,128)(2,1)S(1)}, bf16[32,128]{1,0:T(8,128)(2,1)S(1)}, u32[]{:S(2)}, u32[]{:S(2)}) collective-permute-start(bf16[32,128]{1,0:T(8,128)(2,1)S(1)} %get-tuple-element.363), channel_id=1, source_target_pairs={{0,1},{1,2},{2,3},{3,4},{4,5},{5,6},{6,7},{7,8},{8,9},{9,10},{10,1... | collective-permute-start | bytes 24584 | tf_op jit(solution)/shard_map/ppermute | solution.py:262
  218.1 19.8 %all-to-all-start.6 = ((f32[32,8,128]{2,1,0:T(8,128)}), f32[32,8,128]{2,1,0:T(8,128)S(1)}, u32[]{:S(2)}, u32[]{:S(2)}) async-start(f32[32,8,128]{2,1,0:T(8,128)} %get-tuple-element.251), calls=%async_computation.7 | async-start | bytes 262144 | tf_op jit(solution)/shard_map/all_to_all | solution.py:237
  246.9 22.4 %all-to-all-start.7 = ((f32[32,8,128]{2,1,0:T(8,128)}), f32[32,8,128]{2,1,0:T(8,128)S(1)}, u32[]{:S(2)}, u32[]{:S(2)}) async-start(f32[32,8,128]{2,1,0:T(8,128)} %get-tuple-element.261), calls=%async_computation.8 | async-start | bytes 262144 | tf_op jit(solution)/shard_map/all_to_all | solution.py:237
  289.4 18.2 %all-to-all-start.8 = ((f32[32,16,128]{2,1,0:T(8,128)}), f32[32,16,128]{2,1,0:T(8,128)S(1)}, u32[]{:S(2)}, u32[]{:S(2)}) async-start(f32[32,16,128]{2,1,0:T(8,128)} %get-tuple-element.264), calls=%async_computation.9 | async-start | bytes 524288 | tf_op jit(solution)/shard_map/all_to_all | solution.py:237
  348.2 24.7 %all-to-all-start.9 = ((f32[32,16,128]{2,1,0:T(8,128)}), f32[32,16,128]{2,1,0:T(8,128)S(1)}, u32[]{:S(2)}, u32[]{:S(2)}) async-start(f32[32,16,128]{2,1,0:T(8,128)} %broadcast_in_dim.36), calls=%async_computation.10 | async-start | bytes 524288 | tf_op jit(solution)/shard_map/all_to_all | solution.py:237
  359.7 85.4 %all-gather.20.cloned.1.call-start = ((), (), s32[]{:S(2)}) async-start(), calls=%async_computation.22 | async-start | bytes 6488064 | tf_op jit(solution)/shard_map/all_gather | solution.py:1479
  374.0 109.1 %reduce-scatter.6.cloned.1.call-start = ((), (), s32[]{:S(2)}) async-start(), calls=%async_computation.16 | async-start | bytes 3686400 | tf_op jit(solution)/shard_map/reduce_scatter | solution.py:1471
  486.1 23.3 %all-to-all-start.10 = ((bf16[8,158,256]{2,1,0:T(8,128)(2,1)}), bf16[8,158,256]{2,1,0:T(8,128)(2,1)S(1)}, u32[]{:S(2)}, u32[]{:S(2)}) async-start(bf16[8,158,256]{2,1,0:T(8,128)(2,1)} %pad_maximum_fusion.3), calls=%async_computation.12 | async-start | bytes 1310720 | tf_op jit(solution)/shard_map/all_to_all | solution.py:1499
  491.6 147.9 %all-gather.12.cloned.1.call-start = ((), (), s32[]{:S(2)}) async-start(), calls=%async_computation.18 | async-start | bytes 2211840 | tf_op jit(solution)/shard_map/all_gather | solution.py:1540
  512.5 161.9 %reduce-scatter.8.cloned.1.call-start = ((), (), s32[]{:S(2)}) async-start(), calls=%async_computation.17 | async-start | bytes 5898240 | tf_op jit(solution)/shard_map/reduce_scatter | solution.py:1539
  534.0 24.1 %collective-permute-start.24 = (bf16[1984,256]{1,0:T(8,128)(2,1)}, bf16[1984,256]{1,0:T(8,128)(2,1)S(1)}, u32[]{:S(2)}, u32[]{:S(2)}) collective-permute-start(bf16[1984,256]{1,0:T(8,128)(2,1)} %scatter.4.refs_7_.refs_24_.refs_41_), channel_id=1, source_target_pairs={{0,4},{4,0},{8,12},{12,8},{16,20},{20,16},{24,28},{28,24},{1,5},{5... | collective-permute-start | bytes 3047432 | tf_op jit(solution)/shard_map/ppermute | solution.py:210
  536.0 25.3 %collective-permute-start.23 = (bf16[1984,256]{1,0:T(8,128)(2,1)}, bf16[1984,256]{1,0:T(8,128)(2,1)S(1)}, u32[]{:S(2)}, u32[]{:S(2)}) collective-permute-start(bf16[1984,256]{1,0:T(8,128)(2,1)} %scatter.4.refs_7_.refs_24_.refs_41_), channel_id=1, source_target_pairs={{8,0},{12,4},{16,8},{20,12},{24,16},{28,20},{9,1},{13,5},{17,9},{2... | collective-permute-start | bytes 3047432 | tf_op jit(solution)/shard_map/ppermute | solution.py:207
  537.3 25.3 %collective-permute-start.22 = (bf16[1984,256]{1,0:T(8,128)(2,1)}, bf16[1984,256]{1,0:T(8,128)(2,1)S(1)}, u32[]{:S(2)}, u32[]{:S(2)}) collective-permute-start(bf16[1984,256]{1,0:T(8,128)(2,1)} %scatter.4.refs_7_.refs_24_.refs_41_), channel_id=1, source_target_pairs={{0,8},{4,12},{8,16},{12,20},{16,24},{20,28},{1,9},{5,13},{9,17},{1... | collective-permute-start | bytes 3047432 | tf_op jit(solution)/shard_map/ppermute | solution.py:207
  565.8 24.0 %collective-permute-start.28 = (bf16[1984,256]{1,0:T(8,128)(2,1)S(1)}, bf16[1984,256]{1,0:T(8,128)(2,1)}, u32[]{:S(2)}, u32[]{:S(2)}) collective-permute-start(bf16[1984,256]{1,0:T(8,128)(2,1)S(1)} %collective-permute-done.23.refs_9_.refs_26_.refs_43_), channel_id=1, source_target_pairs={{0,4},{4,0},{1,5},{5,1},{2,6},{6,2},{3,7},{7,3}} | collective-permute-start | bytes 3047432 | tf_op jit(solution)/shard_map/ppermute | solution.py:210
  568.1 27.2 %collective-permute-start.26 = (bf16[1984,256]{1,0:T(8,128)(2,1)S(1)}, bf16[1984,256]{1,0:T(8,128)(2,1)}, u32[]{:S(2)}, u32[]{:S(2)}) collective-permute-start(bf16[1984,256]{1,0:T(8,128)(2,1)S(1)} %collective-permute-done.23.refs_9_.refs_26_.refs_43_), channel_id=1, source_target_pairs={{8,0},{12,4},{16,8},{20,12},{9,1},{13,5},{17,9},{21,13},{10,2},{14... | collective-permute-start | bytes 3047432 | tf_op jit(solution)/shard_map/ppermute | solution.py:207
  600.5 23.3 %collective-permute-start.33 = (bf16[1984,256]{1,0:T(8,128)(2,1)}, bf16[1984,256]{1,0:T(8,128)(2,1)}, u32[]{:S(2)}, u32[]{:S(2)}) collective-permute-start(bf16[1984,256]{1,0:T(8,128)(2,1)} %collective-permute-done.26.refs_12_.refs_29_.refs_46_), channel_id=1, source_target_pairs={{0,4},{4,0},{1,5},{5,1},{2,6},{6,2},{3,7},{7,3}} | collective-permute-start | bytes 3047432 | tf_op jit(solution)/shard_map/ppermute | solution.py:210
  604.0 22.9 %collective-permute-start.30 = (bf16[1984,256]{1,0:T(8,128)(2,1)}, bf16[1984,256]{1,0:T(8,128)(2,1)}, u32[]{:S(2)}, u32[]{:S(2)}) collective-permute-start(bf16[1984,256]{1,0:T(8,128)(2,1)} %collective-permute-done.26.refs_12_.refs_29_.refs_46_), channel_id=1, source_target_pairs={{8,0},{12,4},{9,1},{13,5},{10,2},{14,6},{11,3},{15,7}} | collective-permute-start | bytes 3047432 | tf_op jit(solution)/shard_map/ppermute | solution.py:207
  626.9 28.9 %collective-permute-start.34 = (bf16[1984,256]{1,0:T(8,128)(2,1)}, bf16[1984,256]{1,0:T(8,128)(2,1)S(1)}, u32[]{:S(2)}, u32[]{:S(2)}) collective-permute-start(bf16[1984,256]{1,0:T(8,128)(2,1)} %collective-permute-done.29.refs_0_.refs_17_.refs_34_), channel_id=1, source_target_pairs={{24,28},{28,24},{25,29},{29,25},{26,30},{30,26},{27,31},{31,27}} | collective-permute-start | bytes 3047432 | tf_op jit(solution)/shard_map/ppermute | solution.py:210
  627.6 28.2 %collective-permute-start.35 = (bf16[1984,256]{1,0:T(8,128)(2,1)}, bf16[1984,256]{1,0:T(8,128)(2,1)S(1)}, u32[]{:S(2)}, u32[]{:S(2)}) collective-permute-start(bf16[1984,256]{1,0:T(8,128)(2,1)} %collective-permute-done.25.refs_2_.refs_19_.refs_36_), channel_id=1, source_target_pairs={{16,20},{20,16},{17,21},{21,17},{18,22},{22,18},{19,23},{23,19}} | collective-permute-start | bytes 3047432 | tf_op jit(solution)/shard_map/ppermute | solution.py:210
  628.4 27.5 %collective-permute-start.36 = (bf16[1984,256]{1,0:T(8,128)(2,1)}, bf16[1984,256]{1,0:T(8,128)(2,1)S(1)}, u32[]{:S(2)}, u32[]{:S(2)}) collective-permute-start(bf16[1984,256]{1,0:T(8,128)(2,1)} %collective-permute-done.26.refs_12_.refs_29_.refs_46_), channel_id=1, source_target_pairs={{8,12},{12,8},{9,13},{13,9},{10,14},{14,10},{11,15},{15,11}} | collective-permute-start | bytes 3047432 | tf_op jit(solution)/shard_map/ppermute | solution.py:210
  629.1 26.8 %collective-permute-start.37 = (bf16[1984,256]{1,0:T(8,128)(2,1)}, bf16[1984,256]{1,0:T(8,128)(2,1)}, u32[]{:S(2)}, u32[]{:S(2)}) collective-permute-start(bf16[1984,256]{1,0:T(8,128)(2,1)} %collective-permute-done.30.refs_15_.refs_32_.refs_49_), channel_id=1, source_target_pairs={{0,4},{4,0},{1,5},{5,1},{2,6},{6,2},{3,7},{7,3}} | collective-permute-start | bytes 3047432 | tf_op jit(solution)/shard_map/ppermute | solution.py:210
  (114 other events, 1959.9 us)
Sparse Core Ops, SparseCore 0:
  47.9 25.9 all-gather.13
  77.0 29.3 reduce-scatter.3
  108.7 25.0 all-gather.15
  135.3 40.6 all-gather.17
  178.8 91.0 all-gather.21
  374.1 70.8 all-gather.19
  447.7 35.2 reduce-scatter.5
  512.6 21.2 all-gather.11
  536.4 47.8 reduce-scatter.7

commit v3 on v2

--- a/solution.py
+++ b/solution.py
@@ -202,7 +202,7 @@
     return lax.psum_scatter(jnp.stack(blocks), "ch", scatter_dimension=0).astype(F32)
 
 
-def gather_line(x):
+def gather_line(x, later, finish):
     def along(v, places, step):
         return lax.ppermute(v, "row", [(2 * i + e, 2 * (i + step) + e) for i in places for e in range(2)])
 
@@ -216,6 +216,8 @@
     got[-1, 0, 0], got[1, 0, 0] = along(x, (0, 1, 2), 1), along(x, (1, 2, 3), -1)
     got[0, 1, 0] = beside(x, (0, 1, 2, 3))
     together((-1, 0, 0), (1, 0, 0), (0, 1, 0))
+    got[0, 1, 0], later = lax.optimization_barrier((got[0, 1, 0], later))
+    finished = finish(*later)
     got[-2, 0, 0], got[2, 0, 0] = along(got[-1, 0, 0], (1, 2), 1), along(got[1, 0, 0], (1, 2), -1)
     got[-1, 1, 0], got[1, 1, 0] = beside(got[-1, 0, 0], (1, 2, 3)), beside(got[1, 0, 0], (0,))
     together((-2, 0, 0), (2, 0, 0), (-1, 1, 0), (1, 1, 0), (1, 0, 0))
@@ -225,7 +227,8 @@
     together((-3, 0, 0), (3, 0, 0), (1, 1, 1), (-2, 1, 0), (2, 1, 0), (-2, 0, 0), (2, 0, 0))
     got[-2, 1, 1], got[2, 1, 1] = beside(got[-2, 0, 0], (2,)), beside(got[2, 0, 0], (1,))
     got[-3, 1, 0], got[3, 1, 0] = beside(got[-3, 0, 0], (3,)), beside(got[3, 0, 0], (0,))
-    return got
+    got[-3, 1, 0], finished = lax.optimization_barrier((got[-3, 1, 0], finished))
+    return got, finished
 
 
 def line_part(place, steps, side):
@@ -265,13 +268,6 @@
 def to_previous(x):
     count = lax.axis_size("row") * lax.axis_size("ch")
     return lax.ppermute(x, BOTH, [(i + 1, i) for i in range(count - 1)])
-
-
-def local_moments(x, valid):
-    count = jnp.sum(valid)
-    mean = jnp.sum(x * valid[None], axis=1) / jnp.maximum(count, 1.0)
-    centered = (x - mean[:, None]) * valid[None]
-    return mean, jnp.sum(centered * centered, axis=1)
 
 
 def merge_moments(means, spreads, counts, total):
@@ -768,7 +764,7 @@
 
 
 def project_kernel(
-    swapped, told, counts, gains, w_ref, broad, member, valid, low_stats, scalars, places, out_ref, left_ref, right_ref, stats_ref
+    swapped, told, counts, gains, w_ref, broad, member, valid, low_ref, valid_fine, scalars, places, out_ref, left_ref, right_ref, stats_ref
 ):
     devices, four, share = swapped.shape
     groups = told.shape[0]
@@ -791,7 +787,13 @@
     count = jnp.maximum(jnp.sum(valid[...]), 1.0)
     mean = jnp.sum(total * valid[...], axis=1, keepdims=True) / count
     away = (total - mean) * valid[...]
-    pack_vectors(stats_ref, *as_rows([mean, jnp.sum(away * away, axis=1, keepdims=True)]), low_stats[...])
+    rows = as_rows([mean, jnp.sum(away * away, axis=1, keepdims=True)])
+    low_count = jnp.maximum(jnp.sum(valid_fine[...]), 1.0)
+    low_mean = jnp.sum(low_ref[...] * valid_fine[...], axis=1, keepdims=True) / low_count
+    away = (low_ref[...] - low_mean) * valid_fine[...]
+    low_rows = as_rows([low_mean, jnp.sum(away * away, axis=1, keepdims=True)])
+    more = [part for row in low_rows for part in (row[:, :128], row[:, 128:])]
+    pack_vectors(stats_ref, *rows, jnp.concatenate(more, axis=0))
 
 
 def small_call(kernel, operands, smem, outputs, flops):
@@ -944,7 +946,7 @@
         ),
         out_shape=jax.ShapeDtypeStruct((blocks, depth, pixels), BF),
         compiler_params=params(),
-        cost_estimate=pl.CostEstimate(flops=2 * 29 * outs * cin * pixels, bytes_accessed=2 * (29 * outs + pixels) * cin, transcendentals=0),
+        cost_estimate=BRIEF,
     )(perm, dz, spread, masks, w_taps.reshape(27 * outs, cin), w_one, w_pool)
 
 
@@ -1302,7 +1304,6 @@
 
     member_mine, valid_mine = mine_rows[:images], mine_rows[members : members + 1]
     valid_fine = valid_wide[:, WF:-WF]
-    low_stats = vector_tile(*local_moments(low_pre, valid_fine[0]))[:4]
 
     order = jnp.argsort(perm)
 
@@ -1333,9 +1334,9 @@
         project_kernel,
         [
             swapped, told_branch.reshape(groups, devices, 8, 128), strip_counts, branch_gains, wp_acts, broad_part, member_mine,
-            valid_mine, low_stats, scalars, jnp.concatenate([strip[None].astype(jnp.int32), perm]),
+            valid_mine, low_pre, valid_fine, scalars, jnp.concatenate([strip[None].astype(jnp.int32), perm]),
         ],
-        (9, 10),
+        (10, 11),
         [
             jax.ShapeDtypeStruct((wide, share), F32),
             jax.ShapeDtypeStruct((wide, margin), F32),
@@ -1346,8 +1347,8 @@
     )
     proj_prev, proj_next = to_next(proj_right), to_previous(proj_left)
     low_prev, low_next = to_next(low_pre[:, -WF:]), to_previous(low_pre[:, :WF])
-    told_proj, proj_prev, proj_next, low_prev, low_next = lax.optimization_barrier(
-        (swap_all(stats), proj_prev, proj_next, low_prev, low_next)
+    told_proj, proj_prev, proj_next, low_prev, low_next, cotangent, w_cls, b_cls = lax.optimization_barrier(
+        (swap_all(stats), proj_prev, proj_next, low_prev, low_next, cotangent, w_cls, b_cls)
     )
     canvas_centered = lax.all_gather(centered, "row", axis=0)
     own_told = lax.dynamic_index_in_dim(told_branch.reshape(groups, devices, 8 * 128), me, 1, False)
@@ -1468,7 +1469,9 @@
     both = vector_tile(jnp.sum(dy, axis=1), jnp.sum(dy * proj_normed, axis=1), low_part_sums[0], low_part_sums[1])
     both = jnp.concatenate([both, jnp.pad(class_share, ((0, 8 - class_rows), (0, 0)))])
     told_both, g_dec1 = lax.optimization_barrier((tell_all(both), g_dec1))
-    part_dec = lax.psum_scatter(jnp.concatenate([g_dec2, g_dec1], axis=3), "ch", scatter_dimension=0)
+    decs = jnp.concatenate([g_dec2, g_dec1], axis=3)
+    pick = lambda i: lax.dynamic_index_in_dim(decs, i, 0, False)
+    part_dec = reduce_blocks([pick(i) for i in origin]).astype(BF)
     both = jnp.sum(told_both[:, :8], axis=0).reshape(4, 256)
     class_sums = told_both[:, 8 : 8 + class_rows].reshape(-1)
     bias_sums = class_sums[classes * wide : classes * wide + classes]
@@ -1478,7 +1481,7 @@
     proj_dz = norm_back(dy, proj_normed, proj_scale, proj_gain[0], proj_sums, valid_mine, count).astype(BF)
     canvas_dz = lax.all_gather(proj_dz, BOTH, axis=0)
     slope = slopes(0, groups, canvas_centered, canvas_rows, cols, offsets)
-    canvas_dz, *slope = lax.optimization_barrier((canvas_dz, *slope))
+    canvas_dz, part_dec, *slope = lax.optimization_barrier((canvas_dz, part_dec, *slope))
 
     wp_own = lax.dynamic_index_in_dim(wp_acts, me, 0, False)
     wp_pool_own = lax.dynamic_slice_in_dim(wp_pool, me * outs, outs, axis=1)
@@ -1488,7 +1491,6 @@
     branch_sums = branch_sums[:, :2].T
     image_dz = image_dz[:, :images]
 
-    padded_dz, part_dec = lax.optimization_barrier((padded_dz, part_dec))
 
     def by_row(v):
         v = v.reshape(groups, -1)
@@ -1503,55 +1505,59 @@
     part = pyramid_weight_grad(padded_dz, x_canvas, canvas_rows, (0, 1, 2), True, 3 * outs if lined else 0)
     if lined:
         part = part.at[27 * outs : 27 * outs + shares.shape[0]].set(shares)
-    part, padded_dz, first_told, image_dz, strips_dz, dy_low = lax.optimization_barrier(
-        (part, padded_dz, first_told, image_dz, strips_dz, dy_low)
-    )
-
-    low_mean, low_scale = merge_moments(proj_told[:, 512 : 512 + LOWC], proj_told[:, 768 : 768 + LOWC], counts_f[:, 0], fine_count)
-    low_normed = (low_pre - low_mean[:, None]) * low_scale[:, None]
-    low_dz = norm_back(dy_low, low_normed, low_scale, low_gains[0, :LOWC], low_sums, valid_fine, fine_count).astype(BF)
-
-    pool_sums = first_told[:, :images, :depth].transpose(0, 2, 1).reshape(devices * depth, images)
-    pooled = (pool_sums / area[None]).astype(BF)
-    pool_pre = dot(w_pool, pooled)
-    pool_mean = jnp.mean(pool_pre, axis=1)
-    pool_scale = lax.rsqrt(jnp.mean(pool_pre * pool_pre, axis=1) - pool_mean * pool_mean + EPSILON)
-    pool_normed = (pool_pre - pool_mean[:, None]) * pool_scale[:, None]
-    pool_shifted = gain_mid[4][:, None] * pool_normed + shift_mid[4][:, None]
-    pool_act = jax.nn.silu(pool_shifted).astype(BF)
-
-    g_proj_pool = jnp.dot(image_dz, pool_act.astype(F32).T, precision=HIGHEST)
-
-    grad_pool_act = lax.dot_general(wp_pool_own.astype(F32), image_dz, (((0,), (0,)), ((), ())), precision=HIGHEST)
-    dy_pool = grad_pool_act * silu_slope(pool_shifted)
-    pool_gain_sum = jnp.sum(dy_pool * pool_normed, axis=1)
-    pool_shift_sum = jnp.sum(dy_pool, axis=1)
-    pool_dz = (
-        (pool_scale * gain_mid[4])[:, None]
-        * (dy_pool - (pool_shift_sum[:, None] + pool_normed * pool_gain_sum[:, None]) / images)
-    ).astype(BF)
-    g_w_pool = dot_nt(pool_dz, pooled)
-    spread = jnp.dot(pool_dz.astype(F32) / area[None], member_strip[:images].astype(F32), precision=HIGHEST).astype(BF)
-
     strip_pad = lax.dynamic_slice_in_dim(padded_dz, strip * pixels, pixels + 2 * PAD, axis=1)
 
-    parts = input_grad(strip_pad, spread, strip_rows, w_taps, w_one, w_pool, jnp.arange(devices, dtype=jnp.int32))
-    g_feats = lax.psum_scatter(parts, "ch", scatter_dimension=0).astype(F32) * valid_strip
-    low_dz_all = lax.all_gather(low_dz, "ch", axis=1, tiled=True)
-    g_lowlevel = lax.dot_general(w_low, low_dz_all, (((0,), (0,)), ((), ())), preferred_element_type=F32)
-    g_lowlevel = g_lowlevel * valid_fine_strip.astype(F32)
-    g_low = jnp.sum(tell_row(dot_nt(low_dz_all, low_in)), axis=0)
-    g_proj_acts = jnp.einsum("gop,gcp->oc", strips_dz, slope[1], preferred_element_type=F32)
-    g_proj_part = jnp.concatenate([g_proj_acts, g_proj_pool], axis=1).astype(BF)
-    g_proj = jnp.take(swap_ch(g_proj_part.reshape(devices, outs, 5 * outs)), order, axis=0)
-    g_w_proj = g_proj.reshape(devices, outs, 5, outs).transpose(1, 2, 0, 3).reshape(outs, -1).astype(F32)
-
+    def finish(strip_pad, first_told, image_dz, strips_dz, dy_low):
+        low_mean, low_scale = merge_moments(proj_told[:, 512 : 512 + LOWC], proj_told[:, 768 : 768 + LOWC], counts_f[:, 0], fine_count)
+        low_normed = (low_pre - low_mean[:, None]) * low_scale[:, None]
+        low_dz = norm_back(dy_low, low_normed, low_scale, low_gains[0, :LOWC], low_sums, valid_fine, fine_count).astype(BF)
+
+        pool_sums = first_told[:, :images, :depth].transpose(0, 2, 1).reshape(devices * depth, images)
+        pooled = (pool_sums / area[None]).astype(BF)
+        pool_pre = dot(w_pool, pooled)
+        pool_mean = jnp.mean(pool_pre, axis=1)
+        pool_scale = lax.rsqrt(jnp.mean(pool_pre * pool_pre, axis=1) - pool_mean * pool_mean + EPSILON)
+        pool_normed = (pool_pre - pool_mean[:, None]) * pool_scale[:, None]
+        pool_shifted = gain_mid[4][:, None] * pool_normed + shift_mid[4][:, None]
+        pool_act = jax.nn.silu(pool_shifted).astype(BF)
+
+        g_proj_pool = jnp.dot(image_dz, pool_act.astype(F32).T, precision=HIGHEST)
+
+        grad_pool_act = lax.dot_general(wp_pool_own.astype(F32), image_dz, (((0,), (0,)), ((), ())), precision=HIGHEST)
+        dy_pool = grad_pool_act * silu_slope(pool_shifted)
+        pool_gain_sum = jnp.sum(dy_pool * pool_normed, axis=1)
+        pool_shift_sum = jnp.sum(dy_pool, axis=1)
+        pool_dz = (
+            (pool_scale * gain_mid[4])[:, None]
+            * (dy_pool - (pool_shift_sum[:, None] + pool_normed * pool_gain_sum[:, None]) / images)
+        ).astype(BF)
+        g_w_pool = dot_nt(pool_dz, pooled)
+        spread = jnp.dot(pool_dz.astype(F32) / area[None], member_strip[:images].astype(F32), precision=HIGHEST).astype(BF)
+
+
+        parts = input_grad(strip_pad, spread, strip_rows, w_taps, w_one, w_pool, jnp.arange(devices, dtype=jnp.int32))
+        g_feats = lax.psum_scatter(parts, "ch", scatter_dimension=0).astype(F32) * valid_strip
+        low_dz_all = lax.all_gather(low_dz, "ch", axis=1, tiled=True)
+        g_lowlevel = lax.dot_general(w_low, low_dz_all, (((0,), (0,)), ((), ())), preferred_element_type=F32)
+        g_lowlevel = g_lowlevel * valid_fine_strip.astype(F32)
+        g_low = jnp.sum(tell_row(dot_nt(low_dz_all, low_in)), axis=0)
+        g_proj_acts = jnp.einsum("gop,gcp->oc", strips_dz, slope[1], preferred_element_type=F32)
+        g_proj_part = jnp.concatenate([g_proj_acts, g_proj_pool], axis=1).astype(BF)
+        g_proj = jnp.take(swap_ch(g_proj_part.reshape(devices, outs, 5 * outs)), order, axis=0)
+        g_w_proj = g_proj.reshape(devices, outs, 5, outs).transpose(1, 2, 0, 3).reshape(outs, -1).astype(F32)
+        return g_feats, g_lowlevel, g_low, g_w_proj, g_w_pool, pool_gain_sum, pool_shift_sum
+
+    later = (strip_pad, first_told, image_dz, strips_dz, dy_low)
     if lined:
-        into, g_w_one, rest = assemble(gather_line(part), devices, groups, strip, outs, devices * depth)
+        found, finished = gather_line(part, later, finish)
+        into, g_w_one, rest = assemble(found, devices, groups, strip, outs, devices * depth)
     else:
+        part, later = lax.optimization_barrier((part, later))
+        finished = finish(*later)
         found = columns(lax.all_gather(part, "row", axis=0), (28 * outs,))
         into, g_w_one = found[: 27 * outs], found[27 * outs :]
         rest = lax.all_gather(shares, "row", axis=0)
+    g_feats, g_lowlevel, g_low, g_w_proj, g_w_pool, pool_gain_sum, pool_shift_sum = finished
     g_w_atrous = into.reshape(3, 9, outs, devices * depth).transpose(0, 2, 1, 3)
 
     rest = rest[:, : shares.shape[0]].astype(F32)

time: 696 us -> 691 us (level)
  waiting for transfers between devices: 156 us -> 134 us
    ppermute x10, waiting for transfers between devices: 32.1 us -> 1.34 us  [beside(): lax.ppermute(v, 'row', [(2 * i + e, 2 * i + 1 - e) for i in places for e...]
    ppermute x6, waiting for transfers between devices: 13.1 us -> 36.3 us  [along(): lax.ppermute(v, 'row', [(2 * i + e, 2 * (i + step) + e) for i in places f...]
    all_gather x1, waiting for transfers between devices: 50.2 us -> 28.3 us  [local(): canvas_dz = lax.all_gather(proj_dz, BOTH, axis=0)]
    ppermute x0 -> x2, waiting for transfers between devices: none -> 17.1 us  [reduce_blocks(): lax.ppermute(v, 'ch', [(i, i ^ m) for i in range(count)])]
    reduce_scatter x2 -> x1, waiting for transfers between devices: 14.5 us -> 0.01 us  [finish(): lax.psum_scatter(parts, 'ch', scatter_dimension=0).astype(F32) * valid_strip]
    convert_element_type x3 -> x6, other arithmetic: 2.05 us -> 9.4 us  [the longest x1 2.53 us: local(): part_dec = reduce_blocks([pick(i) for i in origin]).astype(BF)]
  transfers between devices with their start and end apart: 62 -> 63, of which waited for: 20 -> 18; matrix products, arithmetic and copies ran while one was open for 15% -> 17% of each run, Pallas kernels for 34% -> 32%
where the time goes in v3:
time: 691 us; the launch traced here: 679 us
  Pallas kernels  234 us (34%)
  starting transfers between devices  154 us (22%)
  waiting for transfers between devices  134 us (19%)
  local copies, waits for them, and re-layouts  65 us (9%)
  other arithmetic  51.6 us (7%)
  matrix products  22.6 us (3%)
  between operations  17.7 us (3%)
    pallas_call x5, Pallas kernels, decoder_call(): pl.pallas_call(kernel, grid=(pixels // lanes,), in_specs=in_specs, out_sp...  88.4 us
    all_to_all x7, starting transfers between devices, swap_all(): return lax.all_to_all(values, BOTH, 0, 0)  54.3 us
    ppermute x6, waiting for transfers between devices, along(): lax.ppermute(v, 'row', [(2 * i + e, 2 * (i + step) + e) for i in places f...  36.3 us
    all_gather x1, waiting for transfers between devices, local(): canvas_dz = lax.all_gather(proj_dz, BOTH, axis=0)  28.3 us
    pallas_call x2, Pallas kernels, decoder_weight_grad(): pl.pallas_call(lambda *refs: decoder_weight_kernel(lanes, outs, *refs), g...  24 us
    pallas_call x1, Pallas kernels, canvas_grad(): pl.pallas_call(lambda *refs: canvas_kernel(groups, devices, *refs), grid=...  23.2 us
    ppermute x7, starting transfers between devices, to_next(): return lax.ppermute(x, BOTH, [(i, i + 1) for i in range(count - 1)])  21.1 us
    ppermute x10, starting transfers between devices, beside(): lax.ppermute(v, 'row', [(2 * i + e, 2 * i + 1 - e) for i in places for e...  20.7 us
  transfers between devices with their start and end apart: 63, of which 18 were waited for; matrix products, arithmetic and copies ran while one was open for 17% of the time, Pallas kernels for 32%

profile of v3, /device:TPU:0, one launch (start us, length us, event | category | flops | bytes accessed | tf_op | source)
XLA Modules:
  0.0 678.8 jit_solution(10340370390389126419)
XLA Ops:
  19.0 5.8 all-to-all-start
  25.3 6.8 %all-to-all-done = f32[8,8,512]{2,1,0:T(8,128)S(1)} async-done(((f32[8,8,512]{2,1,0:T(8,128)}), f32[8,8,512]{2,1,0:T(8,128)S(1)}, u32[]{:S(2)}, u32[]{:S(2)}) %all-to-all-start) | async-done | bytes 131104 | tf_op jit(solution)/shard_map/all_to_all | solution.py:250
  36.3 10.0 %shard_map.332 = (f32[8,8,1152]{2,1,0:T(8,128)}, f32[8,16,1152]{2,1,0:T(8,128)}, f32[8,1]{1,0:T(8,128)}, f32[32,1]{1,0:T(8,128)}, f32[32,1]{1,0:T(8,128)}, /*ind...) custom-call(s32[6]{0:T(128)} %refs_0_.1, ...), custom_call_target="tpu_custom_call" | custom-call | flops 20000000 | bytes 6000000 | tf_op jit(solution)/shard_map/pallas_call | solution.py:161
  60.6 18.1 %shard_map.333 = (f32[4,64,1152]{2,1,0:T(8,128)}, bf16[3,64,640]{2,1,0:T(8,128)(2,1)}, bf16[3,64,640]{2,1,0:T(8,128)(2,1)}) custom-call(s32[4]{0:T(128)} %pad_add_fusion.refs_0_, bf16[512,1152]{1,0:T(8,128)(2,1)} %broadcast_multiply_fusion.refs_1_, bf16[512,1152]{1,0:T(8,128)(2,1)} %copy-done.87, bf16[512,1152]{1,0:T(8,128)(2,1)} %collective-permute-done.1.refs_3_, ...), custom_call_target="tpu_custom_call" | custom-call | flops 8455716864 | bytes 12058624 | tf_op jit(solution)/shard_map/pallas_call | solution.py:862
  78.8 6.2 all-to-all-done.2
  126.9 9.6 %collective-permute-done.6 = bf16[256,288]{1,0:T(8,128)(2,1)S(1)} collective-permute-done((bf16[256,288]{1,0:T(8,128)(2,1)S(1)}, bf16[256,288]{1,0:T(8,128)(2,1)S(1)}, u32[]{:S(2)}, u32[]{:S(2)}) %collective-permute-start.6) | collective-permute-done | bytes 147488 | tf_op jit(solution)/shard_map/ppermute | solution.py:191
  138.2 4.7 shard_map.336
  159.4 19.0 %shard_map.337 = (bf16[304,4864]{1,0:T(8,128)(2,1)}, f32[256,4608]{1,0:T(8,128)}, f32[256,128]{1,0:T(8,128)}, f32[256,128]{1,0:T(8,128)}, f32[32,8,128]{2,1,0:T(8,128)}) custom-call(f32[256,32]{1,0:T(8,128)} %copy-done.41, f32[256,288]{1,0:T(8,128)} %get-tuple-element.239.refs_1_, f32[256,32]{1,0:T(8,128)} %copy-done.42, f32[32,8,128]{2,1,0:T(8,128)} %copy-done.12, ...), custom_call_target="tpu_custom_call" | custom-call | flops 1 | bytes 1 | tf_op jit(solution)/shard_map/pallas_call | solution.py:691
  178.5 10.5 %all-to-all-start.5 = ((f32[32,8,128]{2,1,0:T(8,128)}), f32[32,8,128]{2,1,0:T(8,128)S(1)}, u32[]{:S(2)}, u32[]{:S(2)}) async-start(f32[32,8,128]{2,1,0:T(8,128)} %get-tuple-element.252), calls=%async_computation.6 | async-start | bytes 262144 | tf_op jit(solution)/shard_map/all_to_all | solution.py:240
  199.5 16.1 %shard_map.338 = (bf16[256,4864]{1,0:T(8,128)(2,1)}, f32[256,4608]{1,0:T(8,128)}, f32[256,128]{1,0:T(8,128)}, f32[256,128]{1,0:T(8,128)}, f32[32,8,128]{2,1,0:T(8,128)}) custom-call(f32[256,128]{1,0:T(8,128)} %copy-done.30, f32[256,4608]{1,0:T(8,128)} %get-tuple-element.256.refs_1_.refs_14_, f32[256,128]{1,0:T(8,128)} %copy-done.31, ...), custom_call_target="tpu_custom_call" | custom-call | flops 1 | bytes 1 | tf_op jit(solution)/shard_map/pallas_call | solution.py:691
  215.7 13.8 %all-to-all-start.6 = ((f32[32,8,128]{2,1,0:T(8,128)}), f32[32,8,128]{2,1,0:T(8,128)S(1)}, u32[]{:S(2)}, u32[]{:S(2)}) async-start(f32[32,8,128]{2,1,0:T(8,128)} %get-tuple-element.262), calls=%async_computation.7 | async-start | bytes 262144 | tf_op jit(solution)/shard_map/all_to_all | solution.py:240
  242.2 8.4 %shard_map.339 = (f32[21,4608]{1,0:T(8,128)}, f32[32,256]{1,0:T(8,128)}, f32[32,128]{1,0:T(8,128)}, f32[32,8,128]{2,1,0:T(8,128)}) custom-call(f32[256,4608]{1,0:T(8,128)} %get-tuple-element.260.pre.refs_1_, bf16[32,4608]{1,0:T(8,128)(2,1)} %pad.60.cotangent.refs_8_, f32[1,4608]{1,0:T(1,128)} %get-tuple-element.391.valid_fine.valid, ...), custom_call_target="tpu_custom_call" | custom-call | flops 1 | bytes 1 | tf_op jit(solution)/shard_map/pallas_call | solution.py:691
  250.6 10.1 %all-to-all-start.7 = ((f32[32,8,128]{2,1,0:T(8,128)}), f32[32,8,128]{2,1,0:T(8,128)S(1)}, u32[]{:S(2)}, u32[]{:S(2)}) async-start(f32[32,8,128]{2,1,0:T(8,128)} %get-tuple-element.274), calls=%async_computation.8 | async-start | bytes 262144 | tf_op jit(solution)/shard_map/all_to_all | solution.py:240
  263.1 6.9 %all-to-all-done.7.refs_6_ = f32[32,8,128]{2,1,0:T(8,128)S(1)} async-done(((f32[32,8,128]{2,1,0:T(8,128)}), f32[32,8,128]{2,1,0:T(8,128)S(1)}, u32[]{:S(2)}, u32[]{:S(2)}) %all-to-all-start.7) | async-done | bytes 131104 | tf_op jit(solution)/shard_map/all_to_all | solution.py:240
  270.7 19.5 %shard_map.340 = (bf16[256,4864]{1,0:T(8,128)(2,1)}, f32[256,4608]{1,0:T(8,128)}, f32[256,128]{1,0:T(8,128)}, f32[256,128]{1,0:T(8,128)}, f32[32,16,128]{2,1,0:T(8,128)}) custom-call(f32[256,128]{1,0:T(8,128)} %copy-done.39, f32[256,4608]{1,0:T(8,128)} %get-tuple-element.260.pre.refs_1_, f32[256,128]{1,0:T(8,128)} %copy-done.40, f32[32,8,128]{2,1,0:T(8,128)} %copy-done.19, ...), custom_call_target="tpu_custom_call" | custom-call | flops 1 | bytes 1 | tf_op jit(solution)/shard_map/pallas_call | solution.py:691
  298.3 10.8 %shard_map.341 = bf16[4,9,64,256]{3,2,1,0:T(8,128)(2,1)} custom-call(bf16[256,4864]{1,0:T(8,128)(2,1)} %get-tuple-element.284.refs_0_, bf16[256,4864]{1,0:T(8,128)(2,1)} %get-tuple-element.285.refs_1_, f32[2,4608]{1,0:T(2,128)} %get-tuple-element.250.refs_15_.refs_7_.refs_12_.refs_2_.refs_11_), custom_call_target="tpu_custom_call" | custom-call | flops 1 | bytes 1 | tf_op jit(solution)/shard_map/pallas_call | solution.py:670
  309.9 25.4 %shard_map.342 = (bf16[256,4864]{1,0:T(8,128)(2,1)}, f32[256,352]{1,0:T(8,128)}, f32[48,4608]{1,0:T(8,128)}, f32[2,256]{1,0:T(2,128)}) custom-call(f32[256,128]{1,0:T(8,128)} %copy-done.30, f32[256,4608]{1,0:T(8,128)} %get-tuple-element.256.refs_1_.refs_14_, f32[256,128]{1,0:T(8,128)} %copy-done.31, f32[256,128]{1,0:T(8,128)} %copy-done.43, ...), custom_call_target="tpu_custom_call" | custom-call | flops 1 | bytes 1 | tf_op jit(solution)/shard_map/pallas_call | solution.py:691
  350.0 9.9 %all-to-all-start.9 = ((f32[32,16,128]{2,1,0:T(8,128)}), f32[32,16,128]{2,1,0:T(8,128)}, u32[]{:S(2)}, u32[]{:S(2)}) async-start(f32[32,16,128]{2,1,0:T(8,128)} %broadcast_in_dim.36), calls=%async_computation.10 | async-start | bytes 524288 | tf_op jit(solution)/shard_map/all_to_all | solution.py:240
  360.2 13.2 %shard_map.343 = bf16[4,9,64,304]{3,2,1,0:T(8,128)(2,1)} custom-call(bf16[256,4864]{1,0:T(8,128)(2,1)} %get-tuple-element.289.refs_0_, bf16[304,4864]{1,0:T(8,128)(2,1)} %get-tuple-element.290.refs_1_, f32[2,4608]{1,0:T(2,128)} %get-tuple-element.250.refs_15_.refs_7_.refs_12_.refs_2_.refs_11_), custom_call_target="tpu_custom_call" | custom-call | flops 1 | bytes 1 | tf_op jit(solution)/shard_map/pallas_call | solution.py:670
  389.8 16.4 %collective-permute-done.23 = bf16[9,64,560]{2,1,0:T(8,128)(2,1)} collective-permute-done((bf16[9,64,560]{2,1,0:T(8,128)(2,1)}, bf16[9,64,560]{2,1,0:T(8,128)(2,1)}, u32[]{:S(2)}, u32[]{:S(2)}) %collective-permute-start.23) | collective-permute-done | bytes 645152 | tf_op jit(solution)/shard_map/ppermute | solution.py:198
  408.7 11.0 %shard_map.344 = (bf16[8,256,1152]{2,1,0:T(8,128)(2,1)}, bf16[8,256,1152]{2,1,0:T(8,128)(2,1)}) custom-call(bf16[8,256,1152]{2,1,0:T(8,128)(2,1)} %bitcast.204, f32[8,8,1152]{2,1,0:T(8,128)} %get-tuple-element.295.refs_1_.refs_6_, f32[256,4]{1,0:T(8,128)} %copy.120.refs_2_.refs_9_, f32[256,8]{1,0:T(8,128)} %get-tuple-element.375.refs_3_.refs_10_), custom_call_target="tpu_custom_call" | custom-call | flops 1 | bytes 1 | tf_op jit(solution)/shard_map/pallas_call | solution.py:1030
  419.7 28.3 %all-gather.20.cloned.1.call-done = bf16[8192,288]{1,0:T(8,128)(2,1)} async-done(((bf16[256,288]{1,0:T(8,128)(2,1)}), bf16[8192,288]{1,0:T(8,128)(2,1)}) %all-gather.20.cloned.1.call-update) | async-done | bytes 4718608 | tf_op jit(solution)/shard_map/all_gather | solution.py:1482
  456.1 23.2 %shard_map.345 = (bf16[256,10496]{1,0:T(8,128)(2,1)}, bf16[8,256,1152]{2,1,0:T(8,128)(2,1)}, f32[256,128]{1,0:T(8,128)}, f32[256,16]{1,0:T(8,128)}) custom-call(bf16[32,256,288]{2,1,0:T(8,128)(2,1)} %bitcast.200, bf16[32,256,288]{2,1,0:T(8,128)(2,1)} %bitcast.201, bf16[32,256,288]{2,1,0:T(8,128)(2,1)} %bitcast.202, bf16[32,256,288]{2,1,0:T(8,128)(2,1)} %bitcast.203, ...), custom_call_target="tpu_custom_call" | custom-call | flops 1207959552 | bytes 18874368 | tf_op jit(solution)/shard_map/pallas_call | solution.py:1098
  479.4 16.6 %shard_map.346 = bf16[1984,256]{1,0:T(8,128)(2,1)} custom-call(bf16[256,10496]{1,0:T(8,128)(2,1)} %get-tuple-element.301.refs_0_, f32[8,8,1152]{2,1,0:T(8,128)} %get-tuple-element.295.refs_1_.refs_6_, bf16[4,8,64,1152]{3,2,1,0:T(8,128)(2,1)} %bitcast.267, bf16[4,8,64,1152]{3,2,1,0:T(8,128)(2,1)} %bitcast.268, bf16[4,8,64,1152]{3,2,1,0:T(8,128)(2,1)} %bitcast.269, ...), custom_call_target="tpu_custom_call" | custom-call | flops 8455716864 | bytes 9437184 | tf_op jit(solution)/shard_map/pallas_call | solution.py:992
  512.0 11.5 %collective-permute-done.24.refs_5_.refs_22_.refs_39_ = bf16[1984,256]{1,0:T(8,128)(2,1)S(1)} collective-permute-done((bf16[1984,256]{1,0:T(8,128)(2,1)}, bf16[1984,256]{1,0:T(8,128)(2,1)S(1)}, u32[]{:S(2)}, u32[]{:S(2)}) %collective-permute-start.24) | collective-permute-done | bytes 1015840 | tf_op jit(solution)/shard_map/ppermute | solution.py:207
  535.0 16.6 %shard_map.347 = bf16[4,512,1152]{2,1,0:T(8,128)(2,1)} custom-call(s32[4]{0:T(128)} %iota.12.perm_ref, bf16[256,2432]{1,0:T(8,128)(2,1)} %constant_dynamic-slice_fusion.2.refs_0_, bf16[64,1152]{1,0:T(8,128)(2,1)} %convolution_convert_fusion.1.refs_1_, f32[8,1152]{1,0:T(8,128)} %get-tuple-element.198.refs_7_.refs_2_, bf16[1728,2048]{1,0:T(8,128)(2,1)} %bitcast.209, ...), custom_call_target="tpu_custom_call" | custom-call | flops 1 | bytes 1 | tf_op jit(solution)/shard_map/pallas_call | solution.py:938
  562.4 6.1 fusion.11
  570.2 11.5 %collective-permute-done.28.refs_12_.refs_29_.refs_46_ = bf16[1984,256]{1,0:T(8,128)(2,1)} collective-permute-done((bf16[1984,256]{1,0:T(8,128)(2,1)S(1)}, bf16[1984,256]{1,0:T(8,128)(2,1)}, u32[]{:S(2)}, u32[]{:S(2)}) %collective-permute-start.28) | collective-permute-done | bytes 1015840 | tf_op jit(solution)/shard_map/ppermute | solution.py:207
  605.5 9.3 %collective-permute-done.32.refs_15_.refs_32_.refs_49_ = bf16[1984,256]{1,0:T(8,128)(2,1)} collective-permute-done((bf16[1984,256]{1,0:T(8,128)(2,1)}, bf16[1984,256]{1,0:T(8,128)(2,1)}, u32[]{:S(2)}, u32[]{:S(2)}) %collective-permute-start.32) | collective-permute-done | bytes 1015840 | tf_op jit(solution)/shard_map/ppermute | solution.py:207
  627.3 6.6 all-to-all-start.11
  638.4 9.0 %all-to-all-done.11 = f32[8,1,3072]{2,1,0:T(1,128)S(1)} async-done(((f32[8,1,3072]{2,1,0:T(1,128)}), f32[8,1,3072]{2,1,0:T(1,128)S(1)}, u32[]{:S(2)}, u32[]{:S(2)}) %all-to-all-start.11) | async-done | bytes 98336 | tf_op jit(solution)/shard_map/all_to_all | solution.py:250
  653.3 13.3 %shard_map.348 = (f32[1728,2048]{1,0:T(8,128)}, f32[64,2048]{1,0:T(8,128)}, bf16[8,192,256]{2,1,0:T(8,128)(2,1)}) custom-call(s32[1]{0:T(128)} %bitcast.4.where_ref, bf16[1984,256]{1,0:T(8,128)(2,1)} %copy-done.5, bf16[1984,256]{1,0:T(8,128)(2,1)} %copy-done.6, bf16[1984,256]{1,0:T(8,128)(2,1)} %copy-done.4, ...), custom_call_target="tpu_custom_call" | custom-call | bytes 21233664 | tf_op jit(solution)/shard_map/pallas_call | solution.py:1157
  (500 shorter events, 257.0 us)
Async XLA Ops:
  13.7 32.7 %collective-permute-start.1 = (bf16[512,1152]{1,0:T(8,128)(2,1)}, bf16[512,1152]{1,0:T(8,128)(2,1)}, u32[]{:S(2)}, u32[]{:S(2)}) collective-permute-start(bf16[512,1152]{1,0:T(8,128)(2,1)} %broadcast_multiply_fusion.refs_1_), channel_id=1, source_target_pairs={{0,2},{1,3},{2,0},{3,1},{4,6},{5,7},{6,4},{7,5},{8,10},{9,11},{10,... | collective-permute-start | bytes 3538952 | tf_op jit(solution)/shard_map/ppermute | solution.py:174
  36.3 58.3 %all-gather.14.cloned.1.call-start = ((), (), s32[]{:S(2)}) async-start(), calls=%async_computation.17 | async-start | bytes 3604480 | tf_op jit(solution)/shard_map/all_gather | solution.py:1275
  47.7 75.1 %reduce-scatter.3.cloned.1.call-start = ((), (), s32[]{:S(2)}) async-start(), calls=%async_computation.14 | async-start | bytes 2211840 | tf_op jit(solution)/shard_map/reduce_scatter | solution.py:1282
  50.7 108.0 %all-gather.16.cloned.1.call-start = ((), (), s32[]{:S(2)}) async-start(), calls=%async_computation.18 | async-start | bytes 2211840 | tf_op jit(solution)/shard_map/all_gather | solution.py:1284
  51.8 33.2 %all-to-all-start.2 = ((bf16[8,64,1152]{2,1,0:T(8,128)(2,1)}), bf16[8,64,1152]{2,1,0:T(8,128)(2,1)S(1)}, u32[]{:S(2)}, u32[]{:S(2)}) async-start(bf16[8,64,1152]{2,1,0:T(8,128)(2,1)} %bitcast.8), calls=%async_computation.2 | async-start | bytes 2359296 | tf_op jit(solution)/shard_map/all_to_all | solution.py:1270
  55.6 185.9 %all-gather.18.cloned.1.call-start = ((), (), s32[]{:S(2)}) async-start(), calls=%async_computation.19 | async-start | bytes 5898240 | tf_op jit(solution)/shard_map/all_gather | solution.py:1299
  86.0 322.7 %all-gather.22.cloned.1.call-start = ((), (), s32[]{:S(2)}) async-start(), calls=%async_computation.21 | async-start | bytes 5308416 | tf_op jit(solution)/shard_map/all_gather | solution.py:1353
  115.4 21.0 %collective-permute-start.6 = (bf16[256,288]{1,0:T(8,128)(2,1)S(1)}, bf16[256,288]{1,0:T(8,128)(2,1)S(1)}, u32[]{:S(2)}, u32[]{:S(2)}) collective-permute-start(bf16[256,288]{1,0:T(8,128)(2,1)S(1)} %get-tuple-element.371), channel_id=1, source_target_pairs={{0,2},{1,3},{2,0},{3,1},{4,6},{5,7},{6,4},{7,5},{8,10},{9,11},{10,... | collective-permute-start | bytes 442376 | tf_op jit(solution)/shard_map/ppermute | solution.py:191
  117.1 20.3 %all-to-all-start.3 = ((f32[32,8,128]{2,1,0:T(8,128)}), f32[32,8,128]{2,1,0:T(8,128)S(1)}, u32[]{:S(2)}, u32[]{:S(2)}) async-start(f32[32,8,128]{2,1,0:T(8,128)} %get-tuple-element.226), calls=%async_computation.3 | async-start | bytes 262144 | tf_op jit(solution)/shard_map/all_to_all | solution.py:240
  215.7 25.8 %all-to-all-start.6 = ((f32[32,8,128]{2,1,0:T(8,128)}), f32[32,8,128]{2,1,0:T(8,128)S(1)}, u32[]{:S(2)}, u32[]{:S(2)}) async-start(f32[32,8,128]{2,1,0:T(8,128)} %get-tuple-element.262), calls=%async_computation.7 | async-start | bytes 262144 | tf_op jit(solution)/shard_map/all_to_all | solution.py:240
  235.3 27.8 %collective-permute-start.16 = (bf16[32,128]{1,0:T(8,128)(2,1)S(1)}, bf16[32,128]{1,0:T(8,128)(2,1)S(1)}, u32[]{:S(2)}, u32[]{:S(2)}) collective-permute-start(bf16[32,128]{1,0:T(8,128)(2,1)S(1)} %get-tuple-element.382), channel_id=1, source_target_pairs={{0,1},{1,2},{2,3},{3,4},{4,5},{5,6},{6,7},{7,8},{8,9},{9,10},{10,1... | collective-permute-start | bytes 24584 | tf_op jit(solution)/shard_map/ppermute | solution.py:265
  239.4 23.6 %collective-permute-start.17 = (bf16[32,128]{1,0:T(8,128)(2,1)S(1)}, bf16[32,128]{1,0:T(8,128)(2,1)S(1)}, u32[]{:S(2)}, u32[]{:S(2)}) collective-permute-start(bf16[32,128]{1,0:T(8,128)(2,1)S(1)} %get-tuple-element.381), channel_id=1, source_target_pairs={{1,0},{2,1},{3,2},{4,3},{5,4},{6,5},{7,6},{8,7},{9,8},{10,9},{11,1... | collective-permute-start | bytes 24584 | tf_op jit(solution)/shard_map/ppermute | solution.py:270
  350.0 23.4 %all-to-all-start.9 = ((f32[32,16,128]{2,1,0:T(8,128)}), f32[32,16,128]{2,1,0:T(8,128)}, u32[]{:S(2)}, u32[]{:S(2)}) async-start(f32[32,16,128]{2,1,0:T(8,128)} %broadcast_in_dim.36), calls=%async_computation.10 | async-start | bytes 524288 | tf_op jit(solution)/shard_map/all_to_all | solution.py:240
  359.9 88.0 %all-gather.20.cloned.1.call-start = ((), (), s32[]{:S(2)}) async-start(), calls=%async_computation.20 | async-start | bytes 6488064 | tf_op jit(solution)/shard_map/all_gather | solution.py:1482
  449.1 46.8 %all-to-all-start.10 = ((bf16[8,158,256]{2,1,0:T(8,128)(2,1)}), bf16[8,158,256]{2,1,0:T(8,128)(2,1)S(1)}, u32[]{:S(2)}, u32[]{:S(2)}) async-start(bf16[8,158,256]{2,1,0:T(8,128)(2,1)} %pad_maximum_fusion.3), calls=%async_computation.11 | async-start | bytes 1310720 | tf_op jit(solution)/shard_map/all_to_all | solution.py:1501
  453.1 170.4 %all-gather.12.cloned.1.call-start = ((), (), s32[]{:S(2)}) async-start(), calls=%async_computation.16 | async-start | bytes 2211840 | tf_op jit(solution)/shard_map/all_gather | solution.py:1540
  497.7 25.8 %collective-permute-start.24 = (bf16[1984,256]{1,0:T(8,128)(2,1)}, bf16[1984,256]{1,0:T(8,128)(2,1)S(1)}, u32[]{:S(2)}, u32[]{:S(2)}) collective-permute-start(bf16[1984,256]{1,0:T(8,128)(2,1)} %scatter.4.refs_7_.refs_24_.refs_41_), channel_id=1, source_target_pairs={{0,8},{4,12},{8,16},{12,20},{16,24},{20,28},{1,9},{5,13},{9,17},{1... | collective-permute-start | bytes 3047432 | tf_op jit(solution)/shard_map/ppermute | solution.py:207
  501.7 25.9 %collective-permute-start.25 = (bf16[1984,256]{1,0:T(8,128)(2,1)}, bf16[1984,256]{1,0:T(8,128)(2,1)S(1)}, u32[]{:S(2)}, u32[]{:S(2)}) collective-permute-start(bf16[1984,256]{1,0:T(8,128)(2,1)} %scatter.4.refs_7_.refs_24_.refs_41_), channel_id=1, source_target_pairs={{8,0},{12,4},{16,8},{20,12},{24,16},{28,20},{9,1},{13,5},{17,9},{2... | collective-permute-start | bytes 3047432 | tf_op jit(solution)/shard_map/ppermute | solution.py:207
  503.0 24.6 %collective-permute-start.26 = (bf16[1984,256]{1,0:T(8,128)(2,1)}, bf16[1984,256]{1,0:T(8,128)(2,1)S(1)}, u32[]{:S(2)}, u32[]{:S(2)}) collective-permute-start(bf16[1984,256]{1,0:T(8,128)(2,1)} %scatter.4.refs_7_.refs_24_.refs_41_), channel_id=1, source_target_pairs={{0,4},{4,0},{8,12},{12,8},{16,20},{20,16},{24,28},{28,24},{1,5},{5... | collective-permute-start | bytes 3047432 | tf_op jit(solution)/shard_map/ppermute | solution.py:210
  529.0 120.5 %reduce-scatter.5.cloned.1.call-start = ((), (), s32[]{:S(2)}) async-start(), calls=%async_computation.15 | async-start | bytes 5898240 | tf_op jit(solution)/shard_map/reduce_scatter | solution.py:1539
  554.9 26.8 %collective-permute-start.28 = (bf16[1984,256]{1,0:T(8,128)(2,1)S(1)}, bf16[1984,256]{1,0:T(8,128)(2,1)}, u32[]{:S(2)}, u32[]{:S(2)}) collective-permute-start(bf16[1984,256]{1,0:T(8,128)(2,1)S(1)} %collective-permute-done.25.refs_9_.refs_26_.refs_43_), channel_id=1, source_target_pairs={{8,0},{12,4},{16,8},{20,12},{9,1},{13,5},{17,9},{21,13},{10,2},{14... | collective-permute-start | bytes 3047432 | tf_op jit(solution)/shard_map/ppermute | solution.py:207
  556.8 28.6 %collective-permute-start.29 = (bf16[1984,256]{1,0:T(8,128)(2,1)S(1)}, bf16[1984,256]{1,0:T(8,128)(2,1)}, u32[]{:S(2)}, u32[]{:S(2)}) collective-permute-start(bf16[1984,256]{1,0:T(8,128)(2,1)S(1)} %collective-permute-done.24.refs_5_.refs_22_.refs_39_), channel_id=1, source_target_pairs={{8,12},{12,8},{16,20},{20,16},{24,28},{28,24},{9,13},{13,9},{17,21... | collective-permute-start | bytes 3047432 | tf_op jit(solution)/shard_map/ppermute | solution.py:210
  558.5 26.8 %collective-permute-start.30 = (bf16[1984,256]{1,0:T(8,128)(2,1)S(1)}, bf16[1984,256]{1,0:T(8,128)(2,1)}, u32[]{:S(2)}, u32[]{:S(2)}) collective-permute-start(bf16[1984,256]{1,0:T(8,128)(2,1)S(1)} %collective-permute-done.25.refs_9_.refs_26_.refs_43_), channel_id=1, source_target_pairs={{0,4},{4,0},{1,5},{5,1},{2,6},{6,2},{3,7},{7,3}} | collective-permute-start | bytes 3047432 | tf_op jit(solution)/shard_map/ppermute | solution.py:210
  568.6 20.4 %collective-permute-start.38 = (bf16[64,320]{1,0:T(8,128)(2,1)S(1)}, bf16[64,320]{1,0:T(8,128)(2,1)S(1)}, u32[]{:S(2)}, u32[]{:S(2)}) collective-permute-start(bf16[64,320]{1,0:T(8,128)(2,1)S(1)} %get-tuple-element.385), channel_id=1, source_target_pairs={{0,2},{1,3},{2,0},{3,1},{4,6},{5,7},{6,4},{7,5},{8,10},{9,11},{10,... | collective-permute-start | bytes 122888 | tf_op jit(solution)/shard_map/ppermute | solution.py:191
  586.1 28.7 %collective-permute-start.34 = (bf16[1984,256]{1,0:T(8,128)(2,1)S(1)}, bf16[1984,256]{1,0:T(8,128)(2,1)}, u32[]{:S(2)}, u32[]{:S(2)}) collective-permute-start(bf16[1984,256]{1,0:T(8,128)(2,1)S(1)} %collective-permute-done.27.refs_2_.refs_19_.refs_36_), channel_id=1, source_target_pairs={{24,28},{28,24},{25,29},{29,25},{26,30},{30,26},{27,31},{31,27}} | collective-permute-start | bytes 3047432 | tf_op jit(solution)/shard_map/ppermute | solution.py:210
  587.8 27.1 %collective-permute-start.32 = (bf16[1984,256]{1,0:T(8,128)(2,1)}, bf16[1984,256]{1,0:T(8,128)(2,1)}, u32[]{:S(2)}, u32[]{:S(2)}) collective-permute-start(bf16[1984,256]{1,0:T(8,128)(2,1)} %collective-permute-done.28.refs_12_.refs_29_.refs_46_), channel_id=1, source_target_pairs={{8,0},{12,4},{9,1},{13,5},{10,2},{14,6},{11,3},{15,7}} | collective-permute-start | bytes 3047432 | tf_op jit(solution)/shard_map/ppermute | solution.py:207
  589.1 27.1 %collective-permute-start.35 = (bf16[1984,256]{1,0:T(8,128)(2,1)}, bf16[1984,256]{1,0:T(8,128)(2,1)}, u32[]{:S(2)}, u32[]{:S(2)}) collective-permute-start(bf16[1984,256]{1,0:T(8,128)(2,1)} %collective-permute-done.28.refs_12_.refs_29_.refs_46_), channel_id=1, source_target_pairs={{0,4},{4,0},{1,5},{5,1},{2,6},{6,2},{3,7},{7,3}} | collective-permute-start | bytes 3047432 | tf_op jit(solution)/shard_map/ppermute | solution.py:210
  592.5 22.3 %collective-permute-start.33 = (bf16[1984,256]{1,0:T(8,128)(2,1)S(1)}, bf16[1984,256]{1,0:T(8,128)(2,1)}, u32[]{:S(2)}, u32[]{:S(2)}) collective-permute-start(bf16[1984,256]{1,0:T(8,128)(2,1)S(1)} %collective-permute-done.25.refs_9_.refs_26_.refs_43_), channel_id=1, source_target_pairs={{8,12},{12,8},{16,20},{20,16},{9,13},{13,9},{17,21},{21,17},{10,14... | collective-permute-start | bytes 3047432 | tf_op jit(solution)/shard_map/ppermute | solution.py:210
  616.1 36.2 %collective-permute-start.36 = (bf16[1984,256]{1,0:T(8,128)(2,1)S(1)}, bf16[1984,256]{1,0:T(8,128)(2,1)S(1)}, u32[]{:S(2)}, u32[]{:S(2)}) collective-permute-start(bf16[1984,256]{1,0:T(8,128)(2,1)S(1)} %collective-permute-done.31.refs_0_.refs_17_.refs_34_), channel_id=1, source_target_pairs={{24,28},{28,24},{25,29},{29,25},{26,30},{30,26},{27,31},{31,27}} | collective-permute-start | bytes 3047432 | tf_op jit(solution)/shard_map/ppermute | solution.py:210
  616.9 35.5 %collective-permute-start.40 = (bf16[1984,256]{1,0:T(8,128)(2,1)S(1)}, bf16[1984,256]{1,0:T(8,128)(2,1)}, u32[]{:S(2)}, u32[]{:S(2)}) collective-permute-start(bf16[1984,256]{1,0:T(8,128)(2,1)S(1)} %collective-permute-done.27.refs_2_.refs_19_.refs_36_), channel_id=1, source_target_pairs={{16,20},{20,16},{17,21},{21,17},{18,22},{22,18},{19,23},{23,19}} | collective-permute-start | bytes 3047432 | tf_op jit(solution)/shard_map/ppermute | solution.py:210
  618.5 33.8 %collective-permute-start.41 = (bf16[1984,256]{1,0:T(8,128)(2,1)}, bf16[1984,256]{1,0:T(8,128)(2,1)}, u32[]{:S(2)}, u32[]{:S(2)}) collective-permute-start(bf16[1984,256]{1,0:T(8,128)(2,1)} %collective-permute-done.28.refs_12_.refs_29_.refs_46_), channel_id=1, source_target_pairs={{8,12},{12,8},{9,13},{13,9},{10,14},{14,10},{11,15},{15,11}} | collective-permute-start | bytes 3047432 | tf_op jit(solution)/shard_map/ppermute | solution.py:210
  620.1 32.2 %collective-permute-start.42 = (bf16[1984,256]{1,0:T(8,128)(2,1)}, bf16[1984,256]{1,0:T(8,128)(2,1)}, u32[]{:S(2)}, u32[]{:S(2)}) collective-permute-start(bf16[1984,256]{1,0:T(8,128)(2,1)} %collective-permute-done.32.refs_15_.refs_32_.refs_49_), channel_id=1, source_target_pairs={{0,4},{4,0},{1,5},{5,1},{2,6},{6,2},{3,7},{7,3}} | collective-permute-start | bytes 3047432 | tf_op jit(solution)/shard_map/ppermute | solution.py:210
  (127 other events, 1919.2 us)
Sparse Core Ops, SparseCore 0:
  47.8 25.9 all-gather.13
  77.0 29.3 reduce-scatter.2
  108.7 30.3 all-gather.15
  140.6 38.9 all-gather.17
  182.5 88.0 all-gather.21
  376.6 71.3 all-gather.19
  529.1 21.4 all-gather.11
  553.9 47.8 reduce-scatter.4
